TPU v7x, 32 devices: a whole 2x2x4 slice. The times are simulated.
32 devices in a mesh: groups: 2 (over y), fsdp: 8 (over z, x), tp: 2 (over core).
Axes of the slice: x: 2, y: 2, z: 4, core: 2. Of those that a mesh axis runs over, the one named last changes fastest.
Arguments:
- hidden: bfloat16 [4096, 8192], P(('groups', 'fsdp'), 'tp'), parts along dimension 0, may hold values from -6 to 6
- queries: bfloat16 [4096, 8192], P(('groups', 'fsdp'), 'tp'), parts along dimension 0, may hold values from -360 to 360
- lengths: int32 [16, 4], P(('groups', 'fsdp')), parts along dimension 0, may hold values from 1 to 128, 256 in all within a row
- scoring_rank: int32 [4096, 1], P(('groups', 'fsdp')), parts along dimension 0, may hold values from 0 to 7; in each aligned block of 256 rows (0 to 255, 256 to 511, ...) at most 64 rows name the same one
- norm_gain: float32 [8192], P('tp'), may hold values from 0.1 to 1.9
- kv_weight: bfloat16 [8192, 2048], P('fsdp', 'tp'), may hold values from -0.0625 to 0.0625
- kv_bias: float32 [2048], P('tp'), may hold values from -3 to 3
Outputs:
- attended: bfloat16 [4096, 8192], P(('groups', 'fsdp'), 'tp'), parts along dimension 0
- scored_rows: bfloat16 [8192, 2048], P(('groups', 'fsdp'), 'tp'), parts along dimension 0
There are 2 independent parts, one for each index of `groups`. A program takes and returns all parts, laid end to end along the dimension named above; an argument that names none is the same for every part. Nothing has to cross between parts.
Inputs may be any that keep to these rules, and one draw needn't show every extreme that they name: `scoring_rank`: among the tokens of one rollout rank no scoring rank is named more than 64 times.
All inputs are finite; a program needn't handle non-finite values.
Results may differ from a plain program's by a relative error of at most 0.003.
The roundings to bfloat16 on the way count: a program that leaves them out, or rounds other values in their place, can miss the bound.
Values may be sent and summed in bfloat16 or wider, within the bound.
No kernel may reach another device: no remote copies, remote signals or barrier semaphores. Data moves between devices by JAX's collectives and lax.ppermute only.
A program may use at most 128 MiB of HBM per device.

v0:
```python
import jax
import jax.numpy as jnp
from jax import lax
from jax.sharding import PartitionSpec as P

D = 8192
HD = 128


EPSILON = 1e-06
THETA = 1000000.0


def rotate(values, position):
    width = values.shape[-1]
    half = width // 2
    freq = THETA ** (-jnp.arange(half, dtype=jnp.float32) * 2.0 / width)
    angles = position.astype(jnp.float32)[:, None] * freq[None, :]
    cosine = jnp.cos(angles)[:, None, :]
    sine = jnp.sin(angles)[:, None, :]
    first = values[..., :half]
    second = values[..., half:]
    return jnp.concatenate([first * cosine - second * sine, second * cosine + first * sine], -1)


def placement(lengths_row, count):
    ends = jnp.cumsum(lengths_row)
    starts = ends - lengths_row
    index = jnp.arange(count, dtype=jnp.int32)
    segment = jnp.sum((index[:, None] >= ends[None, :]).astype(jnp.int32), 1)
    onehot = segment[:, None] == jnp.arange(lengths_row.shape[0], dtype=jnp.int32)[None, :]
    offset = jnp.sum(jnp.where(onehot, starts[None, :], 0), 1)
    return (segment, index - offset)


def attend_local(query_rows, keyval, lengths_row):
    count = query_rows.shape[0]
    kv_heads = keyval.shape[1] // (2 * HD)
    heads = query_rows.shape[1] // HD
    group = heads // kv_heads
    segment, position = placement(lengths_row, count)
    keyval_heads = keyval.reshape(count, kv_heads, 2, HD)
    keys_rot = rotate(keyval_heads[:, :, 0].astype(jnp.float32), position).astype(jnp.bfloat16)
    values = keyval_heads[:, :, 1]
    queries_rot = rotate(query_rows.reshape(count, heads, HD).astype(jnp.float32), position).astype(
        jnp.bfloat16
    )
    queries_rot = queries_rot.reshape(count, kv_heads, group, HD)
    scores = jnp.einsum(
        "qhgd,khd->hgqk", queries_rot, keys_rot, preferred_element_type=jnp.float32
    ) * HD ** (-0.5)
    index = jnp.arange(count)
    allowed = (segment[:, None] == segment[None, :]) & (index[None, :] <= index[:, None])
    masked = jnp.where(allowed, scores, jnp.float32(-1e30))
    top = jnp.max(masked, -1, keepdims=True)
    weights = jnp.where(allowed, jnp.exp(masked - top), jnp.float32(0.0))
    probs = (weights / jnp.sum(weights, -1, keepdims=True)).astype(jnp.bfloat16)
    output = jnp.einsum("hgqk,khd->qhgd", probs, values, preferred_element_type=jnp.float32)
    return output.astype(jnp.bfloat16).reshape(count, heads * HD)


def project(normed_half, kv_weight, kv_bias):
    full_rows = lax.all_gather(normed_half, "tp", axis=1, tiled=True)
    summed = jnp.dot(
        full_rows,
        lax.all_gather(kv_weight, "fsdp", axis=0, tiled=True),
        preferred_element_type=jnp.float32,
    )
    return (summed + kv_bias[None, :]).astype(jnp.bfloat16)


def shards(hidden, queries, lengths, scoring_rank, norm_gain, kv_weight, kv_bias):
    ranks = lax.axis_size("fsdp")
    count = hidden.shape[0]
    capacity = 2 * count // ranks
    slot_count = capacity * ranks
    hidden_f = hidden.astype(jnp.float32)
    squares = lax.psum(jnp.sum(hidden_f * hidden_f, -1), "tp")
    inverse_rms = lax.rsqrt(squares / D + EPSILON)
    normed = (hidden_f * inverse_rms[:, None] * norm_gain[None, :]).astype(jnp.bfloat16)
    dest = scoring_rank[:, 0]
    onehot = (dest[:, None] == jnp.arange(ranks, dtype=jnp.int32)[None, :]).astype(jnp.int32)
    before = jnp.cumsum(onehot, 0) - onehot
    slot = jnp.sum(before * onehot, 1)
    target = dest * capacity + slot
    bias_rows = jnp.broadcast_to(
        kv_bias.astype(jnp.bfloat16)[None, :], (slot_count, kv_bias.shape[0])
    )
    keyval = project(normed, kv_weight, kv_bias)
    outgoing = bias_rows.at[target].set(keyval)
    scored_rows = lax.all_to_all(outgoing, "fsdp", split_axis=0, concat_axis=0, tiled=True)
    attended = attend_local(queries, keyval, lengths[0])
    return (attended, scored_rows)


def solution(mesh):
    placed = (
        P(("groups", "fsdp"), "tp"),
        P(("groups", "fsdp"), "tp"),
        P(("groups", "fsdp"), None),
        P(("groups", "fsdp"), None),
        P("tp"),
        P("fsdp", "tp"),
        P("tp"),
    )
    return jax.shard_map(
        shards,
        mesh=mesh,
        in_specs=placed,
        out_specs=(P(("groups", "fsdp"), "tp"), P(("groups", "fsdp"), "tp")),
        check_vma=False,
    )
```

profile of v0, /device:TPU:0, one launch (start us, length us, event | category | flops | bytes accessed | tf_op | source)
XLA Modules:
  0.0 319.1 jit_solution(2667687984196481132)
XLA Ops:
  7.2 2.1 fusion.2
  9.3 2.6 psum.7
  11.9 3.7 %fusion.4 = bf16[256,4096]{1,0:T(8,128)(2,1)} fusion(bf16[256,4096]{1,0:T(8,128)(2,1)} %param.7, f32[4096]{0:T(1024)} %param.11, f32[256]{0:T(256)S(1)} %add_rsqrt_fusion), kind=kLoop, calls=%fused_computation.10 | loop fusion | flops 4194304 | bytes 4211712 | tf_op jit(solution)/shard_map/convert_element_type | solution.py:80
  15.7 0.7 all-gather.5.cloned.1.call-update
  16.6 0.6 reduce-window.11
  17.9 0.8 copy.34
  19.6 1.5 fusion.27
  21.1 6.2 %subtract_convert_fusion = (bf16[256,32,64]{2,0,1:T(8,128)(2,1)S(1)}, bf16[256,32,64]{2,0,1:T(8,128)(2,1)}) fusion(f32[256,32,64]{2,1,0:T(8,128)S(1)} %get-tuple-element.11, f32[256,32,64]{2,1,0:T(8,128)S(1)} %get-tuple-element.10, f32[256,64]{1,0:T(8,128)S(1)} %get-tuple-element.17, f32[256,64]{1,0:T(8,128)S(1)} %get-tuple-element.16), kind=kLoop, calls=%fused_computation.15 | loop fusion | flops 4194304 | bytes 6422528 | tf_op jit(solution)/shard_map/convert.5
  27.3 4.8 %all-gather.3.cloned.1.call-done = bf16[256,8192]{1,0:T(8,128)(2,1)} async-done(((bf16[256,4096]{1,0:T(8,128)(2,1)}), bf16[256,8192]{1,0:T(8,128)(2,1)}) %all-gather.3.cloned.1.call-update) | async-done | bytes 4194320 | tf_op jit(solution)/shard_map/all_gather | solution.py:63
  32.1 230.9 %all-gather.5.cloned.1.call-done = bf16[8192,1024]{1,0:T(8,128)(2,1)} async-done(((bf16[1024,1024]{1,0:T(8,128)(2,1)}), bf16[8192,1024]{1,0:T(8,128)(2,1)}) %all-gather.5.cloned.1.call-update) | async-done | bytes 16777232 | tf_op jit(solution)/shard_map/all_gather | solution.py:66
  263.0 11.5 %fusion.14 = bf16[256,1024]{1,0:T(8,128)(2,1)S(1)} fusion(bf16[256,8192]{1,0:T(8,128)(2,1)} %all-gather.3.cloned.1.call-done, bf16[8192,1024]{1,0:T(8,128)(2,1)} %all-gather.5.cloned.1.call-done, f32[1024]{0:T(1024)S(1)} %copy-done.4), kind=kOutput, calls=%fused_computation.24 | convolution fusion | flops 4295491584 | bytes 21499904 | tf_op jit(solution)/shard_map/dot_general | solution.py:64
  274.6 0.5 reshape.117
  275.1 1.1 broadcast_in_dim.32
  276.2 3.9 %scatter_fusion = bf16[512,1024]{1,0:T(8,128)(2,1)} fusion(bf16[512,1024]{1,0:T(8,128)(2,1)} %broadcast_in_dim.32, s32[256]{0:T(256)S(1)} %bitcast.66, bf16[256,1024]{1,0:T(8,128)(2,1)S(1)} %fusion.14), kind=kCustom, calls=%fused_computation | custom fusion | bytes 1573888 | tf_op jit(solution)/shard_map/scatter | solution.py:90
  280.1 4.2 %all-to-all-start = ((bf16[8,64,1024]{2,1,0:T(8,128)(2,1)}), bf16[8,64,1024]{2,1,0:T(8,128)(2,1)}, u32[]{:S(2)}, u32[]{:S(2)}) async-start(bf16[8,64,1024]{2,1,0:T(8,128)(2,1)} %bitcast.22), calls=%async_computation | async-start | bytes 2097152 | tf_op jit(solution)/shard_map/all_to_all | solution.py:91
  284.3 1.5 fusion.28
  285.9 1.9 copy.30
  288.0 1.3 copy-done
  289.3 1.6 fusion.9
  290.9 2.7 fusion.29
  293.6 0.8 fusion.13
  294.4 2.9 copy.26
  297.2 12.7 %all-to-all-done = bf16[8,64,1024]{2,1,0:T(8,128)(2,1)} async-done(((bf16[8,64,1024]{2,1,0:T(8,128)(2,1)}), bf16[8,64,1024]{2,1,0:T(8,128)(2,1)}, u32[]{:S(2)}, u32[]{:S(2)}) %all-to-all-start) | async-done | bytes 1048608 | tf_op jit(solution)/shard_map/all_to_all | solution.py:91
  310.0 2.3 copy.44
  (33 shorter events, 2.3 us)
Async XLA Ops:
  7.2 24.9 %all-gather.3.cloned.1.call-start = ((), (), s32[]{:S(2)}) async-start(), calls=%async_computation.1 | async-start | bytes 6291456 | tf_op jit(solution)/shard_map/all_gather | solution.py:63
  11.9 4.5 %copy-start.4 = (f32[1024]{0:T(1024)S(1)}, f32[1024]{0:T(1024)}, u32[]{:S(2)}) copy-start(f32[1024]{0:T(1024)} %param.13) | copy-start | bytes 12292
  11.9 4.5 %copy-start.5 = (s32[1,4]{1,0:T(1,128)S(1)}, s32[1,4]{1,0:T(1,128)}, u32[]{:S(2)}) copy-start(s32[1,4]{1,0:T(1,128)} %param.9) | copy-start | bytes 52
  11.9 4.7 %copy-start.3 = (s32[256,1]{0,1:T(1,128)S(1)}, s32[256,1]{0,1:T(1,128)}, u32[]{:S(2)}) copy-start(s32[256,1]{0,1:T(1,128)} %param.10) | copy-start | bytes 3076
  11.9 5.5 %copy-start.1 = (bf16[256,4096]{1,0:T(8,128)(2,1)S(1)}, bf16[256,4096]{1,0:T(8,128)(2,1)}, u32[]{:S(2)}) copy-start(bf16[256,4096]{1,0:T(8,128)(2,1)} %param.8) | copy-start | bytes 6291460
  15.6 247.4 %all-gather.5.cloned.1.call-start = ((), (), s32[]{:S(2)}) async-start(), calls=%async_computation.2 | async-start | bytes 18874368 | tf_op jit(solution)/shard_map/all_gather | solution.py:66
  280.1 29.9 %all-to-all-start = ((bf16[8,64,1024]{2,1,0:T(8,128)(2,1)}), bf16[8,64,1024]{2,1,0:T(8,128)(2,1)}, u32[]{:S(2)}, u32[]{:S(2)}) async-start(bf16[8,64,1024]{2,1,0:T(8,128)(2,1)} %bitcast.22), calls=%async_computation | async-start | bytes 2097152 | tf_op jit(solution)/shard_map/all_to_all | solution.py:91
  287.7 1.6 copy-start
  290.9 2.7 copy-start.2
Sparse Core Ops, SparseCore 0:
  15.8 16.2 all-gather.2
  34.2 228.7 all-gather.4
where the time goes:
time: 319 us
  waiting for transfers between devices  249 us (78%)
  local copies, waits for them, and re-layouts  17.8 us (6%)
  other arithmetic  17.2 us (5%)
  between operations  14.2 us (4%)
  matrix products  13.8 us (4%)
  starting transfers between devices  4.31 us (1%)
    all_gather x1, waiting for transfers between devices, project(): lax.all_gather(kv_weight, 'fsdp', axis=0, tiled=True)  231 us
    all_to_all x1, waiting for transfers between devices, shards(): lax.all_to_all(outgoing, 'fsdp', split_axis=0, concat_axis=0, tiled=True)  12.7 us
    dot_general x1, matrix products, project(): jnp.dot(full_rows, lax.all_gather(kv_weight, 'fsdp', axis=0, tiled=True),...  11.5 us
    unnamed x16, local copies, waits for them, and re-layouts  9.05 us
    another operation x5, other arithmetic  7.25 us
  transfers between devices with their start and end apart: 3, of which 3 were waited for; matrix products, arithmetic and copies ran while one was open for 7% of the time, Pallas kernels for 0%

commit v1 on v0

v1 whole, which is shorter than its diff:
```python
import functools

import jax
import jax.numpy as jnp
from jax import lax
from jax.experimental import pallas as pl
from jax.experimental.pallas import tpu as pltpu
from jax.sharding import PartitionSpec as P

HD = 128
EPSILON = 1e-06
THETA = 1000000.0
VMEM = pl.BlockSpec(memory_space=pltpu.VMEM)
SMEM = pl.BlockSpec(memory_space=pltpu.SMEM)
ANY = pl.BlockSpec(memory_space=pl.ANY)
PARAMS = pltpu.CompilerParams(vmem_limit_bytes=24 * 1024 * 1024)


def cost(flops, nbytes):
    return pl.CostEstimate(flops=flops, bytes_accessed=nbytes, transcendentals=0)


def norm_kernel(place, hidden, inverse, gain, *outs, slices, piece):
    for k, out in enumerate(outs):
        x = place[0] ^ (k & 1)
        y = place[1] ^ (k >> 1)
        for i in range(slices):
            start = pl.multiple_of((i * 4 + x * 2 + y) * piece, piece)
            cols = pl.ds(start, piece)
            values = hidden[:, cols].astype(jnp.float32) * inverse[...] * gain[:, cols]
            out[:, i * piece : (i + 1) * piece] = values.astype(jnp.bfloat16)


def matmul_kernel(place, *refs, count, piece, width):
    own, peer = refs[:4], refs[4:8]
    blocks = refs[8 : 8 + count]
    outs = refs[8 + count : 12 + count]
    weights = refs[12 + count]
    z, core = place[2], place[3]
    for s, block in enumerate(blocks):
        at = lax.rem(z - s + count, count)
        weights[pl.ds(pl.multiple_of(at * piece, piece), piece), :] = block[...]
    half = count // 2 * piece
    mine = weights[pl.ds(pl.multiple_of(core * half, half), half), :]
    others = weights[pl.ds(pl.multiple_of((1 - core) * half, half), half), :]
    for k in range(4):
        outs[k][...] = jnp.dot(
            own[k][...], mine, preferred_element_type=jnp.float32
        ) + jnp.dot(peer[k][...], others, preferred_element_type=jnp.float32)


def rows_kernel(a, b, c, d, bias, onehot, used, keyval, outgoing):
    summed = (a[...] + b[...]) + (c[...] + d[...])
    rows = (summed + bias[...]).astype(jnp.bfloat16)
    keyval[...] = rows
    moved = jnp.dot(onehot[...], rows, preferred_element_type=jnp.float32)
    empty = bias[...].astype(jnp.bfloat16).astype(jnp.float32)
    outgoing[...] = jnp.where(used[...] > 0, moved, empty).astype(jnp.bfloat16)


def turn(values, cosine, sine):
    half = HD // 2
    turned = jnp.concatenate([values[:, half:], values[:, :half]], -1)
    return values * cosine + turned * sine


def rotate_kernel(queries, cosine, sine, out):
    for h in range(queries.shape[1] // HD):
        cols = slice(h * HD, (h + 1) * HD)
        values = queries[:, cols].astype(jnp.float32)
        out[:, cols] = turn(values, cosine[...], sine[...]).astype(jnp.bfloat16)


def attend_kernel(queries, keyval, cosine, sine, mask, *rest, heads):
    out = rest[-1]
    count = keyval.shape[0]
    half = count // 2
    keys = turn(keyval[:, :HD].astype(jnp.float32), cosine[...], sine[...])
    keys = keys.astype(jnp.bfloat16)
    values = keyval[:, HD:]
    for h in range(heads):
        cols = slice(h * HD, (h + 1) * HD)
        for first, reach in ((0, half), (half, count)):
            rows = slice(first, first + half)
            scores = lax.dot_general(
                queries[rows, cols],
                keys[:reach],
                (((1,), (1,)), ((), ())),
                preferred_element_type=jnp.float32,
            )
            masked = scores * HD ** (-0.5) + mask[rows, :reach]
            top = jnp.max(masked, -1, keepdims=True)
            weights = jnp.exp(masked - top)
            total = jnp.sum(weights, -1, keepdims=True)
            probs = (weights * (1.0 / total)).astype(jnp.bfloat16)
            out[rows, cols] = jnp.dot(
                probs, values[:reach], preferred_element_type=jnp.float32
            ).astype(jnp.bfloat16)


def shards(hidden, queries, lengths, scoring_rank, norm_gain, kv_weight, kv_bias):
    ranks = lax.axis_size("fsdp")
    steps = ranks // 2
    count, features = hidden.shape
    width = features * lax.axis_size("tp")
    depth, columns = kv_weight.shape
    piece = depth // 2
    heads = columns // (2 * HD)
    group = queries.shape[1] // HD // heads
    capacity = 2 * count // ranks
    slots = capacity * ranks

    f = lax.axis_index("fsdp")
    y = lax.axis_index("groups")
    core = lax.axis_index("tp")
    x, z = lax.rem(f, 2), lax.div(f, 2)
    place = jnp.stack([x, y, z, core]).astype(jnp.int32)

    right = [(i, (i + 2) % ranks) for i in range(ranks)]
    left = [(i, (i - 2) % ranks) for i in range(ranks)]
    flip_x = [(i, i ^ 1) for i in range(ranks)]
    flip_y = [(0, 1), (1, 0)]
    flip_xy = [(g * ranks + i, (1 - g) * ranks + (i ^ 1)) for g in range(2) for i in range(ranks)]

    def to_chip(k, array):
        if k == 1:
            return lax.ppermute(array, "fsdp", flip_x)
        if k == 2:
            return lax.ppermute(array, "groups", flip_y)
        return lax.ppermute(array, ("groups", "fsdp"), flip_xy)

    half_rows = lax.dynamic_slice(kv_weight, (y * piece, 0), (piece, columns))
    gathered = []
    held = None
    for j in range(heads):
        block = half_rows[:, j * 2 * HD : (j + 1) * 2 * HD]
        if held is not None:
            block, _ = lax.optimization_barrier((block, held))
        ups, downs = [block], [block]
        for _ in range(steps // 2):
            ups.append(lax.ppermute(ups[-1], "fsdp", right))
        for _ in range((steps - 1) // 2):
            downs.append(lax.ppermute(downs[-1], "fsdp", left))
        gathered.append(ups + downs[:0:-1])
        held = (ups[1], downs[1])

    hidden_f = hidden.astype(jnp.float32)
    squares = jnp.sum(hidden_f * hidden_f, -1, keepdims=True)
    squares = squares + lax.ppermute(squares, "tp", flip_y)
    inverse_rms = lax.rsqrt(squares / width + EPSILON)
    slices = features // (4 * piece)
    if piece % HD == 0:
        normed = pl.pallas_call(
            functools.partial(norm_kernel, slices=slices, piece=piece),
            out_shape=[jax.ShapeDtypeStruct((count, features // 4), jnp.bfloat16)] * 4,
            in_specs=[SMEM] + [VMEM] * 3,
            out_specs=[VMEM] * 4,
            compiler_params=PARAMS,
            cost_estimate=cost(3 * count * features, 4 * count * features),
            name="norm",
        )(place, hidden, inverse_rms, norm_gain[None, :])
    else:
        whole = (hidden_f * inverse_rms * norm_gain[None, :]).astype(jnp.bfloat16)
        whole = whole.reshape(count, slices, 2, 2, piece)
        normed = []
        for k in range(4):
            part = lax.dynamic_index_in_dim(whole, x ^ (k & 1), 2, False)
            part = lax.dynamic_index_in_dim(part, y ^ (k >> 1), 2, False)
            normed.append(part.reshape(count, features // 4))
    own = [normed[0]] + [to_chip(k, normed[k]) for k in (1, 2, 3)]
    peer = [lax.ppermute(block, "tp", flip_y) for block in own]

    dest = scoring_rank[:, 0]
    index = jnp.arange(count, dtype=jnp.int32)
    earlier = (dest[:, None] == dest[None, :]) & (index[:, None] < index[None, :])
    slot = jnp.sum(earlier.astype(jnp.int32), 0)
    target = dest * capacity + slot
    hits = jnp.arange(slots, dtype=jnp.int32)[:, None] == target[None, :]
    onehot = hits.astype(jnp.bfloat16)
    used = jnp.any(hits, 1, keepdims=True).astype(jnp.float32)

    row = lengths[0]
    ends = jnp.cumsum(row)
    starts = ends - row
    within = (index[:, None] >= starts[None, :]) & (index[:, None] < ends[None, :])
    start = jnp.sum(jnp.where(within, starts[None, :], 0), 1)
    position = index - start
    freq = THETA ** (-jnp.arange(HD // 2, dtype=jnp.float32) * 2.0 / HD)
    angles = position.astype(jnp.float32)[:, None] * freq[None, :]
    cosine, sine = jnp.cos(angles), jnp.sin(angles)
    cosine = jnp.concatenate([cosine, cosine], 1)
    sine = jnp.concatenate([-sine, sine], 1)
    allowed = (index[None, :] >= start[:, None]) & (index[None, :] <= index[:, None])
    mask = jnp.where(allowed, jnp.float32(0.0), jnp.float32(-1e30))
    turned = pl.pallas_call(
        rotate_kernel,
        out_shape=jax.ShapeDtypeStruct(queries.shape, jnp.bfloat16),
        in_specs=[VMEM] * 3,
        out_specs=VMEM,
        compiler_params=PARAMS,
        cost_estimate=cost(4 * count * queries.shape[1], 4 * count * queries.shape[1]),
        name="rotate",
    )(queries, cosine, sine)

    attended = None
    received = []
    bias = kv_bias[None, :]
    for j in range(heads):
        cols = slice(j * 2 * HD, (j + 1) * 2 * HD)
        parts = pl.pallas_call(
            functools.partial(matmul_kernel, count=steps, piece=piece, width=2 * HD),
            out_shape=[jax.ShapeDtypeStruct((count, 2 * HD), jnp.float32)] * 4,
            in_specs=[SMEM] + [VMEM] * (8 + steps),
            out_specs=[VMEM] * 4,
            scratch_shapes=[pltpu.VMEM((steps * piece, 2 * HD), jnp.bfloat16)],
            compiler_params=PARAMS,
            cost_estimate=cost(2 * 4 * count * steps * piece * 2 * HD, 6 << 20),
            name="project",
        )(place, *own, *peer, *gathered[j])
        sums = [parts[0]] + [to_chip(k, parts[k]) for k in (1, 2, 3)]
        keyval, outgoing = pl.pallas_call(
            rows_kernel,
            out_shape=[
                jax.ShapeDtypeStruct((count, 2 * HD), jnp.bfloat16),
                jax.ShapeDtypeStruct((slots, 2 * HD), jnp.bfloat16),
            ],
            in_specs=[VMEM] * 7,
            out_specs=[VMEM] * 2,
            compiler_params=PARAMS,
            cost_estimate=cost(2 * slots * count * 2 * HD, 2 << 20),
            name="rows",
        )(*sums, bias[:, cols], onehot, used)
        received.append(
            lax.all_to_all(outgoing, "fsdp", split_axis=0, concat_axis=0, tiled=True)
        )
        before = [] if attended is None else [attended]
        attended = pl.pallas_call(
            functools.partial(attend_kernel, heads=group),
            out_shape=jax.ShapeDtypeStruct(queries.shape, jnp.bfloat16),
            grid=(1,),
            in_specs=[
                pl.BlockSpec((count, group * HD), lambda i, j=j: (0, j)),
                pl.BlockSpec((count, 2 * HD), lambda i: (0, 0)),
                pl.BlockSpec((count, HD), lambda i: (0, 0)),
                pl.BlockSpec((count, HD), lambda i: (0, 0)),
                pl.BlockSpec((count, count), lambda i: (0, 0)),
            ]
            + [ANY] * len(before),
            out_specs=pl.BlockSpec((count, group * HD), lambda i, j=j: (0, j)),
            input_output_aliases={5: 0} if before else {},
            compiler_params=PARAMS,
            cost_estimate=cost(4 * group * count * count * HD, 2 << 20),
            name="attend",
        )(turned, keyval, cosine, sine, mask, *before)
    scored_rows = jnp.concatenate(received, 1)
    return (attended, scored_rows)


def solution(mesh):
    placed = (
        P(("groups", "fsdp"), "tp"),
        P(("groups", "fsdp"), "tp"),
        P(("groups", "fsdp"), None),
        P(("groups", "fsdp"), None),
        P("tp"),
        P("fsdp", "tp"),
        P("tp"),
    )
    return jax.shard_map(
        shards,
        mesh=mesh,
        in_specs=placed,
        out_specs=(P(("groups", "fsdp"), "tp"), P(("groups", "fsdp"), "tp")),
        check_vma=False,
    )
```

time: 319 us -> 184 us (0.58)
  waiting for transfers between devices: 249 us -> 52 us
  starting transfers between devices: 4.31 us -> 65.6 us
  Pallas kernels: 0 us -> 35.3 us
  matrix products: 13.8 us -> 0 us
  between operations: 14.2 us -> 0.97 us
  other arithmetic: 17.2 us -> 8.32 us
    all_gather x2 -> x0, waiting for transfers between devices: 236 us -> none  [the longest x1 231 us: project(): lax.all_gather(kv_weight, 'fsdp', axis=0, tiled=True)]
    ppermute x0 -> x32, waiting for transfers between devices: none -> 52 us  [the longest x5 21.8 us: to_chip(): return lax.ppermute(array, 'groups', flip_y)]
    ppermute x0 -> x32, starting transfers between devices: none -> 40.7 us  [the longest x4 10.9 us: shards(): downs.append(lax.ppermute(downs[-1], 'fsdp', left))]
    pallas_call x0 -> x14, Pallas kernels: none -> 35.3 us  [the longest x4 17.2 us: shards(): pl.pallas_call(functools.partial(attend_kernel, heads=group), out_shape=j...]
    all_to_all x1 -> x4, starting transfers between devices: 4.23 us -> 24.9 us  [shards(): lax.all_to_all(outgoing, 'fsdp', split_axis=0, concat_axis=0, tiled=True)]
    dot_general x3 -> x0, matrix products: 13.8 us -> none  [the longest x1 11.5 us: project(): jnp.dot(full_rows, lax.all_gather(kv_weight, 'fsdp', axis=0, tiled=True),...]
    all_to_all x1 -> x4, waiting for transfers between devices: 12.7 us -> 0.01 us  [shards(): lax.all_to_all(outgoing, 'fsdp', split_axis=0, concat_axis=0, tiled=True)]
    unnamed x16 -> x62, local copies, waits for them, and re-layouts: 9.05 us -> 17.5 us
  transfers between devices with their start and end apart: 3 -> 36, of which waited for: 3 -> 11; matrix products, arithmetic and copies ran while one was open for 7% -> 4% of each run, Pallas kernels for 0% -> 18%
where the time goes in v1:
time: 184 us; the launch traced here: 183 us
  starting transfers between devices  65.6 us (36%)
  waiting for transfers between devices  52 us (28%)
  Pallas kernels  35.3 us (19%)
  local copies, waits for them, and re-layouts  20.6 us (11%)
  other arithmetic  8.32 us (5%)
    all_to_all x4, starting transfers between devices, shards(): lax.all_to_all(outgoing, 'fsdp', split_axis=0, concat_axis=0, tiled=True)  24.9 us
    ppermute x5, waiting for transfers between devices, to_chip(): return lax.ppermute(array, 'groups', flip_y)  21.8 us
    ppermute x8, waiting for transfers between devices, shards(): ups.append(lax.ppermute(ups[-1], 'fsdp', right))  19.1 us
    unnamed x62, local copies, waits for them, and re-layouts  17.5 us
    pallas_call x4, Pallas kernels, shards(): pl.pallas_call(functools.partial(attend_kernel, heads=group), out_shape=j...  17.2 us
    pallas_call x4, Pallas kernels, shards(): pl.pallas_call(functools.partial(matmul_kernel, count=steps, piece=piece,...  11 us
    ppermute x4, starting transfers between devices, shards(): downs.append(lax.ppermute(downs[-1], 'fsdp', left))  10.9 us
    ppermute x5, starting transfers between devices, to_chip(): return lax.ppermute(array, 'fsdp', flip_x)  10.4 us
  transfers between devices with their start and end apart: 36, of which 11 were waited for; matrix products, arithmetic and copies ran while one was open for 4% of the time, Pallas kernels for 18%

profile of v1, /device:TPU:0, one launch (start us, length us, event | category | flops | bytes accessed | tf_op | source)
XLA Modules:
  0.0 182.8 jit_solution(10328250635601601084)
XLA Ops:
  6.4 2.8 %collective-permute-start.1 = (bf16[256,1024]{1,0:T(8,128)(2,1)S(1)}, bf16[256,1024]{1,0:T(8,128)(2,1)S(1)}, u32[]{:S(2)}, u32[]{:S(2)}) collective-permute-start(bf16[256,1024]{1,0:T(8,128)(2,1)S(1)} %get-tuple-element.34), channel_id=1, source_target_pairs={{0,2},{2,0},{4,6},{6,4},{8,10},{10,8},{12,14},{14,12},{1,3},{3,1},... | collective-permute-start | bytes 1572872 | tf_op jit(solution)/shard_map/ppermute | solution.py:127
  16.9 7.2 %collective-permute-done.8.refs_9_ = bf16[512,256]{1,0:T(8,128)(2,1)S(1)} collective-permute-done((bf16[512,256]{1,0:T(8,128)(2,1)S(1)}, bf16[512,256]{1,0:T(8,128)(2,1)S(1)}, u32[]{:S(2)}, u32[]{:S(2)}) %collective-permute-start.8) | collective-permute-done | bytes 262176 | tf_op jit(solution)/shard_map/ppermute | solution.py:141
  24.7 9.7 %collective-permute-done.2.refs_2_ = bf16[256,1024]{1,0:T(8,128)(2,1)S(1)} collective-permute-done((bf16[256,1024]{1,0:T(8,128)(2,1)}, bf16[256,1024]{1,0:T(8,128)(2,1)S(1)}, u32[]{:S(2)}, u32[]{:S(2)}) %collective-permute-start.2) | collective-permute-done | bytes 524320 | tf_op jit(solution)/shard_map/ppermute | solution.py:129
  36.6 8.4 %collective-permute-done.28.refs_10_ = bf16[512,256]{1,0:T(8,128)(2,1)S(1)} collective-permute-done((bf16[512,256]{1,0:T(8,128)(2,1)S(1)}, bf16[512,256]{1,0:T(8,128)(2,1)S(1)}, u32[]{:S(2)}, u32[]{:S(2)}) %collective-permute-start.28) | collective-permute-done | bytes 262176 | tf_op jit(solution)/shard_map/ppermute | solution.py:141
  45.0 3.8 %collective-permute-start.11 = (bf16[512,256]{1,0:T(8,128)(2,1)}, bf16[512,256]{1,0:T(8,128)(2,1)}, u32[]{:S(2)}, u32[]{:S(2)}) collective-permute-start(bf16[512,256]{1,0:T(8,128)(2,1)} %get-tuple-element.37.refs_8_), channel_id=1, source_target_pairs={{0,12},{2,14},{4,0},{6,2},{8,4},{10,6},{12,8},{14,10},{1,13},{3,15... | collective-permute-start | bytes 786440 | tf_op jit(solution)/shard_map/ppermute | solution.py:143
  48.9 2.7 %project.7 = (f32[256,256]{1,0:T(8,128)S(1)}, f32[256,256]{1,0:T(8,128)}, f32[256,256]{1,0:T(8,128)}, f32[256,256]{1,0:T(8,128)}) custom-call(s32[4]{0:T(128)S(1)} %pad_add_fusion.place, bf16[256,1024]{1,0:T(8,128)(2,1)S(1)} %get-tuple-element.33.refs_0_, bf16[256,1024]{1,0:T(8,128)(2,1)S(1)} %collective-permute-done.1.refs_1_, ...), custom_call_target="tpu_custom_call" | custom-call | flops 1073741824 | bytes 6291456 | tf_op jit(solution)/shard_map/project/pallas_call | solution.py:210
  56.8 5.0 %collective-permute-done.29.b = f32[256,256]{1,0:T(8,128)} collective-permute-done((f32[256,256]{1,0:T(8,128)}, f32[256,256]{1,0:T(8,128)}, u32[]{:S(2)}, u32[]{:S(2)}) %collective-permute-start.29) | collective-permute-done | bytes 262176 | tf_op jit(solution)/shard_map/ppermute | solution.py:127
  61.9 4.5 %collective-permute-done.30.c = f32[256,256]{1,0:T(8,128)} collective-permute-done((f32[256,256]{1,0:T(8,128)}, f32[256,256]{1,0:T(8,128)}, u32[]{:S(2)}, u32[]{:S(2)}) %collective-permute-start.30) | collective-permute-done | bytes 262176 | tf_op jit(solution)/shard_map/ppermute | solution.py:129
  70.3 4.0 %all-to-all-start = ((bf16[8,64,256]{2,1,0:T(8,128)(2,1)}), bf16[8,64,256]{2,1,0:T(8,128)(2,1)}, u32[]{:S(2)}, u32[]{:S(2)}) async-start(bf16[8,64,256]{2,1,0:T(8,128)(2,1)} %bitcast.25), calls=%async_computation | async-start | bytes 524288 | tf_op jit(solution)/shard_map/all_to_all | solution.py:234
  86.5 3.5 %collective-permute-done.12.refs_9_ = bf16[512,256]{1,0:T(8,128)(2,1)} collective-permute-done((bf16[512,256]{1,0:T(8,128)(2,1)}, bf16[512,256]{1,0:T(8,128)(2,1)}, u32[]{:S(2)}, u32[]{:S(2)}) %collective-permute-start.12) | collective-permute-done | bytes 262176 | tf_op jit(solution)/shard_map/ppermute | solution.py:141
  94.0 2.6 %collective-permute-start.14 = (bf16[512,256]{1,0:T(8,128)(2,1)}, bf16[512,256]{1,0:T(8,128)(2,1)}, u32[]{:S(2)}, u32[]{:S(2)}) collective-permute-start(bf16[512,256]{1,0:T(8,128)(2,1)} %get-tuple-element.39.refs_8_), channel_id=1, source_target_pairs={{0,4},{2,6},{4,8},{6,10},{8,12},{10,14},{12,0},{14,2},{1,5},{3,7},... | collective-permute-start | bytes 786440 | tf_op jit(solution)/shard_map/ppermute | solution.py:141
  98.2 11.2 %all-to-all-start.1 = ((bf16[8,64,256]{2,1,0:T(8,128)(2,1)}), bf16[8,64,256]{2,1,0:T(8,128)(2,1)}, u32[]{:S(2)}, u32[]{:S(2)}) async-start(bf16[8,64,256]{2,1,0:T(8,128)(2,1)} %bitcast.27), calls=%async_computation.1 | async-start | bytes 524288 | tf_op jit(solution)/shard_map/all_to_all | solution.py:234
  113.5 3.2 %project.5 = (f32[256,256]{1,0:T(8,128)S(1)}, f32[256,256]{1,0:T(8,128)}, f32[256,256]{1,0:T(8,128)}, f32[256,256]{1,0:T(8,128)}) custom-call(s32[4]{0:T(128)S(1)} %pad_add_fusion.place, bf16[256,1024]{1,0:T(8,128)(2,1)S(1)} %get-tuple-element.33.refs_0_, bf16[256,1024]{1,0:T(8,128)(2,1)S(1)} %collective-permute-done.1.refs_1_, ...), custom_call_target="tpu_custom_call" | custom-call | flops 1073741824 | bytes 6291456 | tf_op jit(solution)/shard_map/project/pallas_call | solution.py:210
  117.3 2.7 %collective-permute-start.21 = (f32[256,256]{1,0:T(8,128)}, f32[256,256]{1,0:T(8,128)}, u32[]{:S(2)}, u32[]{:S(2)}) collective-permute-start(f32[256,256]{1,0:T(8,128)} %get-tuple-element.46), channel_id=1, source_target_pairs={{0,2},{2,0},{4,6},{6,4},{8,10},{10,8},{12,14},{14,12},{1,3},{3,1},... | collective-permute-start | bytes 786440 | tf_op jit(solution)/shard_map/ppermute | solution.py:127
  122.4 3.1 %collective-permute-start.16 = (bf16[512,256]{1,0:T(8,128)(2,1)}, bf16[512,256]{1,0:T(8,128)(2,1)}, u32[]{:S(2)}, u32[]{:S(2)}) collective-permute-start(bf16[512,256]{1,0:T(8,128)(2,1)} %get-tuple-element.39.refs_8_), channel_id=1, source_target_pairs={{0,12},{2,14},{4,0},{6,2},{8,4},{10,6},{12,8},{14,10},{1,13},{3,15... | collective-permute-start | bytes 786440 | tf_op jit(solution)/shard_map/ppermute | solution.py:143
  126.7 2.9 %collective-permute-done.22.c = f32[256,256]{1,0:T(8,128)} collective-permute-done((f32[256,256]{1,0:T(8,128)}, f32[256,256]{1,0:T(8,128)}, u32[]{:S(2)}, u32[]{:S(2)}) %collective-permute-start.22) | collective-permute-done | bytes 262176 | tf_op jit(solution)/shard_map/ppermute | solution.py:129
  134.2 4.1 %all-to-all-start.2 = ((bf16[8,64,256]{2,1,0:T(8,128)(2,1)}), bf16[8,64,256]{2,1,0:T(8,128)(2,1)}, u32[]{:S(2)}, u32[]{:S(2)}) async-start(bf16[8,64,256]{2,1,0:T(8,128)(2,1)} %bitcast.26), calls=%async_computation.2 | async-start | bytes 524288 | tf_op jit(solution)/shard_map/all_to_all | solution.py:234
  147.2 2.9 %collective-permute-done.17.b = f32[256,256]{1,0:T(8,128)S(1)} collective-permute-done((f32[256,256]{1,0:T(8,128)S(1)}, f32[256,256]{1,0:T(8,128)S(1)}, u32[]{:S(2)}, u32[]{:S(2)}) %collective-permute-start.17) | collective-permute-done | bytes 262176 | tf_op jit(solution)/shard_map/ppermute | solution.py:127
  150.1 4.7 %collective-permute-done.18.c = f32[256,256]{1,0:T(8,128)S(1)} collective-permute-done((f32[256,256]{1,0:T(8,128)S(1)}, f32[256,256]{1,0:T(8,128)S(1)}, u32[]{:S(2)}, u32[]{:S(2)}) %collective-permute-start.18) | collective-permute-done | bytes 262176 | tf_op jit(solution)/shard_map/ppermute | solution.py:129
  155.8 5.6 %all-to-all-start.3 = ((bf16[8,64,256]{2,1,0:T(8,128)(2,1)}), bf16[8,64,256]{2,1,0:T(8,128)(2,1)S(1)}, u32[]{:S(2)}, u32[]{:S(2)}) async-start(bf16[8,64,256]{2,1,0:T(8,128)(2,1)} %bitcast.19), calls=%async_computation.3 | async-start | bytes 524288 | tf_op jit(solution)/shard_map/all_to_all | solution.py:234
  163.3 4.3 %attend.4.rest_0_ = bf16[256,4096]{1,0:T(8,128)(2,1)} custom-call(bf16[256,4096]{1,0:T(8,128)(2,1)S(1)} %rotate.1.queries, bf16[256,256]{1,0:T(8,128)(2,1)S(1)} %get-tuple-element.59.keyval, f32[256,128]{1,0:T(8,128)S(1)} %get-tuple-element.77.cosine, f32[256,128]{1,0:T(8,128)S(1)} %get-tuple-element.78.sine, f32[256,256]{1,0:T(8,128)S(1)} %fusion.4.mask), custom_call_target="tpu_custom_call" | custom-call | flops 268435456 | bytes 2097152 | tf_op jit(solution)/shard_map/attend/pallas_call | solution.py:237
  167.6 4.3 %attend.5.rest_0_ = bf16[256,4096]{1,0:T(8,128)(2,1)} custom-call(bf16[256,4096]{1,0:T(8,128)(2,1)S(1)} %rotate.1.queries, bf16[256,256]{1,0:T(8,128)(2,1)S(1)} %copy-done.25, f32[256,128]{1,0:T(8,128)S(1)} %get-tuple-element.77.cosine, f32[256,128]{1,0:T(8,128)S(1)} %get-tuple-element.78.sine, ...), custom_call_target="tpu_custom_call", output_to_operand_aliasing={{}: (5, {})} | custom-call | flops 268435456 | bytes 2097152 | tf_op jit(solution)/shard_map/attend/pallas_call | solution.py:237
  171.9 4.3 %attend.6.rest_0_ = bf16[256,4096]{1,0:T(8,128)(2,1)} custom-call(bf16[256,4096]{1,0:T(8,128)(2,1)S(1)} %rotate.1.queries, bf16[256,256]{1,0:T(8,128)(2,1)S(1)} %copy-done.27, f32[256,128]{1,0:T(8,128)S(1)} %get-tuple-element.77.cosine, f32[256,128]{1,0:T(8,128)S(1)} %get-tuple-element.78.sine, ...), custom_call_target="tpu_custom_call", output_to_operand_aliasing={{}: (5, {})} | custom-call | flops 268435456 | bytes 2097152 | tf_op jit(solution)/shard_map/attend/pallas_call | solution.py:237
  176.2 4.3 %attend.7 = bf16[256,4096]{1,0:T(8,128)(2,1)} custom-call(bf16[256,4096]{1,0:T(8,128)(2,1)S(1)} %rotate.1.queries, bf16[256,256]{1,0:T(8,128)(2,1)S(1)} %get-tuple-element.44.keyval, f32[256,128]{1,0:T(8,128)S(1)} %get-tuple-element.77.cosine, f32[256,128]{1,0:T(8,128)S(1)} %get-tuple-element.78.sine, ...), custom_call_target="tpu_custom_call", output_to_operand_aliasing={{}: (5, {})} | custom-call | flops 268435456 | bytes 2097152 | tf_op jit(solution)/shard_map/attend/pallas_call | solution.py:237
  (145 shorter events, 69.9 us)
Async XLA Ops:
  6.4 17.8 %collective-permute-start.1 = (bf16[256,1024]{1,0:T(8,128)(2,1)S(1)}, bf16[256,1024]{1,0:T(8,128)(2,1)S(1)}, u32[]{:S(2)}, u32[]{:S(2)}) collective-permute-start(bf16[256,1024]{1,0:T(8,128)(2,1)S(1)} %get-tuple-element.34), channel_id=1, source_target_pairs={{0,2},{2,0},{4,6},{6,4},{8,10},{10,8},{12,14},{14,12},{1,3},{3,1},... | collective-permute-start | bytes 1572872 | tf_op jit(solution)/shard_map/ppermute | solution.py:127
  9.2 25.2 %collective-permute-start.2 = (bf16[256,1024]{1,0:T(8,128)(2,1)}, bf16[256,1024]{1,0:T(8,128)(2,1)S(1)}, u32[]{:S(2)}, u32[]{:S(2)}) collective-permute-start(bf16[256,1024]{1,0:T(8,128)(2,1)} %get-tuple-element.35), channel_id=1, source_target_pairs={{0,16},{16,0},{1,17},{17,1},{2,18},{18,2},{3,19},{19,3},{4,20},{20... | collective-permute-start | bytes 1572872 | tf_op jit(solution)/shard_map/ppermute | solution.py:129
  10.7 23.7 %collective-permute-start.3 = (bf16[256,1024]{1,0:T(8,128)(2,1)}, bf16[256,1024]{1,0:T(8,128)(2,1)S(1)}, u32[]{:S(2)}, u32[]{:S(2)}) collective-permute-start(bf16[256,1024]{1,0:T(8,128)(2,1)} %get-tuple-element.36), channel_id=1, source_target_pairs={{0,18},{2,16},{4,22},{6,20},{8,26},{10,24},{12,30},{14,28},{16,2},... | collective-permute-start | bytes 1572872 | tf_op jit(solution)/shard_map/ppermute | solution.py:130
  14.9 20.0 %collective-permute-start.9 = (bf16[512,256]{1,0:T(8,128)(2,1)S(1)}, bf16[512,256]{1,0:T(8,128)(2,1)S(1)}, u32[]{:S(2)}, u32[]{:S(2)}) collective-permute-start(bf16[512,256]{1,0:T(8,128)(2,1)S(1)} %get-tuple-element.64.refs_8_), channel_id=1, source_target_pairs={{0,12},{2,14},{4,0},{6,2},{8,4},{10,6},{12,8},{14,10},{1,13},{3,15... | collective-permute-start | bytes 786440 | tf_op jit(solution)/shard_map/ppermute | solution.py:143
  24.2 20.9 %collective-permute-start.4 = (bf16[256,1024]{1,0:T(8,128)(2,1)S(1)}, bf16[256,1024]{1,0:T(8,128)(2,1)S(1)}, u32[]{:S(2)}, u32[]{:S(2)}) collective-permute-start(bf16[256,1024]{1,0:T(8,128)(2,1)S(1)} %get-tuple-element.33.refs_0_), channel_id=1, source_target_pairs={{0,1},{1,0},{2,3},{3,2},{4,5},{5,4},{6,7},{7,6},{8,9},{9,8},{10,11... | collective-permute-start | bytes 1572872 | tf_op jit(solution)/shard_map/ppermute | solution.py:171
  24.2 24.7 %collective-permute-start.5 = (bf16[256,1024]{1,0:T(8,128)(2,1)S(1)}, bf16[256,1024]{1,0:T(8,128)(2,1)S(1)}, u32[]{:S(2)}, u32[]{:S(2)}) collective-permute-start(bf16[256,1024]{1,0:T(8,128)(2,1)S(1)} %collective-permute-done.1.refs_1_), channel_id=1, source_target_pairs={{0,1},{1,0},{2,3},{3,2},{4,5},{5,4},{6,7},{7,6},{8,9},{9,8},{10,11... | collective-permute-start | bytes 1572872 | tf_op jit(solution)/shard_map/ppermute | solution.py:171
  34.4 14.5 %collective-permute-start.6 = (bf16[256,1024]{1,0:T(8,128)(2,1)S(1)}, bf16[256,1024]{1,0:T(8,128)(2,1)S(1)}, u32[]{:S(2)}, u32[]{:S(2)}) collective-permute-start(bf16[256,1024]{1,0:T(8,128)(2,1)S(1)} %collective-permute-done.2.refs_2_), channel_id=1, source_target_pairs={{0,1},{1,0},{2,3},{3,2},{4,5},{5,4},{6,7},{7,6},{8,9},{9,8},{10,11... | collective-permute-start | bytes 1572872 | tf_op jit(solution)/shard_map/ppermute | solution.py:171
  34.4 14.5 %collective-permute-start.7 = (bf16[256,1024]{1,0:T(8,128)(2,1)S(1)}, bf16[256,1024]{1,0:T(8,128)(2,1)S(1)}, u32[]{:S(2)}, u32[]{:S(2)}) collective-permute-start(bf16[256,1024]{1,0:T(8,128)(2,1)S(1)} %collective-permute-done.3.refs_3_), channel_id=1, source_target_pairs={{0,1},{1,0},{2,3},{3,2},{4,5},{5,4},{6,7},{7,6},{8,9},{9,8},{10,11... | collective-permute-start | bytes 1572872 | tf_op jit(solution)/shard_map/ppermute | solution.py:171
  45.0 11.8 %collective-permute-start.10 = (bf16[512,256]{1,0:T(8,128)(2,1)}, bf16[512,256]{1,0:T(8,128)(2,1)}, u32[]{:S(2)}, u32[]{:S(2)}) collective-permute-start(bf16[512,256]{1,0:T(8,128)(2,1)} %get-tuple-element.37.refs_8_), channel_id=1, source_target_pairs={{0,4},{2,6},{4,8},{6,10},{8,12},{10,14},{12,0},{14,2},{1,5},{3,7},... | collective-permute-start | bytes 786440 | tf_op jit(solution)/shard_map/ppermute | solution.py:141
  45.0 29.4 %collective-permute-start.11 = (bf16[512,256]{1,0:T(8,128)(2,1)}, bf16[512,256]{1,0:T(8,128)(2,1)}, u32[]{:S(2)}, u32[]{:S(2)}) collective-permute-start(bf16[512,256]{1,0:T(8,128)(2,1)} %get-tuple-element.37.refs_8_), channel_id=1, source_target_pairs={{0,12},{2,14},{4,0},{6,2},{8,4},{10,6},{12,8},{14,10},{1,13},{3,15... | collective-permute-start | bytes 786440 | tf_op jit(solution)/shard_map/ppermute | solution.py:143
  53.3 13.1 %collective-permute-start.30 = (f32[256,256]{1,0:T(8,128)}, f32[256,256]{1,0:T(8,128)}, u32[]{:S(2)}, u32[]{:S(2)}) collective-permute-start(f32[256,256]{1,0:T(8,128)} %get-tuple-element.57), channel_id=1, source_target_pairs={{0,16},{16,0},{1,17},{17,1},{2,18},{18,2},{3,19},{19,3},{4,20},{20... | collective-permute-start | bytes 786440 | tf_op jit(solution)/shard_map/ppermute | solution.py:129
  54.4 12.0 %collective-permute-start.31 = (f32[256,256]{1,0:T(8,128)}, f32[256,256]{1,0:T(8,128)}, u32[]{:S(2)}, u32[]{:S(2)}) collective-permute-start(f32[256,256]{1,0:T(8,128)} %get-tuple-element.58), channel_id=1, source_target_pairs={{0,18},{2,16},{4,22},{6,20},{8,26},{10,24},{12,30},{14,28},{16,2},... | collective-permute-start | bytes 786440 | tf_op jit(solution)/shard_map/ppermute | solution.py:130
  56.8 21.5 %collective-permute-start.24 = (bf16[512,256]{1,0:T(8,128)(2,1)}, bf16[512,256]{1,0:T(8,128)(2,1)}, u32[]{:S(2)}, u32[]{:S(2)}) collective-permute-start(bf16[512,256]{1,0:T(8,128)(2,1)} %collective-permute-done.10.refs_9_), channel_id=1, source_target_pairs={{0,4},{2,6},{4,8},{6,10},{8,12},{10,14},{12,0},{14,2},{1,5},{3,7},... | collective-permute-start | bytes 786440 | tf_op jit(solution)/shard_map/ppermute | solution.py:141
  70.3 27.9 %all-to-all-start = ((bf16[8,64,256]{2,1,0:T(8,128)(2,1)}), bf16[8,64,256]{2,1,0:T(8,128)(2,1)}, u32[]{:S(2)}, u32[]{:S(2)}) async-start(bf16[8,64,256]{2,1,0:T(8,128)(2,1)} %bitcast.25), calls=%async_computation | async-start | bytes 524288 | tf_op jit(solution)/shard_map/all_to_all | solution.py:234
  74.4 15.6 %collective-permute-start.12 = (bf16[512,256]{1,0:T(8,128)(2,1)}, bf16[512,256]{1,0:T(8,128)(2,1)}, u32[]{:S(2)}, u32[]{:S(2)}) collective-permute-start(bf16[512,256]{1,0:T(8,128)(2,1)} %get-tuple-element.38.refs_8_), channel_id=1, source_target_pairs={{0,4},{2,6},{4,8},{6,10},{8,12},{10,14},{12,0},{14,2},{1,5},{3,7},... | collective-permute-start | bytes 786440 | tf_op jit(solution)/shard_map/ppermute | solution.py:141
  76.3 17.0 %collective-permute-start.13 = (bf16[512,256]{1,0:T(8,128)(2,1)}, bf16[512,256]{1,0:T(8,128)(2,1)S(1)}, u32[]{:S(2)}, u32[]{:S(2)}) collective-permute-start(bf16[512,256]{1,0:T(8,128)(2,1)} %get-tuple-element.38.refs_8_), channel_id=1, source_target_pairs={{0,12},{2,14},{4,0},{6,2},{8,4},{10,6},{12,8},{14,10},{1,13},{3,15... | collective-permute-start | bytes 786440 | tf_op jit(solution)/shard_map/ppermute | solution.py:143
  82.9 13.6 %collective-permute-start.25 = (f32[256,256]{1,0:T(8,128)S(1)}, f32[256,256]{1,0:T(8,128)S(1)}, u32[]{:S(2)}, u32[]{:S(2)}) collective-permute-start(f32[256,256]{1,0:T(8,128)S(1)} %get-tuple-element.51), channel_id=1, source_target_pairs={{0,2},{2,0},{4,6},{6,4},{8,10},{10,8},{12,14},{14,12},{1,3},{3,1},... | collective-permute-start | bytes 786440 | tf_op jit(solution)/shard_map/ppermute | solution.py:127
  90.0 19.5 %collective-permute-start.20 = (bf16[512,256]{1,0:T(8,128)(2,1)}, bf16[512,256]{1,0:T(8,128)(2,1)}, u32[]{:S(2)}, u32[]{:S(2)}) collective-permute-start(bf16[512,256]{1,0:T(8,128)(2,1)} %collective-permute-done.12.refs_9_), channel_id=1, source_target_pairs={{0,4},{2,6},{4,8},{6,10},{8,12},{10,14},{12,0},{14,2},{1,5},{3,7},... | collective-permute-start | bytes 786440 | tf_op jit(solution)/shard_map/ppermute | solution.py:141
  94.0 31.5 %collective-permute-start.14 = (bf16[512,256]{1,0:T(8,128)(2,1)}, bf16[512,256]{1,0:T(8,128)(2,1)}, u32[]{:S(2)}, u32[]{:S(2)}) collective-permute-start(bf16[512,256]{1,0:T(8,128)(2,1)} %get-tuple-element.39.refs_8_), channel_id=1, source_target_pairs={{0,4},{2,6},{4,8},{6,10},{8,12},{10,14},{12,0},{14,2},{1,5},{3,7},... | collective-permute-start | bytes 786440 | tf_op jit(solution)/shard_map/ppermute | solution.py:141
  98.2 36.0 %all-to-all-start.1 = ((bf16[8,64,256]{2,1,0:T(8,128)(2,1)}), bf16[8,64,256]{2,1,0:T(8,128)(2,1)}, u32[]{:S(2)}, u32[]{:S(2)}) async-start(bf16[8,64,256]{2,1,0:T(8,128)(2,1)} %bitcast.27), calls=%async_computation.1 | async-start | bytes 524288 | tf_op jit(solution)/shard_map/all_to_all | solution.py:234
  122.4 16.6 %collective-permute-start.16 = (bf16[512,256]{1,0:T(8,128)(2,1)}, bf16[512,256]{1,0:T(8,128)(2,1)}, u32[]{:S(2)}, u32[]{:S(2)}) collective-permute-start(bf16[512,256]{1,0:T(8,128)(2,1)} %get-tuple-element.39.refs_8_), channel_id=1, source_target_pairs={{0,12},{2,14},{4,0},{6,2},{8,4},{10,6},{12,8},{14,10},{1,13},{3,15... | collective-permute-start | bytes 786440 | tf_op jit(solution)/shard_map/ppermute | solution.py:143
  125.5 13.5 %collective-permute-start.15 = (bf16[512,256]{1,0:T(8,128)(2,1)}, bf16[512,256]{1,0:T(8,128)(2,1)}, u32[]{:S(2)}, u32[]{:S(2)}) collective-permute-start(bf16[512,256]{1,0:T(8,128)(2,1)} %collective-permute-done.14.refs_9_), channel_id=1, source_target_pairs={{0,4},{2,6},{4,8},{6,10},{8,12},{10,14},{12,0},{14,2},{1,5},{3,7},... | collective-permute-start | bytes 786440 | tf_op jit(solution)/shard_map/ppermute | solution.py:141
  134.2 21.6 %all-to-all-start.2 = ((bf16[8,64,256]{2,1,0:T(8,128)(2,1)}), bf16[8,64,256]{2,1,0:T(8,128)(2,1)}, u32[]{:S(2)}, u32[]{:S(2)}) async-start(bf16[8,64,256]{2,1,0:T(8,128)(2,1)} %bitcast.26), calls=%async_computation.2 | async-start | bytes 524288 | tf_op jit(solution)/shard_map/all_to_all | solution.py:234
  155.8 24.7 %all-to-all-start.3 = ((bf16[8,64,256]{2,1,0:T(8,128)(2,1)}), bf16[8,64,256]{2,1,0:T(8,128)(2,1)S(1)}, u32[]{:S(2)}, u32[]{:S(2)}) async-start(bf16[8,64,256]{2,1,0:T(8,128)(2,1)} %bitcast.19), calls=%async_computation.3 | async-start | bytes 524288 | tf_op jit(solution)/shard_map/all_to_all | solution.py:234
  (43 other events, 246.9 us)

commit v2 on v1

v2 whole, which is shorter than its diff:
```python
import functools

import jax
import jax.numpy as jnp
from jax import lax
from jax.experimental import pallas as pl
from jax.experimental.pallas import tpu as pltpu
from jax.sharding import PartitionSpec as P

HD = 128
EPSILON = 1e-06
THETA = 1000000.0
VMEM = pl.BlockSpec(memory_space=pltpu.VMEM)
SMEM = pl.BlockSpec(memory_space=pltpu.SMEM)
FULL = pltpu.CompilerParams(vmem_limit_bytes=56 * 1024 * 1024)
ANY = pl.BlockSpec(memory_space=pl.ANY)
PARAMS = pltpu.CompilerParams(vmem_limit_bytes=16 * 1024 * 1024)


def after(value, *others):
    return lax.optimization_barrier((value, *others))[0]


def cost(flops, nbytes):
    return pl.CostEstimate(flops=flops, bytes_accessed=nbytes, transcendentals=0)


def squares_kernel(hidden, out):
    values = hidden[...].astype(jnp.float32)
    out[...] = jnp.sum(values * values, -1, keepdims=True)


def norm_kernel(place, hidden, inverse, gain, *outs, slices, piece):
    for k, out in enumerate(outs):
        x = place[0] ^ (k & 1)
        y = place[1] ^ (k >> 1)
        for i in range(slices):
            start = pl.multiple_of((i * 4 + x * 2 + y) * piece, piece)
            cols = pl.ds(start, piece)
            values = hidden[:, cols].astype(jnp.float32) * inverse[...] * gain[:, cols]
            out[:, i * piece : (i + 1) * piece] = values.astype(jnp.bfloat16)


def matmul_kernel(place, *refs, count, piece):
    rows = refs[:8]
    blocks = refs[8 : 8 + count]
    outs = refs[8 + count : -4]
    held, weights, row_sems, sems = refs[-4:]
    z, core = place[2], place[3]
    copies = []
    for s, block in enumerate(blocks):
        at = pl.multiple_of(lax.rem(z - s + count, count) * piece, piece)
        copies.append(pltpu.make_async_copy(block, weights.at[pl.ds(at, piece), :], sems.at[s]))
    loads = [pltpu.make_async_copy(rows[i], held.at[i], row_sems.at[i]) for i in range(8)]
    for copy in copies:
        copy.start()
    for k in range(4):
        loads[k].start()
        loads[4 + k].start()
    for copy in copies:
        copy.wait()
    half = count // 2 * piece
    mine = pl.ds(pl.multiple_of(core * half, half), half)
    others = pl.ds(pl.multiple_of((1 - core) * half, half), half)
    middle = weights.shape[1] // 2
    for k in range(4):
        loads[k].wait()
        loads[4 + k].wait()
        total = jnp.dot(
            held[k], weights[mine, :], preferred_element_type=jnp.float32
        ) + jnp.dot(held[4 + k], weights[others, :], preferred_element_type=jnp.float32)
        outs[k & 1][k >> 1] = total[:, :middle]
        outs[2 + (k >> 1)][k & 1] = total[:, middle:]


def fold_kernel(kept_a, came_a, kept_b, came_b, mine, next_a, next_b):
    middle = kept_a.shape[2]
    mine[:, :middle] = kept_a[0] + came_a[0]
    mine[:, middle:] = kept_b[0] + came_b[0]
    next_a[...] = kept_a[1] + came_a[1]
    next_b[...] = kept_b[1] + came_b[1]


def rows_kernel(bias, target, mine, came_a, came_b, *refs, earlier):
    before = refs[:earlier]
    keyval = refs[earlier]
    wide = keyval.shape[1]
    at = bias.shape[1] - wide
    summed = mine[...] + jnp.concatenate([came_a[...], came_b[...]], 1)
    rows = (summed + bias[:, at:]).astype(jnp.bfloat16)
    keyval[...] = rows
    if len(refs) == earlier + 1:
        return
    outgoing = refs[-1]
    slots, count = outgoing.shape[0], rows.shape[0]
    hits = lax.broadcasted_iota(jnp.int32, (slots, count), 0) == target[...]
    onehot = hits.astype(jnp.float32)
    used = jnp.sum(onehot, 1, keepdims=True)
    onehot = onehot.astype(jnp.bfloat16)
    begin = 0
    for block in [ref[...] for ref in before] + [rows]:
        cols = slice(begin, begin + block.shape[1])
        moved = jnp.dot(onehot, block, preferred_element_type=jnp.float32)
        empty = bias[:, cols].astype(jnp.bfloat16).astype(jnp.float32)
        outgoing[:, cols] = jnp.where(used > 0, moved, empty).astype(jnp.bfloat16)
        begin += block.shape[1]


def turn(values, cosine, sine):
    half = HD // 2
    turned = jnp.concatenate([values[:, half:], values[:, :half]], -1)
    return values * cosine + turned * sine


def rotate_kernel(queries, cosine, sine, out):
    for h in range(queries.shape[1] // HD):
        cols = slice(h * HD, (h + 1) * HD)
        values = queries[:, cols].astype(jnp.float32)
        out[:, cols] = turn(values, cosine[...], sine[...]).astype(jnp.bfloat16)


def attend_kernel(queries, keyval, cosine, sine, start, *rest, group):
    out = rest[-1]
    count = keyval.shape[0]
    token = lax.broadcasted_iota(jnp.int32, (count, count), 0)
    other = lax.broadcasted_iota(jnp.int32, (count, count), 1)
    allowed = (other >= start[...]) & (other <= token)
    mask = jnp.where(allowed, jnp.float32(0.0), jnp.float32(-1e30))
    half = count // 2
    keys = turn(keyval[:, :HD].astype(jnp.float32), cosine[...], sine[...])
    keys = keys.astype(jnp.bfloat16)
    values = keyval[:, HD:]
    for first, reach in ((0, half), (half, count)):
        rows = slice(first, first + half)
        stacked = jnp.concatenate(
            [queries[rows, h * HD : (h + 1) * HD] for h in range(group)], 0
        )
        scores = lax.dot_general(
            stacked,
            keys[:reach],
            (((1,), (1,)), ((), ())),
            preferred_element_type=jnp.float32,
        )
        masked = scores.reshape(group, half, reach) * HD ** (-0.5) + mask[rows, :reach]
        top = jnp.max(masked, -1, keepdims=True)
        weights = jnp.exp(masked - top)
        total = jnp.sum(weights, -1, keepdims=True)
        probs = (weights * (1.0 / total)).astype(jnp.bfloat16)
        mixed = jnp.dot(
            probs.reshape(group * half, reach),
            values[:reach],
            preferred_element_type=jnp.float32,
        ).astype(jnp.bfloat16)
        for h in range(group):
            out[rows, h * HD : (h + 1) * HD] = mixed[h * half : (h + 1) * half]


def chunks_of(heads):
    sizes = [heads // 2, heads - heads // 2]
    return [(sum(sizes[:i]), size) for i, size in enumerate(sizes) if size]


def shards(hidden, queries, lengths, scoring_rank, norm_gain, kv_weight, kv_bias):
    ranks = lax.axis_size("fz") * 2
    steps = ranks // 2
    count, features = hidden.shape
    width = features * lax.axis_size("tp")
    depth, columns = kv_weight.shape
    piece = depth // 2
    heads = columns // (2 * HD)
    group = queries.shape[1] // HD // heads
    capacity = 2 * count // ranks
    slots = capacity * ranks

    y = lax.axis_index("groups")
    core = lax.axis_index("tp")
    x, z = lax.axis_index("fx"), lax.axis_index("fz")
    place = jnp.stack([x, y, z, core]).astype(jnp.int32)

    right = [(i, (i + 1) % steps) for i in range(steps)]
    left = [(i, (i - 1) % steps) for i in range(steps)]
    flip = [(0, 1), (1, 0)]
    flip_both = [(i, 3 - i) for i in range(4)]

    def to_chip(k, array):
        if k == 1:
            return lax.ppermute(array, "fx", flip)
        if k == 2:
            return lax.ppermute(array, "groups", flip)
        return lax.ppermute(array, ("groups", "fx"), flip_both)

    hidden_f = hidden.astype(jnp.float32)
    squares = pl.pallas_call(
        squares_kernel,
        out_shape=jax.ShapeDtypeStruct((count, 1), jnp.float32),
        in_specs=[VMEM],
        out_specs=VMEM,
        compiler_params=PARAMS,
        cost_estimate=cost(2 * count * features, 1 << 20),
        name="squares",
    )(hidden)

    chunks = chunks_of(heads)
    gathered = []

    def gather(first, number, *waits):
        cut = (piece, number * 2 * HD)
        if not gathered:
            source, end = kv_weight, squares
        else:
            source, end = after(kv_weight, gathered[-1][-1], *waits), gathered[-1][steps // 2]
        block = lax.dynamic_slice(source, (y * piece, first * 2 * HD), cut)
        ups, downs = [block], [after(block, end)]
        for _ in range(steps // 2):
            ups.append(lax.ppermute(ups[-1], "fz", right))
        for _ in range((steps - 1) // 2):
            downs.append(lax.ppermute(downs[-1], "fz", left))
        gathered.append(ups + downs[:0:-1])

    for chunk in chunks:
        gather(*chunk)

    squares = squares + lax.ppermute(squares, "tp", flip)
    inverse_rms = lax.rsqrt(squares / width + EPSILON)
    slices = features // (4 * piece)
    if piece % HD == 0:
        normed = pl.pallas_call(
            functools.partial(norm_kernel, slices=slices, piece=piece),
            out_shape=[jax.ShapeDtypeStruct((count, features // 4), jnp.bfloat16)] * 4,
            in_specs=[SMEM] + [VMEM] * 3,
            out_specs=[VMEM] * 4,
            compiler_params=PARAMS,
            cost_estimate=cost(3 * count * features, 4 * count * features),
            name="norm",
        )(place, hidden, inverse_rms, norm_gain[None, :])
    else:
        whole = (hidden_f * inverse_rms * norm_gain[None, :]).astype(jnp.bfloat16)
        whole = whole.reshape(count, slices, 2, 2, piece)
        normed = []
        for k in range(4):
            part = lax.dynamic_index_in_dim(whole, x ^ (k & 1), 2, False)
            part = lax.dynamic_index_in_dim(part, y ^ (k >> 1), 2, False)
            normed.append(part.reshape(count, features // 4))
    own = [normed[0]] + [to_chip(k, normed[k]) for k in (1, 2, 3)]
    late = [after(own[0], own[2]), after(own[1], gathered[0][1])]
    peer = [lax.ppermute(block, "tp", flip) for block in late + own[2:]]

    dest = scoring_rank[:, 0]
    index = jnp.arange(count, dtype=jnp.int32)
    earlier = (dest[:, None] == dest[None, :]) & (index[:, None] < index[None, :])
    slot = jnp.sum(earlier.astype(jnp.int32), 0)
    target = dest * capacity + slot
    row = lengths[0]
    ends = jnp.cumsum(row)
    starts = ends - row
    within = (index[:, None] >= starts[None, :]) & (index[:, None] < ends[None, :])
    start = jnp.sum(jnp.where(within, starts[None, :], 0), 1)
    position = index - start
    freq = THETA ** (-jnp.arange(HD // 2, dtype=jnp.float32) * 2.0 / HD)
    angles = position.astype(jnp.float32)[:, None] * freq[None, :]
    cosine, sine = jnp.cos(angles), jnp.sin(angles)
    cosine = jnp.concatenate([cosine, cosine], 1)
    sine = jnp.concatenate([-sine, sine], 1)
    turned = pl.pallas_call(
        rotate_kernel,
        out_shape=jax.ShapeDtypeStruct(queries.shape, jnp.bfloat16),
        in_specs=[VMEM] * 3,
        out_specs=VMEM,
        compiler_params=PARAMS,
        cost_estimate=cost(4 * count * queries.shape[1], 4 * count * queries.shape[1]),
        name="rotate",
    )(queries, cosine, sine)

    bias = kv_bias[None, :]
    attended = None
    waiting, sent = [], 0
    scored_rows = None
    last = (turned, target, start)
    for n, (first, number) in enumerate(chunks):
        wide = number * 2 * HD
        middle = wide // 2
        where = after(place, *last)
        kept_a, sent_a, kept_b, sent_b = pl.pallas_call(
            functools.partial(matmul_kernel, count=steps, piece=piece),
            out_shape=[jax.ShapeDtypeStruct((2, count, middle), jnp.float32)] * 4,
            in_specs=[SMEM] + [ANY] * (8 + steps),
            out_specs=[VMEM] * 4,
            scratch_shapes=[
                pltpu.VMEM((8, count, steps * piece // 2), jnp.bfloat16),
                pltpu.VMEM((steps * piece, wide), jnp.bfloat16),
                pltpu.SemaphoreType.DMA((8,)),
                pltpu.SemaphoreType.DMA((steps,)),
            ],
            compiler_params=FULL,
            cost_estimate=cost(2 * 4 * count * steps * piece * wide, 1 << 20),
            name="project",
        )(where, *own, *peer, *gathered[n])
        came_a, came_b = to_chip(1, sent_a), to_chip(2, sent_b)
        if n + 1 < len(chunks):
            came_a = after(came_a, gathered[n + 1][1])
        mine, next_a, next_b = pl.pallas_call(
            fold_kernel,
            out_shape=[jax.ShapeDtypeStruct((count, wide), jnp.float32)]
            + [jax.ShapeDtypeStruct((count, middle), jnp.float32)] * 2,
            in_specs=[VMEM] * 4,
            out_specs=[VMEM] * 3,
            compiler_params=PARAMS,
            cost_estimate=cost(2 * count * wide, 1 << 18),
            name="fold",
        )(kept_a, came_a, kept_b, came_b)
        share = [mine, to_chip(2, next_a), to_chip(1, next_b)]
        end = first * 2 * HD + wide
        added = bias[:, sent:end]
        if n + 1 < len(chunks):
            added = after(added, gathered[n + 1][-1])
        if attended is not None:
            added, attended = lax.optimization_barrier((added, attended))
        routed = True
        earlier = waiting if routed else []
        outs = [jax.ShapeDtypeStruct((count, wide), jnp.bfloat16)]
        if routed:
            outs.append(jax.ShapeDtypeStruct((slots, end - sent), jnp.bfloat16))
        keyval, *outgoing = pl.pallas_call(
            functools.partial(rows_kernel, earlier=len(earlier)),
            out_shape=outs,
            in_specs=[VMEM] * (5 + len(earlier)),
            out_specs=[VMEM] * len(outs),
            compiler_params=PARAMS,
            cost_estimate=cost(2 * slots * count * wide, 1 << 20),
            name="rows",
        )(added, target[None, :], *share, *earlier)
        last = (keyval,)
        waiting.append(keyval)
        if routed:
            received = lax.all_to_all(outgoing[0], ("fz", "fx"), split_axis=0, concat_axis=0, tiled=True)
            columns_at = pl.BlockSpec((slots, end - sent), lambda i, at=sent // (end - sent): (0, at))
            before = [] if scored_rows is None else [scored_rows]
            scored_rows = pl.pallas_call(
                lambda *refs: refs[-1].__setitem__(Ellipsis, refs[0][...]),
                out_shape=jax.ShapeDtypeStruct((slots, columns), jnp.bfloat16),
                grid=(1,),
                in_specs=[pl.BlockSpec((slots, end - sent), lambda i: (0, 0))] + [ANY] * len(before),
                out_specs=columns_at,
                input_output_aliases={1: 0} if before else {},
                compiler_params=PARAMS,
                cost_estimate=cost(1, 1 << 19),
                name="store",
            )(received, *before)
            waiting, sent = [], end
        before = [] if attended is None else [attended]
        attended = pl.pallas_call(
            functools.partial(attend_kernel, group=group),
            out_shape=jax.ShapeDtypeStruct(queries.shape, jnp.bfloat16),
            grid=(number,),
            in_specs=[
                pl.BlockSpec((count, group * HD), lambda i, at=first: (0, at + i)),
                pl.BlockSpec((count, 2 * HD), lambda i: (0, i)),
                pl.BlockSpec((count, HD), lambda i: (0, 0)),
                pl.BlockSpec((count, HD), lambda i: (0, 0)),
                pl.BlockSpec((count, 1), lambda i: (0, 0)),
            ]
            + [ANY] * len(before),
            out_specs=pl.BlockSpec((count, group * HD), lambda i, at=first: (0, at + i)),
            input_output_aliases={5: 0} if before else {},
            compiler_params=PARAMS,
            cost_estimate=cost(4 * number * group * count * count * HD, 1 << 20),
            name="attend",
        )(turned, keyval, cosine, sine, start[:, None], *before)
    return (attended, scored_rows)


def solution(mesh):
    groups, ranks, cores = (mesh.shape[name] for name in ("groups", "fsdp", "tp"))
    devices = mesh.devices.reshape(groups, ranks // 2, 2, cores)
    paired = jax.sharding.Mesh(devices, ("groups", "fz", "fx", "tp"))
    rows = ("groups", "fz", "fx")
    placed = (
        P(rows, "tp"),
        P(rows, "tp"),
        P(rows, None),
        P(rows, None),
        P("tp"),
        P(("fz", "fx"), "tp"),
        P("tp"),
    )
    return jax.shard_map(
        shards,
        mesh=paired,
        in_specs=placed,
        out_specs=(P(rows, "tp"), P(rows, "tp")),
        check_vma=False,
    )
```

time: 184 us -> 134 us (0.73)
  starting transfers between devices: 65.6 us -> 30.1 us
  other arithmetic: 8.32 us -> 1.18 us
  Pallas kernels: 35.3 us -> 30.3 us
    ppermute x32 -> x22, starting transfers between devices: 40.7 us -> 21.3 us  [the longest x5 6.45 us: to_chip(): return lax.ppermute(array, 'fx', flip)]
    all_to_all x4 -> x2, starting transfers between devices: 24.9 us -> 8.78 us  [shards(): lax.all_to_all(outgoing[0], ('fz', 'fx'), split_axis=0, concat_axis=0, ti...]
    pallas_call x12 -> x11, Pallas kernels: 32.2 us -> 28.1 us  [the longest x2 15.1 us: shards(): pl.pallas_call(functools.partial(matmul_kernel, count=steps, piece=piece)...]
    ppermute x32 -> x22, waiting for transfers between devices: 52 us -> 48.1 us  [the longest x5 19.8 us: to_chip(): return lax.ppermute(array, 'fx', flip)]
    all_to_all x4 -> x2, waiting for transfers between devices: 0.01 us -> 3.21 us  [shards(): lax.all_to_all(outgoing[0], ('fz', 'fx'), split_axis=0, concat_axis=0, ti...]
    reduce_sum x1 -> x0, other arithmetic: 2.23 us -> none  [shards(): squares = jnp.sum(hidden_f * hidden_f, -1, keepdims=True)]
    concatenate x1 -> x0, other arithmetic: 2.22 us -> none  [shards(): scored_rows = jnp.concatenate(received, 1)]
    slice x2 -> x1, local copies, waits for them, and re-layouts: 2.13 us -> 0.01 us  [shards(): added = bias[:, sent:end]]
  transfers between devices with their start and end apart: 36 -> 24, of which waited for: 11 -> 13; matrix products, arithmetic and copies ran while one was open for 4% -> 2% of each run, Pallas kernels for 18% -> 22%
where the time goes in v2:
time: 134 us; the launch traced here: 133 us
  waiting for transfers between devices  51.3 us (38%)
  Pallas kernels  30.3 us (23%)
  starting transfers between devices  30.1 us (22%)
  local copies, waits for them, and re-layouts  19.3 us (14%)
    ppermute x5, waiting for transfers between devices, to_chip(): return lax.ppermute(array, 'fx', flip)  19.8 us
    unnamed x64, local copies, waits for them, and re-layouts  18.3 us
    pallas_call x2, Pallas kernels, shards(): pl.pallas_call(functools.partial(matmul_kernel, count=steps, piece=piece)...  15.1 us
    ppermute x5, waiting for transfers between devices, to_chip(): return lax.ppermute(array, 'groups', flip)  8.97 us
    ppermute x4, waiting for transfers between devices, gather(): ups.append(lax.ppermute(ups[-1], 'fz', right))  8.96 us
    all_to_all x2, starting transfers between devices, shards(): lax.all_to_all(outgoing[0], ('fz', 'fx'), split_axis=0, concat_axis=0, ti...  8.78 us
    pallas_call x2, Pallas kernels, shards(): pl.pallas_call(functools.partial(attend_kernel, group=group), out_shape=j...  7.4 us
    ppermute x5, starting transfers between devices, to_chip(): return lax.ppermute(array, 'fx', flip)  6.45 us
  transfers between devices with their start and end apart: 24, of which 13 were waited for; matrix products, arithmetic and copies ran while one was open for 2% of the time, Pallas kernels for 22%

profile of v2, /device:TPU:0, one launch (start us, length us, event | category | flops | bytes accessed | tf_op | source)
XLA Modules:
  0.0 133.2 jit_solution(11019915441537902971)
XLA Ops:
  0.7 1.7 %copy-done.4 = bf16[256,4096]{1,0:T(8,128)(2,1)S(1)} copy-done((bf16[256,4096]{1,0:T(8,128)(2,1)S(1)}, bf16[256,4096]{1,0:T(8,128)(2,1)}, u32[]{:S(2)}) %copy-start.4) | copy-done | bytes 2097176
  4.2 2.6 %collective-permute-start.1 = (bf16[512,512]{1,0:T(8,128)(2,1)}, bf16[512,512]{1,0:T(8,128)(2,1)}, u32[]{:S(2)}, u32[]{:S(2)}) collective-permute-start(bf16[512,512]{1,0:T(8,128)(2,1)} %constant_dynamic-slice_fusion.1.refs_8_), channel_id=1, source_target_pairs={{0,4},{4,8},{8,12},{12,0},{1,5},{5,9},{9,13},{13,1},{2,6},{6,10},{... | collective-permute-start | bytes 1572872 | tf_op jit(solution)/shard_map/ppermute | solution.py:215
  6.8 2.0 %collective-permute-start = (bf16[512,512]{1,0:T(8,128)(2,1)}, bf16[512,512]{1,0:T(8,128)(2,1)}, u32[]{:S(2)}, u32[]{:S(2)}) collective-permute-start(bf16[512,512]{1,0:T(8,128)(2,1)} %constant_dynamic-slice_fusion.1.refs_8_), channel_id=1, source_target_pairs={{0,12},{4,0},{8,4},{12,8},{1,13},{5,1},{9,5},{13,9},{2,14},{6,2},{... | collective-permute-start | bytes 1572872 | tf_op jit(solution)/shard_map/ppermute | solution.py:217
  11.8 1.8 %collective-permute-start.6 = (bf16[256,1024]{1,0:T(8,128)(2,1)S(1)}, bf16[256,1024]{1,0:T(8,128)(2,1)S(1)}, u32[]{:S(2)}, u32[]{:S(2)}) collective-permute-start(bf16[256,1024]{1,0:T(8,128)(2,1)S(1)} %get-tuple-element.42), channel_id=1, source_target_pairs={{0,16},{16,0},{1,17},{17,1},{2,18},{18,2},{3,19},{19,3},{4,20},{20... | collective-permute-start | bytes 1572872 | tf_op jit(solution)/shard_map/ppermute | solution.py:189
  15.4 6.5 %collective-permute-done.1.refs_9_ = bf16[512,512]{1,0:T(8,128)(2,1)} collective-permute-done((bf16[512,512]{1,0:T(8,128)(2,1)}, bf16[512,512]{1,0:T(8,128)(2,1)}, u32[]{:S(2)}, u32[]{:S(2)}) %collective-permute-start.1) | collective-permute-done | bytes 524320 | tf_op jit(solution)/shard_map/ppermute | solution.py:215
  21.9 4.0 %collective-permute-done.6.refs_2_ = bf16[256,1024]{1,0:T(8,128)(2,1)S(1)} collective-permute-done((bf16[256,1024]{1,0:T(8,128)(2,1)S(1)}, bf16[256,1024]{1,0:T(8,128)(2,1)S(1)}, u32[]{:S(2)}, u32[]{:S(2)}) %collective-permute-start.6) | collective-permute-done | bytes 524320 | tf_op jit(solution)/shard_map/ppermute | solution.py:189
  25.9 2.5 %collective-permute-done.5.refs_1_ = bf16[256,1024]{1,0:T(8,128)(2,1)S(1)} collective-permute-done((bf16[256,1024]{1,0:T(8,128)(2,1)S(1)}, bf16[256,1024]{1,0:T(8,128)(2,1)S(1)}, u32[]{:S(2)}, u32[]{:S(2)}) %collective-permute-start.5) | collective-permute-done | bytes 524320 | tf_op jit(solution)/shard_map/ppermute | solution.py:187
  28.4 3.9 %collective-permute-done.refs_11_ = bf16[512,512]{1,0:T(8,128)(2,1)} collective-permute-done((bf16[512,512]{1,0:T(8,128)(2,1)}, bf16[512,512]{1,0:T(8,128)(2,1)}, u32[]{:S(2)}, u32[]{:S(2)}) %collective-permute-start) | collective-permute-done | bytes 524320 | tf_op jit(solution)/shard_map/ppermute | solution.py:217
  32.3 6.0 %collective-permute-done.7.refs_3_ = bf16[256,1024]{1,0:T(8,128)(2,1)S(1)} collective-permute-done((bf16[256,1024]{1,0:T(8,128)(2,1)S(1)}, bf16[256,1024]{1,0:T(8,128)(2,1)S(1)}, u32[]{:S(2)}, u32[]{:S(2)}) %collective-permute-start.7) | collective-permute-done | bytes 524320 | tf_op jit(solution)/shard_map/ppermute | solution.py:190
  41.6 2.5 %collective-permute-done.2.refs_10_ = bf16[512,512]{1,0:T(8,128)(2,1)S(1)} collective-permute-done((bf16[512,512]{1,0:T(8,128)(2,1)}, bf16[512,512]{1,0:T(8,128)(2,1)S(1)}, u32[]{:S(2)}, u32[]{:S(2)}) %collective-permute-start.2) | collective-permute-done | bytes 524320 | tf_op jit(solution)/shard_map/ppermute | solution.py:215
  46.3 7.5 %project.2 = (f32[2,256,256]{2,1,0:T(8,128)}, f32[2,256,256]{2,1,0:T(8,128)}, f32[2,256,256]{2,1,0:T(8,128)}, f32[2,256,256]{2,1,0:T(8,128)}) custom-call(s32[4]{0:T(128)} %copy-done.17, bf16[256,1024]{1,0:T(8,128)(2,1)} %copy-done.18, bf16[256,1024]{1,0:T(8,128)(2,1)} %copy-done.23, bf16[256,1024]{1,0:T(8,128)(2,1)} %copy-done.22, ...), custom_call_target="tpu_custom_call" | custom-call | flops 2147483648 | bytes 1048576 | tf_op jit(solution)/shard_map/project/pallas_call | solution.py:283
  56.9 3.6 %collective-permute-start.3 = (bf16[512,512]{1,0:T(8,128)(2,1)S(1)}, bf16[512,512]{1,0:T(8,128)(2,1)S(1)}, u32[]{:S(2)}, u32[]{:S(2)}) collective-permute-start(bf16[512,512]{1,0:T(8,128)(2,1)S(1)} %constant_dynamic-slice_fusion.refs_8_), channel_id=1, source_target_pairs={{0,12},{4,0},{8,4},{12,8},{1,13},{5,1},{9,5},{13,9},{2,14},{6,2},{... | collective-permute-start | bytes 1572872 | tf_op jit(solution)/shard_map/ppermute | solution.py:217
  60.6 6.2 %collective-permute-done.12.came_a = f32[2,256,256]{2,1,0:T(8,128)S(1)} collective-permute-done((f32[2,256,256]{2,1,0:T(8,128)}, f32[2,256,256]{2,1,0:T(8,128)S(1)}, u32[]{:S(2)}, u32[]{:S(2)}) %collective-permute-start.12) | collective-permute-done | bytes 524320 | tf_op jit(solution)/shard_map/ppermute | solution.py:187
  72.9 3.8 %collective-permute-done.15.came_a = f32[256,256]{1,0:T(8,128)S(1)} collective-permute-done((f32[256,256]{1,0:T(8,128)S(1)}, f32[256,256]{1,0:T(8,128)S(1)}, u32[]{:S(2)}, u32[]{:S(2)}) %collective-permute-start.15) | collective-permute-done | bytes 262176 | tf_op jit(solution)/shard_map/ppermute | solution.py:189
  80.1 3.8 %all-to-all-start.1 = ((bf16[8,64,512]{2,1,0:T(8,128)(2,1)}), bf16[8,64,512]{2,1,0:T(8,128)(2,1)S(1)}, u32[]{:S(2)}, u32[]{:S(2)}) async-start(bf16[8,64,512]{2,1,0:T(8,128)(2,1)} %bitcast.16), calls=%async_computation.1 | async-start | bytes 1048576 | tf_op jit(solution)/shard_map/all_to_all | solution.py:335
  83.9 7.5 %project.3 = (f32[2,256,256]{2,1,0:T(8,128)}, f32[2,256,256]{2,1,0:T(8,128)}, f32[2,256,256]{2,1,0:T(8,128)}, f32[2,256,256]{2,1,0:T(8,128)}) custom-call(s32[4]{0:T(128)} %copy-done.17, bf16[256,1024]{1,0:T(8,128)(2,1)} %copy-done.18, bf16[256,1024]{1,0:T(8,128)(2,1)} %copy-done.23, bf16[256,1024]{1,0:T(8,128)(2,1)} %copy-done.22, ...), custom_call_target="tpu_custom_call" | custom-call | flops 2147483648 | bytes 1048576 | tf_op jit(solution)/shard_map/project/pallas_call | solution.py:283
  91.4 2.1 %collective-permute-start.18 = (f32[2,256,256]{2,1,0:T(8,128)}, f32[2,256,256]{2,1,0:T(8,128)S(1)}, u32[]{:S(2)}, u32[]{:S(2)}) collective-permute-start(f32[2,256,256]{2,1,0:T(8,128)} %get-tuple-element.58), channel_id=1, source_target_pairs={{0,2},{2,0},{1,3},{3,1},{4,6},{6,4},{5,7},{7,5},{8,10},{10,8},{9,1... | collective-permute-start | bytes 1572872 | tf_op jit(solution)/shard_map/ppermute | solution.py:187
  94.0 9.5 %collective-permute-done.18.came_a = f32[2,256,256]{2,1,0:T(8,128)S(1)} collective-permute-done((f32[2,256,256]{2,1,0:T(8,128)}, f32[2,256,256]{2,1,0:T(8,128)S(1)}, u32[]{:S(2)}, u32[]{:S(2)}) %collective-permute-start.18) | collective-permute-done | bytes 524320 | tf_op jit(solution)/shard_map/ppermute | solution.py:187
  108.0 1.6 %copy-done.2 = bf16[256,4096]{1,0:T(8,128)(2,1)S(1)} copy-done((bf16[256,4096]{1,0:T(8,128)(2,1)S(1)}, bf16[256,4096]{1,0:T(8,128)(2,1)}, u32[]{:S(2)}) %copy-start.2) | copy-done | bytes 2097176
  110.5 3.7 %attend.2.rest_0_ = bf16[256,4096]{1,0:T(8,128)(2,1)} custom-call(bf16[256,4096]{1,0:T(8,128)(2,1)S(1)} %copy-done.2, bf16[256,512]{1,0:T(8,128)(2,1)S(1)} %copy-done.13, f32[256,128]{1,0:T(8,128)S(1)} %get-tuple-element.73.cosine, f32[256,128]{1,0:T(8,128)S(1)} %get-tuple-element.74.sine, s32[256,1]{1,0:T(8,128)S(1)} %copy.15.start), custom_call_target="tpu_custom_call" | custom-call | flops 536870912 | bytes 1048576 | tf_op jit(solution)/shard_map/attend/pallas_call | solution.py:351
  117.1 5.0 %all-to-all-start = ((bf16[8,64,512]{2,1,0:T(8,128)(2,1)}), bf16[8,64,512]{2,1,0:T(8,128)(2,1)S(1)}, u32[]{:S(2)}, u32[]{:S(2)}) async-start(bf16[8,64,512]{2,1,0:T(8,128)(2,1)} %bitcast.25), calls=%async_computation | async-start | bytes 1048576 | tf_op jit(solution)/shard_map/all_to_all | solution.py:335
  122.1 1.6 %copy-done.3 = bf16[256,4096]{1,0:T(8,128)(2,1)S(1)} copy-done((bf16[256,4096]{1,0:T(8,128)(2,1)S(1)}, bf16[256,4096]{1,0:T(8,128)(2,1)}, u32[]{:S(2)}) %copy-start.3) | copy-done | bytes 2097176
  124.6 3.7 %attend.3 = bf16[256,4096]{1,0:T(8,128)(2,1)} custom-call(bf16[256,4096]{1,0:T(8,128)(2,1)S(1)} %copy-done.3, bf16[256,512]{1,0:T(8,128)(2,1)S(1)} %copy-done.15, f32[256,128]{1,0:T(8,128)S(1)} %get-tuple-element.73.cosine, f32[256,128]{1,0:T(8,128)S(1)} %get-tuple-element.74.sine, s32[256,1]{1,0:T(8,128)S(1)} %copy.15.start, ...), custom_call_target="tpu_custom_call", output_to_operand_aliasing={{}: (5, {})} | custom-call | flops 536870912 | bytes 1048576 | tf_op jit(solution)/shard_map/attend/pallas_call | solution.py:351
  129.2 3.2 %all-to-all-done = bf16[8,64,512]{2,1,0:T(8,128)(2,1)S(1)} async-done(((bf16[8,64,512]{2,1,0:T(8,128)(2,1)}), bf16[8,64,512]{2,1,0:T(8,128)(2,1)S(1)}, u32[]{:S(2)}, u32[]{:S(2)}) %all-to-all-start) | async-done | bytes 524320 | tf_op jit(solution)/shard_map/all_to_all | solution.py:335
  (116 shorter events, 35.9 us)
Async XLA Ops:
  2.9 6.2 %collective-permute-start.4 = (f32[256,1]{1,0:T(8,128)S(1)}, f32[256,1]{1,0:T(8,128)S(1)}, u32[]{:S(2)}, u32[]{:S(2)}) collective-permute-start(f32[256,1]{1,0:T(8,128)S(1)} %squares.1), channel_id=1, source_target_pairs={{0,1},{1,0},{2,3},{3,2},{4,5},{5,4},{6,7},{7,6},{8,9},{9,8},{10,11... | collective-permute-start | bytes 3080 | tf_op jit(solution)/shard_map/ppermute | solution.py:223
  4.2 17.8 %collective-permute-start.1 = (bf16[512,512]{1,0:T(8,128)(2,1)}, bf16[512,512]{1,0:T(8,128)(2,1)}, u32[]{:S(2)}, u32[]{:S(2)}) collective-permute-start(bf16[512,512]{1,0:T(8,128)(2,1)} %constant_dynamic-slice_fusion.1.refs_8_), channel_id=1, source_target_pairs={{0,4},{4,8},{8,12},{12,0},{1,5},{5,9},{9,13},{13,1},{2,6},{6,10},{... | collective-permute-start | bytes 1572872 | tf_op jit(solution)/shard_map/ppermute | solution.py:215
  6.8 25.6 %collective-permute-start = (bf16[512,512]{1,0:T(8,128)(2,1)}, bf16[512,512]{1,0:T(8,128)(2,1)}, u32[]{:S(2)}, u32[]{:S(2)}) collective-permute-start(bf16[512,512]{1,0:T(8,128)(2,1)} %constant_dynamic-slice_fusion.1.refs_8_), channel_id=1, source_target_pairs={{0,12},{4,0},{8,4},{12,8},{1,13},{5,1},{9,5},{13,9},{2,14},{6,2},{... | collective-permute-start | bytes 1572872 | tf_op jit(solution)/shard_map/ppermute | solution.py:217
  11.8 14.1 %collective-permute-start.6 = (bf16[256,1024]{1,0:T(8,128)(2,1)S(1)}, bf16[256,1024]{1,0:T(8,128)(2,1)S(1)}, u32[]{:S(2)}, u32[]{:S(2)}) collective-permute-start(bf16[256,1024]{1,0:T(8,128)(2,1)S(1)} %get-tuple-element.42), channel_id=1, source_target_pairs={{0,16},{16,0},{1,17},{17,1},{2,18},{18,2},{3,19},{19,3},{4,20},{20... | collective-permute-start | bytes 1572872 | tf_op jit(solution)/shard_map/ppermute | solution.py:189
  13.6 14.8 %collective-permute-start.5 = (bf16[256,1024]{1,0:T(8,128)(2,1)S(1)}, bf16[256,1024]{1,0:T(8,128)(2,1)S(1)}, u32[]{:S(2)}, u32[]{:S(2)}) collective-permute-start(bf16[256,1024]{1,0:T(8,128)(2,1)S(1)} %get-tuple-element.41), channel_id=1, source_target_pairs={{0,2},{2,0},{1,3},{3,1},{4,6},{6,4},{5,7},{7,5},{8,10},{10,8},{9,1... | collective-permute-start | bytes 1572872 | tf_op jit(solution)/shard_map/ppermute | solution.py:187
  15.1 23.2 %collective-permute-start.7 = (bf16[256,1024]{1,0:T(8,128)(2,1)S(1)}, bf16[256,1024]{1,0:T(8,128)(2,1)S(1)}, u32[]{:S(2)}, u32[]{:S(2)}) collective-permute-start(bf16[256,1024]{1,0:T(8,128)(2,1)S(1)} %get-tuple-element.43), channel_id=1, source_target_pairs={{0,18},{2,16},{16,2},{18,0},{1,19},{3,17},{17,3},{19,1},{4,22},{6,... | collective-permute-start | bytes 1572872 | tf_op jit(solution)/shard_map/ppermute | solution.py:190
  21.9 22.2 %collective-permute-start.2 = (bf16[512,512]{1,0:T(8,128)(2,1)}, bf16[512,512]{1,0:T(8,128)(2,1)S(1)}, u32[]{:S(2)}, u32[]{:S(2)}) collective-permute-start(bf16[512,512]{1,0:T(8,128)(2,1)} %collective-permute-done.1.refs_9_), channel_id=1, source_target_pairs={{0,4},{4,8},{8,12},{12,0},{1,5},{5,9},{9,13},{13,1},{2,6},{6,10},{... | collective-permute-start | bytes 1572872 | tf_op jit(solution)/shard_map/ppermute | solution.py:215
  25.9 18.2 %collective-permute-start.8 = (bf16[256,1024]{1,0:T(8,128)(2,1)S(1)}, bf16[256,1024]{1,0:T(8,128)(2,1)S(1)}, u32[]{:S(2)}, u32[]{:S(2)}) collective-permute-start(bf16[256,1024]{1,0:T(8,128)(2,1)S(1)} %get-tuple-element.44.refs_0_), channel_id=1, source_target_pairs={{0,1},{1,0},{2,3},{3,2},{4,5},{5,4},{6,7},{7,6},{8,9},{9,8},{10,11... | collective-permute-start | bytes 1572872 | tf_op jit(solution)/shard_map/ppermute | solution.py:246
  28.4 15.7 %collective-permute-start.9 = (bf16[256,1024]{1,0:T(8,128)(2,1)S(1)}, bf16[256,1024]{1,0:T(8,128)(2,1)S(1)}, u32[]{:S(2)}, u32[]{:S(2)}) collective-permute-start(bf16[256,1024]{1,0:T(8,128)(2,1)S(1)} %collective-permute-done.5.refs_1_), channel_id=1, source_target_pairs={{0,1},{1,0},{2,3},{3,2},{4,5},{5,4},{6,7},{7,6},{8,9},{9,8},{10,11... | collective-permute-start | bytes 1572872 | tf_op jit(solution)/shard_map/ppermute | solution.py:246
  32.3 11.8 %collective-permute-start.10 = (bf16[256,1024]{1,0:T(8,128)(2,1)S(1)}, bf16[256,1024]{1,0:T(8,128)(2,1)S(1)}, u32[]{:S(2)}, u32[]{:S(2)}) collective-permute-start(bf16[256,1024]{1,0:T(8,128)(2,1)S(1)} %collective-permute-done.6.refs_2_), channel_id=1, source_target_pairs={{0,1},{1,0},{2,3},{3,2},{4,5},{5,4},{6,7},{7,6},{8,9},{9,8},{10,11... | collective-permute-start | bytes 1572872 | tf_op jit(solution)/shard_map/ppermute | solution.py:246
  38.3 5.8 %collective-permute-start.11 = (bf16[256,1024]{1,0:T(8,128)(2,1)S(1)}, bf16[256,1024]{1,0:T(8,128)(2,1)S(1)}, u32[]{:S(2)}, u32[]{:S(2)}) collective-permute-start(bf16[256,1024]{1,0:T(8,128)(2,1)S(1)} %collective-permute-done.7.refs_3_), channel_id=1, source_target_pairs={{0,1},{1,0},{2,3},{3,2},{4,5},{5,4},{6,7},{7,6},{8,9},{9,8},{10,11... | collective-permute-start | bytes 1572872 | tf_op jit(solution)/shard_map/ppermute | solution.py:246
  44.1 16.4 %collective-permute-start.13 = (bf16[512,512]{1,0:T(8,128)(2,1)S(1)}, bf16[512,512]{1,0:T(8,128)(2,1)}, u32[]{:S(2)}, u32[]{:S(2)}) collective-permute-start(bf16[512,512]{1,0:T(8,128)(2,1)S(1)} %constant_dynamic-slice_fusion.refs_8_), channel_id=1, source_target_pairs={{0,4},{4,8},{8,12},{12,0},{1,5},{5,9},{9,13},{13,1},{2,6},{6,10},{... | collective-permute-start | bytes 1572872 | tf_op jit(solution)/shard_map/ppermute | solution.py:215
  53.8 13.0 %collective-permute-start.12 = (f32[2,256,256]{2,1,0:T(8,128)}, f32[2,256,256]{2,1,0:T(8,128)S(1)}, u32[]{:S(2)}, u32[]{:S(2)}) collective-permute-start(f32[2,256,256]{2,1,0:T(8,128)} %get-tuple-element.47), channel_id=1, source_target_pairs={{0,2},{2,0},{1,3},{3,1},{4,6},{6,4},{5,7},{7,5},{8,10},{10,8},{9,1... | collective-permute-start | bytes 1572872 | tf_op jit(solution)/shard_map/ppermute | solution.py:187
  55.4 12.7 %collective-permute-start.14 = (f32[2,256,256]{2,1,0:T(8,128)}, f32[2,256,256]{2,1,0:T(8,128)S(1)}, u32[]{:S(2)}, u32[]{:S(2)}) collective-permute-start(f32[2,256,256]{2,1,0:T(8,128)} %get-tuple-element.50), channel_id=1, source_target_pairs={{0,16},{16,0},{1,17},{17,1},{2,18},{18,2},{3,19},{19,3},{4,20},{20... | collective-permute-start | bytes 1572872 | tf_op jit(solution)/shard_map/ppermute | solution.py:189
  56.9 16.0 %collective-permute-start.3 = (bf16[512,512]{1,0:T(8,128)(2,1)S(1)}, bf16[512,512]{1,0:T(8,128)(2,1)S(1)}, u32[]{:S(2)}, u32[]{:S(2)}) collective-permute-start(bf16[512,512]{1,0:T(8,128)(2,1)S(1)} %constant_dynamic-slice_fusion.refs_8_), channel_id=1, source_target_pairs={{0,12},{4,0},{8,4},{12,8},{1,13},{5,1},{9,5},{13,9},{2,14},{6,2},{... | collective-permute-start | bytes 1572872 | tf_op jit(solution)/shard_map/ppermute | solution.py:217
  60.5 23.4 %collective-permute-start.17 = (bf16[512,512]{1,0:T(8,128)(2,1)}, bf16[512,512]{1,0:T(8,128)(2,1)}, u32[]{:S(2)}, u32[]{:S(2)}) collective-permute-start(bf16[512,512]{1,0:T(8,128)(2,1)} %collective-permute-done.13.refs_9_), channel_id=1, source_target_pairs={{0,4},{4,8},{8,12},{12,0},{1,5},{5,9},{9,13},{13,1},{2,6},{6,10},{... | collective-permute-start | bytes 1572872 | tf_op jit(solution)/shard_map/ppermute | solution.py:215
  70.3 6.4 %collective-permute-start.15 = (f32[256,256]{1,0:T(8,128)S(1)}, f32[256,256]{1,0:T(8,128)S(1)}, u32[]{:S(2)}, u32[]{:S(2)}) collective-permute-start(f32[256,256]{1,0:T(8,128)S(1)} %get-tuple-element.52), channel_id=1, source_target_pairs={{0,16},{16,0},{1,17},{17,1},{2,18},{18,2},{3,19},{19,3},{4,20},{20... | collective-permute-start | bytes 786440 | tf_op jit(solution)/shard_map/ppermute | solution.py:189
  71.8 6.4 %collective-permute-start.16 = (f32[256,256]{1,0:T(8,128)S(1)}, f32[256,256]{1,0:T(8,128)S(1)}, u32[]{:S(2)}, u32[]{:S(2)}) collective-permute-start(f32[256,256]{1,0:T(8,128)S(1)} %get-tuple-element.53), channel_id=1, source_target_pairs={{0,2},{2,0},{1,3},{3,1},{4,6},{6,4},{5,7},{7,5},{8,10},{10,8},{9,1... | collective-permute-start | bytes 786440 | tf_op jit(solution)/shard_map/ppermute | solution.py:187
  80.1 37.0 %all-to-all-start.1 = ((bf16[8,64,512]{2,1,0:T(8,128)(2,1)}), bf16[8,64,512]{2,1,0:T(8,128)(2,1)S(1)}, u32[]{:S(2)}, u32[]{:S(2)}) async-start(bf16[8,64,512]{2,1,0:T(8,128)(2,1)} %bitcast.16), calls=%async_computation.1 | async-start | bytes 1048576 | tf_op jit(solution)/shard_map/all_to_all | solution.py:335
  91.4 12.1 %collective-permute-start.18 = (f32[2,256,256]{2,1,0:T(8,128)}, f32[2,256,256]{2,1,0:T(8,128)S(1)}, u32[]{:S(2)}, u32[]{:S(2)}) collective-permute-start(f32[2,256,256]{2,1,0:T(8,128)} %get-tuple-element.58), channel_id=1, source_target_pairs={{0,2},{2,0},{1,3},{3,1},{4,6},{6,4},{5,7},{7,5},{8,10},{10,8},{9,1... | collective-permute-start | bytes 1572872 | tf_op jit(solution)/shard_map/ppermute | solution.py:187
  93.5 10.0 %collective-permute-start.19 = (f32[2,256,256]{2,1,0:T(8,128)}, f32[2,256,256]{2,1,0:T(8,128)S(1)}, u32[]{:S(2)}, u32[]{:S(2)}) collective-permute-start(f32[2,256,256]{2,1,0:T(8,128)} %get-tuple-element.60), channel_id=1, source_target_pairs={{0,16},{16,0},{1,17},{17,1},{2,18},{18,2},{3,19},{19,3},{4,20},{20... | collective-permute-start | bytes 1572872 | tf_op jit(solution)/shard_map/ppermute | solution.py:189
  106.5 7.7 %collective-permute-start.20 = (f32[256,256]{1,0:T(8,128)}, f32[256,256]{1,0:T(8,128)}, u32[]{:S(2)}, u32[]{:S(2)}) collective-permute-start(f32[256,256]{1,0:T(8,128)} %get-tuple-element.62), channel_id=1, source_target_pairs={{0,16},{16,0},{1,17},{17,1},{2,18},{18,2},{3,19},{19,3},{4,20},{20... | collective-permute-start | bytes 786440 | tf_op jit(solution)/shard_map/ppermute | solution.py:189
  107.0 7.2 %collective-permute-start.21 = (f32[256,256]{1,0:T(8,128)}, f32[256,256]{1,0:T(8,128)}, u32[]{:S(2)}, u32[]{:S(2)}) collective-permute-start(f32[256,256]{1,0:T(8,128)} %get-tuple-element.63), channel_id=1, source_target_pairs={{0,2},{2,0},{1,3},{3,1},{4,6},{6,4},{5,7},{7,5},{8,10},{10,8},{9,1... | collective-permute-start | bytes 786440 | tf_op jit(solution)/shard_map/ppermute | solution.py:187
  117.1 15.3 %all-to-all-start = ((bf16[8,64,512]{2,1,0:T(8,128)(2,1)}), bf16[8,64,512]{2,1,0:T(8,128)(2,1)S(1)}, u32[]{:S(2)}, u32[]{:S(2)}) async-start(bf16[8,64,512]{2,1,0:T(8,128)(2,1)} %bitcast.25), calls=%async_computation | async-start | bytes 1048576 | tf_op jit(solution)/shard_map/all_to_all | solution.py:335
  (32 other events, 217.1 us)

commit v3 on v2

--- a/solution.py
+++ b/solution.py
@@ -12,7 +12,7 @@
 THETA = 1000000.0
 VMEM = pl.BlockSpec(memory_space=pltpu.VMEM)
 SMEM = pl.BlockSpec(memory_space=pltpu.SMEM)
-FULL = pltpu.CompilerParams(vmem_limit_bytes=56 * 1024 * 1024)
+FULL = pltpu.CompilerParams(vmem_limit_bytes=40 * 1024 * 1024)
 ANY = pl.BlockSpec(memory_space=pl.ANY)
 PARAMS = pltpu.CompilerParams(vmem_limit_bytes=16 * 1024 * 1024)
 
@@ -73,37 +73,72 @@
         outs[2 + (k >> 1)][k & 1] = total[:, middle:]
 
 
-def fold_kernel(kept_a, came_a, kept_b, came_b, mine, next_a, next_b):
-    middle = kept_a.shape[2]
-    mine[:, :middle] = kept_a[0] + came_a[0]
-    mine[:, middle:] = kept_b[0] + came_b[0]
-    next_a[...] = kept_a[1] + came_a[1]
-    next_b[...] = kept_b[1] + came_b[1]
-
-
-def rows_kernel(bias, target, mine, came_a, came_b, *refs, earlier):
-    before = refs[:earlier]
-    keyval = refs[earlier]
-    wide = keyval.shape[1]
-    at = bias.shape[1] - wide
-    summed = mine[...] + jnp.concatenate([came_a[...], came_b[...]], 1)
-    rows = (summed + bias[:, at:]).astype(jnp.bfloat16)
-    keyval[...] = rows
-    if len(refs) == earlier + 1:
-        return
-    outgoing = refs[-1]
+def early_kernel(place, *refs, count, piece, order):
+    rows, blocks, outs, later = refs[:8], refs[8:-9], refs[-9:-5], refs[-5]
+    held, weights, row_sems, sems = refs[-4:]
+    z, core = place[2], place[3]
+    copies = [
+        pltpu.make_async_copy(block, weights.at[i], sems.at[i]) for i, block in enumerate(blocks)
+    ]
+    loads = [pltpu.make_async_copy(rows[i], held.at[i], row_sems.at[i]) for i in range(8)]
+    for copy in copies:
+        copy.start()
+    for k in range(4):
+        loads[k].start()
+        loads[4 + k].start()
+    for copy in copies:
+        copy.wait()
+    half = count // 2
+    middle = weights.shape[2] // 2
+
+    def features(k, s):
+        at = lax.rem(z - s + count, count)
+        side = jnp.where(lax.div(at, half) == core, 0, 4)
+        cols = pl.ds(pl.multiple_of(lax.rem(at, half) * piece, piece), piece)
+        return held[side + k, :, cols]
+
+    for k in range(4):
+        loads[k].wait()
+        loads[4 + k].wait()
+        later[k] = features(k, count // 2)
+        total = None
+        for i, s in enumerate(order):
+            part = jnp.dot(features(k, s), weights[i], preferred_element_type=jnp.float32)
+            total = part if total is None else total + part
+        outs[k & 1][k >> 1] = total[:, :middle]
+        outs[2 + (k >> 1)][k & 1] = total[:, middle:]
+
+
+def late_kernel(later, block, *refs):
+    sums, outs = refs[:4], refs[4:]
+    middle = block.shape[1] // 2
+    for k in range(4):
+        total = jnp.dot(later[k], block[...], preferred_element_type=jnp.float32)
+        outs[k & 1][k >> 1] = sums[k & 1][k >> 1] + total[:, :middle]
+        outs[2 + (k >> 1)][k & 1] = sums[2 + (k >> 1)][k & 1] + total[:, middle:]
+
+
+def fold_kernel(kept_a, came_a, kept_b, came_b, next_a, next_b):
+    next_a[...] = kept_a[0] + came_a[0]
+    next_b[...] = kept_b[0] + came_b[0]
+
+
+def rows_kernel(bias, target, *refs):
+    shares, (keyval, outgoing) = refs[:-2], refs[-2:]
+    begin = 0
+    for kept, near, far in zip(shares[::3], shares[1::3], shares[2::3]):
+        cols = slice(begin, begin + far.shape[1])
+        summed = kept[0] + near[0] + far[...] + bias[:, cols]
+        keyval[:, cols] = summed.astype(jnp.bfloat16)
+        begin = cols.stop
+    rows = keyval[...]
     slots, count = outgoing.shape[0], rows.shape[0]
     hits = lax.broadcasted_iota(jnp.int32, (slots, count), 0) == target[...]
     onehot = hits.astype(jnp.float32)
     used = jnp.sum(onehot, 1, keepdims=True)
-    onehot = onehot.astype(jnp.bfloat16)
-    begin = 0
-    for block in [ref[...] for ref in before] + [rows]:
-        cols = slice(begin, begin + block.shape[1])
-        moved = jnp.dot(onehot, block, preferred_element_type=jnp.float32)
-        empty = bias[:, cols].astype(jnp.bfloat16).astype(jnp.float32)
-        outgoing[:, cols] = jnp.where(used > 0, moved, empty).astype(jnp.bfloat16)
-        begin += block.shape[1]
+    moved = jnp.dot(onehot.astype(jnp.bfloat16), rows, preferred_element_type=jnp.float32)
+    empty = bias[...].astype(jnp.bfloat16).astype(jnp.float32)
+    outgoing[...] = jnp.where(used > 0, moved, empty).astype(jnp.bfloat16)
 
 
 def turn(values, cosine, sine):
@@ -190,6 +225,7 @@
         return lax.ppermute(array, ("groups", "fx"), flip_both)
 
     hidden_f = hidden.astype(jnp.float32)
+    ahead = lax.dynamic_slice(kv_weight, (y * piece, 0), (piece, chunks_of(heads)[0][1] * 2 * HD))
     squares = pl.pallas_call(
         squares_kernel,
         out_shape=jax.ShapeDtypeStruct((count, 1), jnp.float32),
@@ -198,7 +234,7 @@
         compiler_params=PARAMS,
         cost_estimate=cost(2 * count * features, 1 << 20),
         name="squares",
-    )(hidden)
+    )(after(hidden, ahead))
 
     chunks = chunks_of(heads)
     gathered = []
@@ -209,7 +245,7 @@
             source, end = kv_weight, squares
         else:
             source, end = after(kv_weight, gathered[-1][-1], *waits), gathered[-1][steps // 2]
-        block = lax.dynamic_slice(source, (y * piece, first * 2 * HD), cut)
+        block = lax.dynamic_slice(source, (y * piece, first * 2 * HD), cut) if gathered else ahead
         ups, downs = [block], [after(block, end)]
         for _ in range(steps // 2):
             ups.append(lax.ppermute(ups[-1], "fz", right))
@@ -272,101 +308,154 @@
     )(queries, cosine, sine)
 
     bias = kv_bias[None, :]
-    attended = None
-    waiting, sent = [], 0
-    scored_rows = None
-    last = (turned, target, start)
-    for n, (first, number) in enumerate(chunks):
-        wide = number * 2 * HD
-        middle = wide // 2
-        where = after(place, *last)
-        kept_a, sent_a, kept_b, sent_b = pl.pallas_call(
-            functools.partial(matmul_kernel, count=steps, piece=piece),
-            out_shape=[jax.ShapeDtypeStruct((2, count, middle), jnp.float32)] * 4,
-            in_specs=[SMEM] + [ANY] * (8 + steps),
-            out_specs=[VMEM] * 4,
+    def begin_sums(blocks, sums, wide):
+        order = [s for s in range(steps) if s != steps // 2]
+        return pl.pallas_call(
+            functools.partial(early_kernel, count=steps, piece=piece, order=order),
+            out_shape=sums + [jax.ShapeDtypeStruct((4, count, piece), jnp.bfloat16)],
+            in_specs=[SMEM] + [ANY] * (7 + steps),
+            out_specs=[VMEM] * 5,
             scratch_shapes=[
                 pltpu.VMEM((8, count, steps * piece // 2), jnp.bfloat16),
-                pltpu.VMEM((steps * piece, wide), jnp.bfloat16),
+                pltpu.VMEM((steps - 1, piece, wide), jnp.bfloat16),
                 pltpu.SemaphoreType.DMA((8,)),
-                pltpu.SemaphoreType.DMA((steps,)),
+                pltpu.SemaphoreType.DMA((steps - 1,)),
             ],
             compiler_params=FULL,
-            cost_estimate=cost(2 * 4 * count * steps * piece * wide, 1 << 20),
-            name="project",
-        )(where, *own, *peer, *gathered[n])
-        came_a, came_b = to_chip(1, sent_a), to_chip(2, sent_b)
-        if n + 1 < len(chunks):
-            came_a = after(came_a, gathered[n + 1][1])
-        mine, next_a, next_b = pl.pallas_call(
+            cost_estimate=cost(2 * 3 * count * steps * piece * wide, 1 << 20),
+            name="early",
+        )(place, *own, *peer, *[blocks[s] for s in order])
+
+    def all_of(*shape):
+        return pl.BlockSpec(shape, lambda i: (0, 0))
+
+    def add_up(n, begun, waits, meanwhile):
+        wide = chunks[n][1] * 2 * HD
+        middle = wide // 2
+        sums = [jax.ShapeDtypeStruct((2, count, middle), jnp.float32)] * 4
+        blocks = gathered[n]
+        flops = 2 * 4 * count * steps * piece * wide
+        if begun is None:
+            parts = pl.pallas_call(
+                functools.partial(matmul_kernel, count=steps, piece=piece),
+                out_shape=sums,
+                in_specs=[SMEM] + [ANY] * (8 + steps),
+                out_specs=[VMEM] * 4,
+                scratch_shapes=[
+                    pltpu.VMEM((8, count, steps * piece // 2), jnp.bfloat16),
+                    pltpu.VMEM((steps * piece, wide), jnp.bfloat16),
+                    pltpu.SemaphoreType.DMA((8,)),
+                    pltpu.SemaphoreType.DMA((steps,)),
+                ],
+                compiler_params=FULL,
+                cost_estimate=cost(flops, 1 << 20),
+                name="project",
+            )(after(place, *waits), *own, *peer, *blocks)
+        else:
+            *parts, later = begun
+            parts = pl.pallas_call(
+                late_kernel,
+                out_shape=[pltpu.HBM(sums[0].shape, jnp.float32), sums[1]] * 2,
+                grid=(1,),
+                in_specs=[VMEM] * 6,
+                out_specs=[pl.BlockSpec((2, count, middle), lambda i: (0, 0, 0)), VMEM] * 2,
+                compiler_params=PARAMS,
+                cost_estimate=cost(flops // 4, 1 << 20),
+                name="late",
+            )(after(later, *waits), blocks[steps // 2], *parts)
+        kept_a, sent_a, kept_b, sent_b = parts
+        near_a, near_b = to_chip(1, sent_a), to_chip(2, sent_b)
+        near_a = after(near_a, *meanwhile)
+        second = pl.BlockSpec((1, count, middle), lambda i: (1, 0, 0))
+        next_a, next_b = pl.pallas_call(
             fold_kernel,
-            out_shape=[jax.ShapeDtypeStruct((count, wide), jnp.float32)]
-            + [jax.ShapeDtypeStruct((count, middle), jnp.float32)] * 2,
-            in_specs=[VMEM] * 4,
-            out_specs=[VMEM] * 3,
+            out_shape=[jax.ShapeDtypeStruct((count, middle), jnp.float32)] * 2,
+            grid=(1,),
+            in_specs=[second] * 4,
+            out_specs=[all_of(count, middle)] * 2,
             compiler_params=PARAMS,
             cost_estimate=cost(2 * count * wide, 1 << 18),
             name="fold",
-        )(kept_a, came_a, kept_b, came_b)
-        share = [mine, to_chip(2, next_a), to_chip(1, next_b)]
-        end = first * 2 * HD + wide
-        added = bias[:, sent:end]
-        if n + 1 < len(chunks):
-            added = after(added, gathered[n + 1][-1])
-        if attended is not None:
-            added, attended = lax.optimization_barrier((added, attended))
-        routed = True
-        earlier = waiting if routed else []
-        outs = [jax.ShapeDtypeStruct((count, wide), jnp.bfloat16)]
-        if routed:
-            outs.append(jax.ShapeDtypeStruct((slots, end - sent), jnp.bfloat16))
-        keyval, *outgoing = pl.pallas_call(
-            functools.partial(rows_kernel, earlier=len(earlier)),
-            out_shape=outs,
-            in_specs=[VMEM] * (5 + len(earlier)),
-            out_specs=[VMEM] * len(outs),
+        )(kept_a, near_a, kept_b, near_b)
+        return [kept_a, near_a, to_chip(2, next_a), kept_b, near_b, to_chip(1, next_b)]
+
+    def rows_of(begin, shares, waits):
+        wide = 2 * sum(share[2].shape[1] for share in shares)
+        first_half = [
+            pl.BlockSpec((1, count, share[2].shape[1]), lambda i: (0, 0, 0)) for share in shares
+        ]
+        specs = [
+            [half, half, all_of(count, share[2].shape[1])] * 2
+            for half, share in zip(first_half, shares)
+        ]
+        keyval, outgoing = pl.pallas_call(
+            rows_kernel,
+            out_shape=[
+                pltpu.HBM((count, wide), jnp.bfloat16),
+                pltpu.HBM((slots, wide), jnp.bfloat16),
+            ],
+            grid=(1,),
+            in_specs=[all_of(1, wide), all_of(1, count)] + sum(specs, []),
+            out_specs=[all_of(count, wide), all_of(slots, wide)],
             compiler_params=PARAMS,
             cost_estimate=cost(2 * slots * count * wide, 1 << 20),
             name="rows",
-        )(added, target[None, :], *share, *earlier)
-        last = (keyval,)
-        waiting.append(keyval)
-        if routed:
-            received = lax.all_to_all(outgoing[0], ("fz", "fx"), split_axis=0, concat_axis=0, tiled=True)
-            columns_at = pl.BlockSpec((slots, end - sent), lambda i, at=sent // (end - sent): (0, at))
-            before = [] if scored_rows is None else [scored_rows]
-            scored_rows = pl.pallas_call(
-                lambda *refs: refs[-1].__setitem__(Ellipsis, refs[0][...]),
-                out_shape=jax.ShapeDtypeStruct((slots, columns), jnp.bfloat16),
-                grid=(1,),
-                in_specs=[pl.BlockSpec((slots, end - sent), lambda i: (0, 0))] + [ANY] * len(before),
-                out_specs=columns_at,
-                input_output_aliases={1: 0} if before else {},
-                compiler_params=PARAMS,
-                cost_estimate=cost(1, 1 << 19),
-                name="store",
-            )(received, *before)
-            waiting, sent = [], end
-        before = [] if attended is None else [attended]
-        attended = pl.pallas_call(
+        )(after(kv_bias[None, begin : begin + wide], *waits), target[None, :], *sum(shares, []))
+        return keyval, outgoing
+
+    def send(begin, outgoing, stored):
+        wide = outgoing.shape[1]
+        received = lax.all_to_all(outgoing, ("fz", "fx"), split_axis=0, concat_axis=0, tiled=True)
+        stored = pl.pallas_call(
+            lambda *refs: refs[-1].__setitem__(Ellipsis, refs[0][...]),
+            out_shape=jax.ShapeDtypeStruct((slots, columns), jnp.bfloat16),
+            grid=(1,),
+            in_specs=[all_of(slots, wide)] + [ANY] * len(stored),
+            out_specs=pl.BlockSpec((slots, wide), lambda i: (0, begin // wide)),
+            input_output_aliases={1: 0} if stored else {},
+            compiler_params=PARAMS,
+            cost_estimate=cost(1, 1 << 19),
+            name="store",
+        )(received, *stored)
+        return stored
+
+    def attend(begin, keyval, before):
+        first, number = begin // (2 * HD), keyval.shape[1] // (2 * HD)
+        return pl.pallas_call(
             functools.partial(attend_kernel, group=group),
             out_shape=jax.ShapeDtypeStruct(queries.shape, jnp.bfloat16),
             grid=(number,),
             in_specs=[
-                pl.BlockSpec((count, group * HD), lambda i, at=first: (0, at + i)),
+                pl.BlockSpec((count, group * HD), lambda i: (0, first + i)),
                 pl.BlockSpec((count, 2 * HD), lambda i: (0, i)),
-                pl.BlockSpec((count, HD), lambda i: (0, 0)),
-                pl.BlockSpec((count, HD), lambda i: (0, 0)),
-                pl.BlockSpec((count, 1), lambda i: (0, 0)),
+                all_of(count, HD),
+                all_of(count, HD),
+                all_of(count, 1),
             ]
             + [ANY] * len(before),
-            out_specs=pl.BlockSpec((count, group * HD), lambda i, at=first: (0, at + i)),
+            out_specs=pl.BlockSpec((count, group * HD), lambda i: (0, first + i)),
             input_output_aliases={5: 0} if before else {},
             compiler_params=PARAMS,
             cost_estimate=cost(4 * number * group * count * count * HD, 1 << 20),
             name="attend",
         )(turned, keyval, cosine, sine, start[:, None], *before)
-    return (attended, scored_rows)
+
+    begun = None
+    if piece % HD == 0:
+        wide = chunks[-1][1] * 2 * HD
+        sums = [jax.ShapeDtypeStruct((2, count, wide // 2), jnp.float32)] * 4
+        begun = begin_sums(gathered[-1], sums, wide)
+    ready = [add_up(0, None, (turned, target, start), (gathered[1][1],))]
+    for n in range(1, len(chunks) - 1):
+        ready.append(add_up(n, None, (ready[-1][0],)))
+    split = chunks[1][0] * 2 * HD
+    keyval, outgoing = rows_of(0, ready[:1], (gathered[1][-1], *([] if begun is None else begun[:1])))
+    attended = attend(0, keyval, [])
+    ready.append(add_up(len(chunks) - 1, begun, (keyval,), (attended,)))
+    stored = send(0, after(outgoing, ready[1][0]), [])
+    keyval, outgoing = rows_of(split, ready[1:], (attended,))
+    stored = send(split, outgoing, [stored])
+    return (attend(split, keyval, [attended]), stored)
 
 
 def solution(mesh):

time: 134 us -> 132 us (0.985)
  waiting for transfers between devices: 51.3 us -> 58.2 us
  local copies, waits for them, and re-layouts: 19.3 us -> 13 us
  Pallas kernels: 30.3 us -> 25.7 us
  starting transfers between devices: 30.1 us -> 32.2 us
    unnamed x64 -> x34, local copies, waits for them, and re-layouts: 18.3 us -> 12.8 us
    pallas_call x10 -> x11, Pallas kernels: 27.6 us -> 23 us  [the longest x2 7.41 us: attend(): pl.pallas_call(functools.partial(attend_kernel, group=group), out_shape=j...]
    ppermute x5, waiting for transfers between devices: 19.8 us -> 16.9 us  [to_chip(): return lax.ppermute(array, 'fx', flip)]
    ppermute x5, waiting for transfers between devices: 8.97 us -> 11.7 us  [to_chip(): return lax.ppermute(array, 'groups', flip)]
    ppermute x5, starting transfers between devices: 5.92 us -> 8.47 us  [to_chip(): return lax.ppermute(array, 'groups', flip)]
    ppermute x2, waiting for transfers between devices: 4.41 us -> 6.33 us  [gather(): downs.append(lax.ppermute(downs[-1], 'fz', left))]
    all_to_all x2, waiting for transfers between devices: 3.21 us -> 5.11 us  [send(): lax.all_to_all(outgoing, ('fz', 'fx'), split_axis=0, concat_axis=0, tiled...]
    ppermute x1, waiting for transfers between devices: 5.96 us -> 7.63 us  [to_chip(): return lax.ppermute(array, ('groups', 'fx'), flip_both)]
  transfers between devices with their start and end apart: 24 -> 24, of which waited for: 13 -> 14; matrix products, arithmetic and copies ran while one was open for 2% -> 1% of each run, Pallas kernels for 22% -> 18%
where the time goes in v3:
time: 132 us; the launch traced here: 131 us
  waiting for transfers between devices  58.2 us (44%)
  starting transfers between devices  32.2 us (24%)
  Pallas kernels  25.7 us (19%)
  local copies, waits for them, and re-layouts  13 us (10%)
    ppermute x5, waiting for transfers between devices, to_chip(): return lax.ppermute(array, 'fx', flip)  16.9 us
    unnamed x34, local copies, waits for them, and re-layouts  12.8 us
    ppermute x5, waiting for transfers between devices, to_chip(): return lax.ppermute(array, 'groups', flip)  11.7 us
    ppermute x4, waiting for transfers between devices, gather(): ups.append(lax.ppermute(ups[-1], 'fz', right))  10.5 us
    ppermute x5, starting transfers between devices, to_chip(): return lax.ppermute(array, 'groups', flip)  8.47 us
    all_to_all x2, starting transfers between devices, send(): lax.all_to_all(outgoing, ('fz', 'fx'), split_axis=0, concat_axis=0, tiled...  8.19 us
    ppermute x1, waiting for transfers between devices, to_chip(): return lax.ppermute(array, ('groups', 'fx'), flip_both)  7.63 us
    pallas_call x2, Pallas kernels, attend(): pl.pallas_call(functools.partial(attend_kernel, group=group), out_shape=j...  7.41 us
  transfers between devices with their start and end apart: 24, of which 14 were waited for; matrix products, arithmetic and copies ran while one was open for 1% of the time, Pallas kernels for 18%

profile of v3, /device:TPU:0, one launch (start us, length us, event | category | flops | bytes accessed | tf_op | source)
XLA Modules:
  0.0 131.2 jit_solution(14630108390975300469)
XLA Ops:
  2.3 3.1 %collective-permute-start.1 = (bf16[512,512]{1,0:T(8,128)(2,1)S(1)}, bf16[512,512]{1,0:T(8,128)(2,1)}, u32[]{:S(2)}, u32[]{:S(2)}) collective-permute-start(bf16[512,512]{1,0:T(8,128)(2,1)S(1)} %constant_dynamic-slice_fusion.1.refs_8_), channel_id=1, source_target_pairs={{0,4},{4,8},{8,12},{12,0},{1,5},{5,9},{9,13},{13,1},{2,6},{6,10},{... | collective-permute-start | bytes 1572872 | tf_op jit(solution)/shard_map/ppermute | solution.py:251
  7.4 2.1 %collective-permute-start = (bf16[512,512]{1,0:T(8,128)(2,1)S(1)}, bf16[512,512]{1,0:T(8,128)(2,1)}, u32[]{:S(2)}, u32[]{:S(2)}) collective-permute-start(bf16[512,512]{1,0:T(8,128)(2,1)S(1)} %constant_dynamic-slice_fusion.1.refs_8_), channel_id=1, source_target_pairs={{0,12},{4,0},{8,4},{12,8},{1,13},{5,1},{9,5},{13,9},{2,14},{6,2},{... | collective-permute-start | bytes 1572872 | tf_op jit(solution)/shard_map/ppermute | solution.py:253
  16.1 4.2 %collective-permute-done.1.refs_9_ = bf16[512,512]{1,0:T(8,128)(2,1)} collective-permute-done((bf16[512,512]{1,0:T(8,128)(2,1)S(1)}, bf16[512,512]{1,0:T(8,128)(2,1)}, u32[]{:S(2)}, u32[]{:S(2)}) %collective-permute-start.1) | collective-permute-done | bytes 524320 | tf_op jit(solution)/shard_map/ppermute | solution.py:251
  20.4 6.2 %collective-permute-done.6.refs_2_ = bf16[256,1024]{1,0:T(8,128)(2,1)S(1)} collective-permute-done((bf16[256,1024]{1,0:T(8,128)(2,1)S(1)}, bf16[256,1024]{1,0:T(8,128)(2,1)S(1)}, u32[]{:S(2)}, u32[]{:S(2)}) %collective-permute-start.6) | collective-permute-done | bytes 524320 | tf_op jit(solution)/shard_map/ppermute | solution.py:224
  26.6 2.5 %collective-permute-done.5.refs_1_ = bf16[256,1024]{1,0:T(8,128)(2,1)S(1)} collective-permute-done((bf16[256,1024]{1,0:T(8,128)(2,1)S(1)}, bf16[256,1024]{1,0:T(8,128)(2,1)S(1)}, u32[]{:S(2)}, u32[]{:S(2)}) %collective-permute-start.5) | collective-permute-done | bytes 524320 | tf_op jit(solution)/shard_map/ppermute | solution.py:222
  29.1 2.3 %collective-permute-done.refs_11_ = bf16[512,512]{1,0:T(8,128)(2,1)} collective-permute-done((bf16[512,512]{1,0:T(8,128)(2,1)S(1)}, bf16[512,512]{1,0:T(8,128)(2,1)}, u32[]{:S(2)}, u32[]{:S(2)}) %collective-permute-start) | collective-permute-done | bytes 524320 | tf_op jit(solution)/shard_map/ppermute | solution.py:253
  31.4 7.6 %collective-permute-done.7.refs_3_ = bf16[256,1024]{1,0:T(8,128)(2,1)S(1)} collective-permute-done((bf16[256,1024]{1,0:T(8,128)(2,1)S(1)}, bf16[256,1024]{1,0:T(8,128)(2,1)S(1)}, u32[]{:S(2)}, u32[]{:S(2)}) %collective-permute-start.7) | collective-permute-done | bytes 524320 | tf_op jit(solution)/shard_map/ppermute | solution.py:225
  39.1 2.7 %collective-permute-done.2.refs_10_ = bf16[512,512]{1,0:T(8,128)(2,1)S(1)} collective-permute-done((bf16[512,512]{1,0:T(8,128)(2,1)}, bf16[512,512]{1,0:T(8,128)(2,1)S(1)}, u32[]{:S(2)}, u32[]{:S(2)}) %collective-permute-start.2) | collective-permute-done | bytes 524320 | tf_op jit(solution)/shard_map/ppermute | solution.py:251
  45.0 4.8 %project.1 = (f32[2,256,256]{2,1,0:T(8,128)S(1)}, f32[2,256,256]{2,1,0:T(8,128)S(1)}, f32[2,256,256]{2,1,0:T(8,128)S(1)}, f32[2,256,256]{2,1,0:T(8,128)S(1)}) custom-call(s32[4]{0:T(128)S(1)} %pad_add_fusion.place, bf16[256,1024]{1,0:T(8,128)(2,1)S(1)} %get-tuple-element.48.refs_0_, bf16[256,1024]{1,0:T(8,128)(2,1)S(1)} %collective-permute-done.5.refs_1_, ...), custom_call_target="tpu_custom_call" | custom-call | flops 2147483648 | bytes 1048576 | tf_op jit(solution)/shard_map/project/pallas_call | solution.py:339
  52.8 3.8 %collective-permute-start.3 = (bf16[512,512]{1,0:T(8,128)(2,1)S(1)}, bf16[512,512]{1,0:T(8,128)(2,1)S(1)}, u32[]{:S(2)}, u32[]{:S(2)}) collective-permute-start(bf16[512,512]{1,0:T(8,128)(2,1)S(1)} %constant_dynamic-slice_fusion.refs_8_), channel_id=1, source_target_pairs={{0,12},{4,0},{8,4},{12,8},{1,13},{5,1},{9,5},{13,9},{2,14},{6,2},{... | collective-permute-start | bytes 1572872 | tf_op jit(solution)/shard_map/ppermute | solution.py:253
  56.8 5.2 %collective-permute-done.13.came_a.refs_1_ = f32[2,256,256]{2,1,0:T(8,128)S(1)} collective-permute-done((f32[2,256,256]{2,1,0:T(8,128)S(1)}, f32[2,256,256]{2,1,0:T(8,128)S(1)}, u32[]{:S(2)}, u32[]{:S(2)}) %collective-permute-start.13) | collective-permute-done | bytes 524320 | tf_op jit(solution)/shard_map/ppermute | solution.py:222
  65.5 4.0 %collective-permute-done.3.refs_10_ = bf16[512,512]{1,0:T(8,128)(2,1)S(1)} collective-permute-done((bf16[512,512]{1,0:T(8,128)(2,1)S(1)}, bf16[512,512]{1,0:T(8,128)(2,1)S(1)}, u32[]{:S(2)}, u32[]{:S(2)}) %collective-permute-start.3) | collective-permute-done | bytes 524320 | tf_op jit(solution)/shard_map/ppermute | solution.py:253
  69.5 3.4 %early.1 = (f32[2,256,256]{2,1,0:T(8,128)S(1)}, f32[2,256,256]{2,1,0:T(8,128)S(1)}, f32[2,256,256]{2,1,0:T(8,128)S(1)}, f32[2,256,256]{2,1,0:T(8,128)S(1)}, bf16[4,256,512]{2,1,0:T(8,128)(2,1)S(1)}) custom-call(s32[4]{0:T(128)S(1)} %pad_add_fusion.place, bf16[256,1024]{1,0:T(8,128)(2,1)S(1)} %get-tuple-element.48.refs_0_, ...), custom_call_target="tpu_custom_call" | custom-call | flops 1610612736 | bytes 1048576 | tf_op jit(solution)/shard_map/early/pallas_call | solution.py:313
  74.1 3.7 %collective-permute-done.17.block = bf16[512,512]{1,0:T(8,128)(2,1)S(1)} collective-permute-done((bf16[512,512]{1,0:T(8,128)(2,1)S(1)}, bf16[512,512]{1,0:T(8,128)(2,1)S(1)}, u32[]{:S(2)}, u32[]{:S(2)}) %collective-permute-start.17) | collective-permute-done | bytes 524320 | tf_op jit(solution)/shard_map/ppermute | solution.py:251
  80.8 3.5 %all-to-all-start.1 = ((bf16[8,64,512]{2,1,0:T(8,128)(2,1)}), bf16[8,64,512]{2,1,0:T(8,128)(2,1)S(1)}, u32[]{:S(2)}, u32[]{:S(2)}) async-start(bf16[8,64,512]{2,1,0:T(8,128)(2,1)} %bitcast.17), calls=%async_computation.1 | async-start | bytes 1048576 | tf_op jit(solution)/shard_map/all_to_all | solution.py:408
  84.3 1.9 %collective-permute-start.18 = (f32[2,256,256]{2,1,0:T(8,128)}, f32[2,256,256]{2,1,0:T(8,128)S(1)}, u32[]{:S(2)}, u32[]{:S(2)}) collective-permute-start(f32[2,256,256]{2,1,0:T(8,128)} %copy-done.13), channel_id=1, source_target_pairs={{0,2},{2,0},{1,3},{3,1},{4,6},{6,4},{5,7},{7,5},{8,10},{10,8},{9,1... | collective-permute-start | bytes 1572872 | tf_op jit(solution)/shard_map/ppermute | solution.py:222
  90.6 3.7 %attend.2.rest_0_ = bf16[256,4096]{1,0:T(8,128)(2,1)} custom-call(bf16[256,4096]{1,0:T(8,128)(2,1)S(1)} %copy-done.2, bf16[256,512]{1,0:T(8,128)(2,1)S(1)} %copy-done.9, f32[256,128]{1,0:T(8,128)S(1)} %get-tuple-element.83.cosine, f32[256,128]{1,0:T(8,128)S(1)} %get-tuple-element.84.sine, s32[256,1]{1,0:T(8,128)S(1)} %copy.15.start), custom_call_target="tpu_custom_call" | custom-call | flops 536870912 | bytes 1048576 | tf_op jit(solution)/shard_map/attend/pallas_call | solution.py:424
  94.3 7.7 %collective-permute-done.18.came_a.refs_1_ = f32[2,256,256]{2,1,0:T(8,128)S(1)} collective-permute-done((f32[2,256,256]{2,1,0:T(8,128)}, f32[2,256,256]{2,1,0:T(8,128)S(1)}, u32[]{:S(2)}, u32[]{:S(2)}) %collective-permute-start.18) | collective-permute-done | bytes 524320 | tf_op jit(solution)/shard_map/ppermute | solution.py:222
  103.1 1.9 %collective-permute-start.20 = (f32[256,256]{1,0:T(8,128)S(1)}, f32[256,256]{1,0:T(8,128)S(1)}, u32[]{:S(2)}, u32[]{:S(2)}) collective-permute-start(f32[256,256]{1,0:T(8,128)S(1)} %get-tuple-element.72), channel_id=1, source_target_pairs={{0,16},{16,0},{1,17},{17,1},{2,18},{18,2},{3,19},{19,3},{4,20},{20... | collective-permute-start | bytes 786440 | tf_op jit(solution)/shard_map/ppermute | solution.py:224
  105.7 4.3 %collective-permute-done.20.refs_2_ = f32[256,256]{1,0:T(8,128)S(1)} collective-permute-done((f32[256,256]{1,0:T(8,128)S(1)}, f32[256,256]{1,0:T(8,128)S(1)}, u32[]{:S(2)}, u32[]{:S(2)}) %collective-permute-start.20) | collective-permute-done | bytes 262176 | tf_op jit(solution)/shard_map/ppermute | solution.py:224
  111.3 2.1 %rows.3 = (bf16[256,512]{1,0:T(8,128)(2,1)}, bf16[512,512]{1,0:T(8,128)(2,1)}) custom-call(f32[1,512]{1,0:T(1,128)S(1)} %bitcast.27, s32[1,256]{1,0:T(1,128)S(1)} %bitcast_add_fusion.target, f32[2,256,256]{2,1,0:T(8,128)S(1)} %copy-done.7, f32[2,256,256]{2,1,0:T(8,128)S(1)} %collective-permute-done.18.came_a.refs_1_, ...), custom_call_target="tpu_custom_call" | custom-call | flops 134217728 | bytes 1048576 | tf_op jit(solution)/shard_map/rows/pallas_call | solution.py:391
  113.5 4.7 %all-to-all-start = ((bf16[8,64,512]{2,1,0:T(8,128)(2,1)}), bf16[8,64,512]{2,1,0:T(8,128)(2,1)S(1)}, u32[]{:S(2)}, u32[]{:S(2)}) async-start(bf16[8,64,512]{2,1,0:T(8,128)(2,1)} %bitcast.29), calls=%async_computation | async-start | bytes 1048576 | tf_op jit(solution)/shard_map/all_to_all | solution.py:408
  120.7 3.7 %attend.3 = bf16[256,4096]{1,0:T(8,128)(2,1)} custom-call(bf16[256,4096]{1,0:T(8,128)(2,1)S(1)} %copy-done.3, bf16[256,512]{1,0:T(8,128)(2,1)S(1)} %copy-done.10, f32[256,128]{1,0:T(8,128)S(1)} %get-tuple-element.83.cosine, f32[256,128]{1,0:T(8,128)S(1)} %get-tuple-element.84.sine, s32[256,1]{1,0:T(8,128)S(1)} %copy.15.start, ...), custom_call_target="tpu_custom_call", output_to_operand_aliasing={{}: (5, {})} | custom-call | flops 536870912 | bytes 1048576 | tf_op jit(solution)/shard_map/attend/pallas_call | solution.py:424
  125.2 5.1 %all-to-all-done = bf16[8,64,512]{2,1,0:T(8,128)(2,1)S(1)} async-done(((bf16[8,64,512]{2,1,0:T(8,128)(2,1)}), bf16[8,64,512]{2,1,0:T(8,128)(2,1)S(1)}, u32[]{:S(2)}, u32[]{:S(2)}) %all-to-all-start) | async-done | bytes 524320 | tf_op jit(solution)/shard_map/all_to_all | solution.py:408
  (87 shorter events, 36.0 us)
Async XLA Ops:
  2.3 18.0 %collective-permute-start.1 = (bf16[512,512]{1,0:T(8,128)(2,1)S(1)}, bf16[512,512]{1,0:T(8,128)(2,1)}, u32[]{:S(2)}, u32[]{:S(2)}) collective-permute-start(bf16[512,512]{1,0:T(8,128)(2,1)S(1)} %constant_dynamic-slice_fusion.1.refs_8_), channel_id=1, source_target_pairs={{0,4},{4,8},{8,12},{12,0},{1,5},{5,9},{9,13},{13,1},{2,6},{6,10},{... | collective-permute-start | bytes 1572872 | tf_op jit(solution)/shard_map/ppermute | solution.py:251
  7.4 2.4 %collective-permute-start.4 = (f32[256,1]{1,0:T(8,128)S(1)}, f32[256,1]{1,0:T(8,128)S(1)}, u32[]{:S(2)}, u32[]{:S(2)}) collective-permute-start(f32[256,1]{1,0:T(8,128)S(1)} %squares.1), channel_id=1, source_target_pairs={{0,1},{1,0},{2,3},{3,2},{4,5},{5,4},{6,7},{7,6},{8,9},{9,8},{10,11... | collective-permute-start | bytes 3080 | tf_op jit(solution)/shard_map/ppermute | solution.py:259
  7.4 24.0 %collective-permute-start = (bf16[512,512]{1,0:T(8,128)(2,1)S(1)}, bf16[512,512]{1,0:T(8,128)(2,1)}, u32[]{:S(2)}, u32[]{:S(2)}) collective-permute-start(bf16[512,512]{1,0:T(8,128)(2,1)S(1)} %constant_dynamic-slice_fusion.1.refs_8_), channel_id=1, source_target_pairs={{0,12},{4,0},{8,4},{12,8},{1,13},{5,1},{9,5},{13,9},{2,14},{6,2},{... | collective-permute-start | bytes 1572872 | tf_op jit(solution)/shard_map/ppermute | solution.py:253
  12.5 14.1 %collective-permute-start.6 = (bf16[256,1024]{1,0:T(8,128)(2,1)S(1)}, bf16[256,1024]{1,0:T(8,128)(2,1)S(1)}, u32[]{:S(2)}, u32[]{:S(2)}) collective-permute-start(bf16[256,1024]{1,0:T(8,128)(2,1)S(1)} %get-tuple-element.46), channel_id=1, source_target_pairs={{0,16},{16,0},{1,17},{17,1},{2,18},{18,2},{3,19},{19,3},{4,20},{20... | collective-permute-start | bytes 1572872 | tf_op jit(solution)/shard_map/ppermute | solution.py:224
  14.3 14.8 %collective-permute-start.5 = (bf16[256,1024]{1,0:T(8,128)(2,1)S(1)}, bf16[256,1024]{1,0:T(8,128)(2,1)S(1)}, u32[]{:S(2)}, u32[]{:S(2)}) collective-permute-start(bf16[256,1024]{1,0:T(8,128)(2,1)S(1)} %get-tuple-element.45), channel_id=1, source_target_pairs={{0,2},{2,0},{1,3},{3,1},{4,6},{6,4},{5,7},{7,5},{8,10},{10,8},{9,1... | collective-permute-start | bytes 1572872 | tf_op jit(solution)/shard_map/ppermute | solution.py:222
  15.8 23.3 %collective-permute-start.7 = (bf16[256,1024]{1,0:T(8,128)(2,1)S(1)}, bf16[256,1024]{1,0:T(8,128)(2,1)S(1)}, u32[]{:S(2)}, u32[]{:S(2)}) collective-permute-start(bf16[256,1024]{1,0:T(8,128)(2,1)S(1)} %get-tuple-element.47), channel_id=1, source_target_pairs={{0,18},{2,16},{16,2},{18,0},{1,19},{3,17},{17,3},{19,1},{4,22},{6,... | collective-permute-start | bytes 1572872 | tf_op jit(solution)/shard_map/ppermute | solution.py:225
  20.3 21.5 %collective-permute-start.2 = (bf16[512,512]{1,0:T(8,128)(2,1)}, bf16[512,512]{1,0:T(8,128)(2,1)S(1)}, u32[]{:S(2)}, u32[]{:S(2)}) collective-permute-start(bf16[512,512]{1,0:T(8,128)(2,1)} %collective-permute-done.1.refs_9_), channel_id=1, source_target_pairs={{0,4},{4,8},{8,12},{12,0},{1,5},{5,9},{9,13},{13,1},{2,6},{6,10},{... | collective-permute-start | bytes 1572872 | tf_op jit(solution)/shard_map/ppermute | solution.py:251
  26.6 18.4 %collective-permute-start.8 = (bf16[256,1024]{1,0:T(8,128)(2,1)S(1)}, bf16[256,1024]{1,0:T(8,128)(2,1)S(1)}, u32[]{:S(2)}, u32[]{:S(2)}) collective-permute-start(bf16[256,1024]{1,0:T(8,128)(2,1)S(1)} %get-tuple-element.48.refs_0_), channel_id=1, source_target_pairs={{0,1},{1,0},{2,3},{3,2},{4,5},{5,4},{6,7},{7,6},{8,9},{9,8},{10,11... | collective-permute-start | bytes 1572872 | tf_op jit(solution)/shard_map/ppermute | solution.py:282
  29.1 15.9 %collective-permute-start.9 = (bf16[256,1024]{1,0:T(8,128)(2,1)S(1)}, bf16[256,1024]{1,0:T(8,128)(2,1)S(1)}, u32[]{:S(2)}, u32[]{:S(2)}) collective-permute-start(bf16[256,1024]{1,0:T(8,128)(2,1)S(1)} %collective-permute-done.5.refs_1_), channel_id=1, source_target_pairs={{0,1},{1,0},{2,3},{3,2},{4,5},{5,4},{6,7},{7,6},{8,9},{9,8},{10,11... | collective-permute-start | bytes 1572872 | tf_op jit(solution)/shard_map/ppermute | solution.py:282
  31.4 13.6 %collective-permute-start.10 = (bf16[256,1024]{1,0:T(8,128)(2,1)S(1)}, bf16[256,1024]{1,0:T(8,128)(2,1)S(1)}, u32[]{:S(2)}, u32[]{:S(2)}) collective-permute-start(bf16[256,1024]{1,0:T(8,128)(2,1)S(1)} %collective-permute-done.6.refs_2_), channel_id=1, source_target_pairs={{0,1},{1,0},{2,3},{3,2},{4,5},{5,4},{6,7},{7,6},{8,9},{9,8},{10,11... | collective-permute-start | bytes 1572872 | tf_op jit(solution)/shard_map/ppermute | solution.py:282
  39.1 5.9 %collective-permute-start.11 = (bf16[256,1024]{1,0:T(8,128)(2,1)S(1)}, bf16[256,1024]{1,0:T(8,128)(2,1)S(1)}, u32[]{:S(2)}, u32[]{:S(2)}) collective-permute-start(bf16[256,1024]{1,0:T(8,128)(2,1)S(1)} %collective-permute-done.7.refs_3_), channel_id=1, source_target_pairs={{0,1},{1,0},{2,3},{3,2},{4,5},{5,4},{6,7},{7,6},{8,9},{9,8},{10,11... | collective-permute-start | bytes 1572872 | tf_op jit(solution)/shard_map/ppermute | solution.py:282
  41.8 14.9 %collective-permute-start.12 = (bf16[512,512]{1,0:T(8,128)(2,1)S(1)}, bf16[512,512]{1,0:T(8,128)(2,1)S(1)}, u32[]{:S(2)}, u32[]{:S(2)}) collective-permute-start(bf16[512,512]{1,0:T(8,128)(2,1)S(1)} %constant_dynamic-slice_fusion.refs_8_), channel_id=1, source_target_pairs={{0,4},{4,8},{8,12},{12,0},{1,5},{5,9},{9,13},{13,1},{2,6},{6,10},{... | collective-permute-start | bytes 1572872 | tf_op jit(solution)/shard_map/ppermute | solution.py:251
  49.8 12.3 %collective-permute-start.13 = (f32[2,256,256]{2,1,0:T(8,128)S(1)}, f32[2,256,256]{2,1,0:T(8,128)S(1)}, u32[]{:S(2)}, u32[]{:S(2)}) collective-permute-start(f32[2,256,256]{2,1,0:T(8,128)S(1)} %get-tuple-element.54), channel_id=1, source_target_pairs={{0,2},{2,0},{1,3},{3,1},{4,6},{6,4},{5,7},{7,5},{8,10},{10,8},{9,1... | collective-permute-start | bytes 1572872 | tf_op jit(solution)/shard_map/ppermute | solution.py:222
  51.3 12.0 %collective-permute-start.14 = (f32[2,256,256]{2,1,0:T(8,128)S(1)}, f32[2,256,256]{2,1,0:T(8,128)S(1)}, u32[]{:S(2)}, u32[]{:S(2)}) collective-permute-start(f32[2,256,256]{2,1,0:T(8,128)S(1)} %get-tuple-element.57), channel_id=1, source_target_pairs={{0,16},{16,0},{1,17},{17,1},{2,18},{18,2},{3,19},{19,3},{4,20},{20... | collective-permute-start | bytes 1572872 | tf_op jit(solution)/shard_map/ppermute | solution.py:224
  52.8 16.7 %collective-permute-start.3 = (bf16[512,512]{1,0:T(8,128)(2,1)S(1)}, bf16[512,512]{1,0:T(8,128)(2,1)S(1)}, u32[]{:S(2)}, u32[]{:S(2)}) collective-permute-start(bf16[512,512]{1,0:T(8,128)(2,1)S(1)} %constant_dynamic-slice_fusion.refs_8_), channel_id=1, source_target_pairs={{0,12},{4,0},{8,4},{12,8},{1,13},{5,1},{9,5},{13,9},{2,14},{6,2},{... | collective-permute-start | bytes 1572872 | tf_op jit(solution)/shard_map/ppermute | solution.py:253
  56.7 21.1 %collective-permute-start.17 = (bf16[512,512]{1,0:T(8,128)(2,1)S(1)}, bf16[512,512]{1,0:T(8,128)(2,1)S(1)}, u32[]{:S(2)}, u32[]{:S(2)}) collective-permute-start(bf16[512,512]{1,0:T(8,128)(2,1)S(1)} %collective-permute-done.12.refs_9_), channel_id=1, source_target_pairs={{0,4},{4,8},{8,12},{12,0},{1,5},{5,9},{9,13},{13,1},{2,6},{6,10},{... | collective-permute-start | bytes 1572872 | tf_op jit(solution)/shard_map/ppermute | solution.py:251
  63.3 9.6 %collective-permute-start.15 = (f32[256,256]{1,0:T(8,128)S(1)}, f32[256,256]{1,0:T(8,128)S(1)}, u32[]{:S(2)}, u32[]{:S(2)}) collective-permute-start(f32[256,256]{1,0:T(8,128)S(1)} %get-tuple-element.58), channel_id=1, source_target_pairs={{0,16},{16,0},{1,17},{17,1},{2,18},{18,2},{3,19},{19,3},{4,20},{20... | collective-permute-start | bytes 786440 | tf_op jit(solution)/shard_map/ppermute | solution.py:224
  64.9 8.0 %collective-permute-start.16 = (f32[256,256]{1,0:T(8,128)S(1)}, f32[256,256]{1,0:T(8,128)S(1)}, u32[]{:S(2)}, u32[]{:S(2)}) collective-permute-start(f32[256,256]{1,0:T(8,128)S(1)} %get-tuple-element.59), channel_id=1, source_target_pairs={{0,2},{2,0},{1,3},{3,1},{4,6},{6,4},{5,7},{7,5},{8,10},{10,8},{9,1... | collective-permute-start | bytes 786440 | tf_op jit(solution)/shard_map/ppermute | solution.py:222
  80.8 32.6 %all-to-all-start.1 = ((bf16[8,64,512]{2,1,0:T(8,128)(2,1)}), bf16[8,64,512]{2,1,0:T(8,128)(2,1)S(1)}, u32[]{:S(2)}, u32[]{:S(2)}) async-start(bf16[8,64,512]{2,1,0:T(8,128)(2,1)} %bitcast.17), calls=%async_computation.1 | async-start | bytes 1048576 | tf_op jit(solution)/shard_map/all_to_all | solution.py:408
  84.3 17.7 %collective-permute-start.18 = (f32[2,256,256]{2,1,0:T(8,128)}, f32[2,256,256]{2,1,0:T(8,128)S(1)}, u32[]{:S(2)}, u32[]{:S(2)}) collective-permute-start(f32[2,256,256]{2,1,0:T(8,128)} %copy-done.13), channel_id=1, source_target_pairs={{0,2},{2,0},{1,3},{3,1},{4,6},{6,4},{5,7},{7,5},{8,10},{10,8},{9,1... | collective-permute-start | bytes 1572872 | tf_op jit(solution)/shard_map/ppermute | solution.py:222
  86.2 15.8 %collective-permute-start.19 = (f32[2,256,256]{2,1,0:T(8,128)}, f32[2,256,256]{2,1,0:T(8,128)}, u32[]{:S(2)}, u32[]{:S(2)}) collective-permute-start(f32[2,256,256]{2,1,0:T(8,128)} %copy-done.12), channel_id=1, source_target_pairs={{0,16},{16,0},{1,17},{17,1},{2,18},{18,2},{3,19},{19,3},{4,20},{20... | collective-permute-start | bytes 1572872 | tf_op jit(solution)/shard_map/ppermute | solution.py:224
  103.1 6.9 %collective-permute-start.20 = (f32[256,256]{1,0:T(8,128)S(1)}, f32[256,256]{1,0:T(8,128)S(1)}, u32[]{:S(2)}, u32[]{:S(2)}) collective-permute-start(f32[256,256]{1,0:T(8,128)S(1)} %get-tuple-element.72), channel_id=1, source_target_pairs={{0,16},{16,0},{1,17},{17,1},{2,18},{18,2},{3,19},{19,3},{4,20},{20... | collective-permute-start | bytes 786440 | tf_op jit(solution)/shard_map/ppermute | solution.py:224
  105.0 6.4 %collective-permute-start.21 = (f32[256,256]{1,0:T(8,128)S(1)}, f32[256,256]{1,0:T(8,128)S(1)}, u32[]{:S(2)}, u32[]{:S(2)}) collective-permute-start(f32[256,256]{1,0:T(8,128)S(1)} %get-tuple-element.73), channel_id=1, source_target_pairs={{0,2},{2,0},{1,3},{3,1},{4,6},{6,4},{5,7},{7,5},{8,10},{10,8},{9,1... | collective-permute-start | bytes 786440 | tf_op jit(solution)/shard_map/ppermute | solution.py:222
  113.5 16.9 %all-to-all-start = ((bf16[8,64,512]{2,1,0:T(8,128)(2,1)}), bf16[8,64,512]{2,1,0:T(8,128)(2,1)S(1)}, u32[]{:S(2)}, u32[]{:S(2)}) async-start(bf16[8,64,512]{2,1,0:T(8,128)(2,1)} %bitcast.29), calls=%async_computation | async-start | bytes 1048576 | tf_op jit(solution)/shard_map/all_to_all | solution.py:408
  (17 other events, 108.3 us)

commit v4 on v3

--- a/solution.py
+++ b/solution.py
@@ -191,7 +191,7 @@
 
 
 def chunks_of(heads):
-    sizes = [heads // 2, heads - heads // 2]
+    sizes = [heads // 2] + [1] * (heads - heads // 2)
     return [(sum(sizes[:i]), size) for i, size in enumerate(sizes) if size]
 
 
@@ -239,22 +239,22 @@
     chunks = chunks_of(heads)
     gathered = []
 
-    def gather(first, number, *waits):
+    def gather(first, number, relay=()):
         cut = (piece, number * 2 * HD)
         if not gathered:
             source, end = kv_weight, squares
         else:
-            source, end = after(kv_weight, gathered[-1][-1], *waits), gathered[-1][steps // 2]
+            source, end = after(kv_weight, gathered[-1][-1]), gathered[-1][steps // 2]
         block = lax.dynamic_slice(source, (y * piece, first * 2 * HD), cut) if gathered else ahead
         ups, downs = [block], [after(block, end)]
-        for _ in range(steps // 2):
-            ups.append(lax.ppermute(ups[-1], "fz", right))
+        for i in range(steps // 2):
+            held = after(ups[-1], *relay) if relay and i == 1 else ups[-1]
+            ups.append(lax.ppermute(held, "fz", right))
         for _ in range((steps - 1) // 2):
             downs.append(lax.ppermute(downs[-1], "fz", left))
         gathered.append(ups + downs[:0:-1])
 
-    for chunk in chunks:
-        gather(*chunk)
+    gather(*chunks[0])
 
     squares = squares + lax.ppermute(squares, "tp", flip)
     inverse_rms = lax.rsqrt(squares / width + EPSILON)
@@ -329,7 +329,7 @@
     def all_of(*shape):
         return pl.BlockSpec(shape, lambda i: (0, 0))
 
-    def add_up(n, begun, waits, meanwhile):
+    def add_up(n, begun, waits):
         wide = chunks[n][1] * 2 * HD
         middle = wide // 2
         sums = [jax.ShapeDtypeStruct((2, count, middle), jnp.float32)] * 4
@@ -338,9 +338,10 @@
         if begun is None:
             parts = pl.pallas_call(
                 functools.partial(matmul_kernel, count=steps, piece=piece),
-                out_shape=sums,
+                out_shape=[pltpu.HBM(each.shape, each.dtype) for each in sums] if n else sums,
+                grid=(1,),
                 in_specs=[SMEM] + [ANY] * (8 + steps),
-                out_specs=[VMEM] * 4,
+                out_specs=[pl.BlockSpec((2, count, middle), lambda i: (0, 0, 0)) if n else VMEM] * 4,
                 scratch_shapes=[
                     pltpu.VMEM((8, count, steps * piece // 2), jnp.bfloat16),
                     pltpu.VMEM((steps * piece, wide), jnp.bfloat16),
@@ -355,17 +356,22 @@
             *parts, later = begun
             parts = pl.pallas_call(
                 late_kernel,
-                out_shape=[pltpu.HBM(sums[0].shape, jnp.float32), sums[1]] * 2,
+                out_shape=[pltpu.HBM(each.shape, each.dtype) for each in sums],
                 grid=(1,),
                 in_specs=[VMEM] * 6,
-                out_specs=[pl.BlockSpec((2, count, middle), lambda i: (0, 0, 0)), VMEM] * 2,
+                out_specs=[pl.BlockSpec((2, count, middle), lambda i: (0, 0, 0))] * 4,
                 compiler_params=PARAMS,
                 cost_estimate=cost(flops // 4, 1 << 20),
                 name="late",
             )(after(later, *waits), blocks[steps // 2], *parts)
+        return parts
+
+    def exchange(n, parts, waits):
+        middle = chunks[n][1] * HD
+        wide = 2 * middle
         kept_a, sent_a, kept_b, sent_b = parts
         near_a, near_b = to_chip(1, sent_a), to_chip(2, sent_b)
-        near_a = after(near_a, *meanwhile)
+        near_a = after(near_a, *waits)
         second = pl.BlockSpec((1, count, middle), lambda i: (1, 0, 0))
         next_a, next_b = pl.pallas_call(
             fold_kernel,
@@ -377,7 +383,7 @@
             cost_estimate=cost(2 * count * wide, 1 << 18),
             name="fold",
         )(kept_a, near_a, kept_b, near_b)
-        return [kept_a, near_a, to_chip(2, next_a), kept_b, near_b, to_chip(1, next_b)]
+        return next_a, [kept_a, near_a, to_chip(2, next_a), kept_b, near_b, to_chip(1, next_b)]
 
     def rows_of(begin, shares, waits):
         wide = 2 * sum(share[2].shape[1] for share in shares)
@@ -440,20 +446,24 @@
             name="attend",
         )(turned, keyval, cosine, sine, start[:, None], *before)
 
+    parts_0 = add_up(0, None, (turned, target, start))
+    gather(*chunks[1], relay=(parts_0[0],))
+    gather(*chunks[2])
     begun = None
     if piece % HD == 0:
         wide = chunks[-1][1] * 2 * HD
         sums = [jax.ShapeDtypeStruct((2, count, wide // 2), jnp.float32)] * 4
         begun = begin_sums(gathered[-1], sums, wide)
-    ready = [add_up(0, None, (turned, target, start), (gathered[1][1],))]
-    for n in range(1, len(chunks) - 1):
-        ready.append(add_up(n, None, (ready[-1][0],)))
+    parts_1 = add_up(1, None, (parts_0[0],))
+    _, share_0 = exchange(0, parts_0, (parts_1[0], gathered[1][-1]))
+    folded, share_1 = exchange(1, parts_1, (gathered[2][-1], *([] if begun is None else begun[:1])))
     split = chunks[1][0] * 2 * HD
-    keyval, outgoing = rows_of(0, ready[:1], (gathered[1][-1], *([] if begun is None else begun[:1])))
+    keyval, outgoing = rows_of(0, [share_0], (*([] if begun is None else begun[:1]),))
     attended = attend(0, keyval, [])
-    ready.append(add_up(len(chunks) - 1, begun, (keyval,), (attended,)))
-    stored = send(0, after(outgoing, ready[1][0]), [])
-    keyval, outgoing = rows_of(split, ready[1:], (attended,))
+    parts_2 = add_up(2, begun, (keyval, folded))
+    _, share_2 = exchange(2, parts_2, (attended,))
+    stored = send(0, after(outgoing, parts_2[0]), [])
+    keyval, outgoing = rows_of(split, [share_1, share_2], (attended,))
     stored = send(split, outgoing, [stored])
     return (attend(split, keyval, [attended]), stored)
 

time: 132 us -> 128 us (0.970)
  waiting for transfers between devices: 58.2 us -> 45.6 us
  starting transfers between devices: 32.2 us -> 38.1 us
  Pallas kernels: 25.7 us -> 30.3 us
  local copies, waits for them, and re-layouts: 13 us -> 11.5 us
    ppermute x5 -> x7, waiting for transfers between devices: 16.9 us -> 7.49 us  [to_chip(): return lax.ppermute(array, 'fx', flip)]
    pallas_call x1 -> x2, Pallas kernels: 4.75 us -> 9.34 us  [add_up(): pl.pallas_call(functools.partial(matmul_kernel, count=steps, piece=piece)...]
    ppermute x2 -> x3, waiting for transfers between devices: 6.33 us -> 2.62 us  [gather(): downs.append(lax.ppermute(downs[-1], 'fz', left))]
    ppermute x4 -> x6, starting transfers between devices: 3.08 us -> 5.51 us  [gather(): ups.append(lax.ppermute(held, 'fz', right))]
    ppermute x5 -> x7, starting transfers between devices: 6.25 us -> 8.62 us  [to_chip(): return lax.ppermute(array, 'fx', flip)]
    all_to_all x2, waiting for transfers between devices: 5.11 us -> 3.4 us  [send(): lax.all_to_all(outgoing, ('fz', 'fx'), split_axis=0, concat_axis=0, tiled...]
    unnamed x34 -> x46, local copies, waits for them, and re-layouts: 12.8 us -> 11.2 us
    ppermute x5 -> x7, waiting for transfers between devices: 11.7 us -> 13.1 us  [to_chip(): return lax.ppermute(array, 'groups', flip)]
  transfers between devices with their start and end apart: 24 -> 31, of which waited for: 14 -> 14; matrix products, arithmetic and copies ran while one was open for 1% -> 1% of each run, Pallas kernels for 18% -> 22%
where the time goes in v4:
time: 128 us
  waiting for transfers between devices  45.6 us (36%)
  starting transfers between devices  38.1 us (30%)
  Pallas kernels  30.3 us (24%)
  local copies, waits for them, and re-layouts  11.5 us (9%)
    ppermute x7, waiting for transfers between devices, to_chip(): return lax.ppermute(array, 'groups', flip)  13.1 us
    ppermute x6, waiting for transfers between devices, gather(): ups.append(lax.ppermute(held, 'fz', right))  11.4 us
    unnamed x46, local copies, waits for them, and re-layouts  11.2 us
    pallas_call x2, Pallas kernels, add_up(): pl.pallas_call(functools.partial(matmul_kernel, count=steps, piece=piece)...  9.34 us
    ppermute x7, starting transfers between devices, to_chip(): return lax.ppermute(array, 'groups', flip)  9.29 us
    ppermute x7, starting transfers between devices, to_chip(): return lax.ppermute(array, 'fx', flip)  8.62 us
    all_to_all x2, starting transfers between devices, send(): lax.all_to_all(outgoing, ('fz', 'fx'), split_axis=0, concat_axis=0, tiled...  8.19 us
    ppermute x1, waiting for transfers between devices, to_chip(): return lax.ppermute(array, ('groups', 'fx'), flip_both)  7.63 us
  transfers between devices with their start and end apart: 31, of which 14 were waited for; matrix products, arithmetic and copies ran while one was open for 1% of the time, Pallas kernels for 22%

profile of v4, /device:TPU:0, one launch (start us, length us, event | category | flops | bytes accessed | tf_op | source)
XLA Modules:
  0.0 127.6 jit_solution(3795259745338117645)
XLA Ops:
  2.3 3.1 %collective-permute-start.5 = (bf16[512,512]{1,0:T(8,128)(2,1)S(1)}, bf16[512,512]{1,0:T(8,128)(2,1)S(1)}, u32[]{:S(2)}, u32[]{:S(2)}) collective-permute-start(bf16[512,512]{1,0:T(8,128)(2,1)S(1)} %constant_dynamic-slice_fusion.2.refs_8_), channel_id=1, source_target_pairs={{0,4},{4,8},{8,12},{12,0},{1,5},{5,9},{9,13},{13,1},{2,6},{6,10},{... | collective-permute-start | bytes 1572872 | tf_op jit(solution)/shard_map/ppermute | solution.py:252
  7.4 2.1 %collective-permute-start.9 = (bf16[512,512]{1,0:T(8,128)(2,1)S(1)}, bf16[512,512]{1,0:T(8,128)(2,1)}, u32[]{:S(2)}, u32[]{:S(2)}) collective-permute-start(bf16[512,512]{1,0:T(8,128)(2,1)S(1)} %constant_dynamic-slice_fusion.2.refs_8_), channel_id=1, source_target_pairs={{0,12},{4,0},{8,4},{12,8},{1,13},{5,1},{9,5},{13,9},{2,14},{6,2},{... | collective-permute-start | bytes 1572872 | tf_op jit(solution)/shard_map/ppermute | solution.py:254
  12.5 1.8 %collective-permute-start.2 = (bf16[256,1024]{1,0:T(8,128)(2,1)S(1)}, bf16[256,1024]{1,0:T(8,128)(2,1)S(1)}, u32[]{:S(2)}, u32[]{:S(2)}) collective-permute-start(bf16[256,1024]{1,0:T(8,128)(2,1)S(1)} %get-tuple-element.54), channel_id=1, source_target_pairs={{0,16},{16,0},{1,17},{17,1},{2,18},{18,2},{3,19},{19,3},{4,20},{20... | collective-permute-start | bytes 1572872 | tf_op jit(solution)/shard_map/ppermute | solution.py:224
  16.2 4.0 %collective-permute-done.5.refs_9_ = bf16[512,512]{1,0:T(8,128)(2,1)S(1)} collective-permute-done((bf16[512,512]{1,0:T(8,128)(2,1)S(1)}, bf16[512,512]{1,0:T(8,128)(2,1)S(1)}, u32[]{:S(2)}, u32[]{:S(2)}) %collective-permute-start.5) | collective-permute-done | bytes 524320 | tf_op jit(solution)/shard_map/ppermute | solution.py:252
  20.2 6.4 %collective-permute-done.2.refs_2_ = bf16[256,1024]{1,0:T(8,128)(2,1)S(1)} collective-permute-done((bf16[256,1024]{1,0:T(8,128)(2,1)S(1)}, bf16[256,1024]{1,0:T(8,128)(2,1)S(1)}, u32[]{:S(2)}, u32[]{:S(2)}) %collective-permute-start.2) | collective-permute-done | bytes 524320 | tf_op jit(solution)/shard_map/ppermute | solution.py:224
  26.6 2.5 %collective-permute-done.1.refs_1_ = bf16[256,1024]{1,0:T(8,128)(2,1)S(1)} collective-permute-done((bf16[256,1024]{1,0:T(8,128)(2,1)S(1)}, bf16[256,1024]{1,0:T(8,128)(2,1)S(1)}, u32[]{:S(2)}, u32[]{:S(2)}) %collective-permute-start.1) | collective-permute-done | bytes 524320 | tf_op jit(solution)/shard_map/ppermute | solution.py:222
  29.1 2.3 %collective-permute-done.9.refs_11_ = bf16[512,512]{1,0:T(8,128)(2,1)} collective-permute-done((bf16[512,512]{1,0:T(8,128)(2,1)S(1)}, bf16[512,512]{1,0:T(8,128)(2,1)}, u32[]{:S(2)}, u32[]{:S(2)}) %collective-permute-start.9) | collective-permute-done | bytes 524320 | tf_op jit(solution)/shard_map/ppermute | solution.py:254
  31.4 7.6 %collective-permute-done.3.refs_3_ = bf16[256,1024]{1,0:T(8,128)(2,1)S(1)} collective-permute-done((bf16[256,1024]{1,0:T(8,128)(2,1)S(1)}, bf16[256,1024]{1,0:T(8,128)(2,1)S(1)}, u32[]{:S(2)}, u32[]{:S(2)}) %collective-permute-start.3) | collective-permute-done | bytes 524320 | tf_op jit(solution)/shard_map/ppermute | solution.py:225
  39.7 2.1 %collective-permute-done.10.refs_10_ = bf16[512,512]{1,0:T(8,128)(2,1)S(1)} collective-permute-done((bf16[512,512]{1,0:T(8,128)(2,1)S(1)}, bf16[512,512]{1,0:T(8,128)(2,1)S(1)}, u32[]{:S(2)}, u32[]{:S(2)}) %collective-permute-start.10) | collective-permute-done | bytes 524320 | tf_op jit(solution)/shard_map/ppermute | solution.py:252
  44.4 3.8 %collective-permute-start.11 = (bf16[512,256]{1,0:T(8,128)(2,1)S(1)}, bf16[512,256]{1,0:T(8,128)(2,1)S(1)}, u32[]{:S(2)}, u32[]{:S(2)}) collective-permute-start(bf16[512,256]{1,0:T(8,128)(2,1)S(1)} %constant_dynamic-slice_fusion.1.refs_8_), channel_id=1, source_target_pairs={{0,12},{4,0},{8,4},{12,8},{1,13},{5,1},{9,5},{13,9},{2,14},{6,2},{... | collective-permute-start | bytes 786440 | tf_op jit(solution)/shard_map/ppermute | solution.py:254
  48.3 4.7 %project.2 = (f32[2,256,256]{2,1,0:T(8,128)S(1)}, f32[2,256,256]{2,1,0:T(8,128)S(1)}, f32[2,256,256]{2,1,0:T(8,128)S(1)}, f32[2,256,256]{2,1,0:T(8,128)S(1)}) custom-call(s32[4]{0:T(128)S(1)} %pad_add_fusion.place, bf16[256,1024]{1,0:T(8,128)(2,1)S(1)} %get-tuple-element.56.refs_0_, bf16[256,1024]{1,0:T(8,128)(2,1)S(1)} %collective-permute-done.1.refs_1_, ...), custom_call_target="tpu_custom_call" | custom-call | flops 2147483648 | bytes 1048576 | tf_op jit(solution)/shard_map/project/pallas_call | solution.py:339
  57.1 5.2 %collective-permute-done.14.refs_10_ = bf16[512,256]{1,0:T(8,128)(2,1)S(1)} collective-permute-done((bf16[512,256]{1,0:T(8,128)(2,1)S(1)}, bf16[512,256]{1,0:T(8,128)(2,1)S(1)}, u32[]{:S(2)}, u32[]{:S(2)}) %collective-permute-start.14) | collective-permute-done | bytes 262176 | tf_op jit(solution)/shard_map/ppermute | solution.py:252
  62.8 4.7 %project.3 = (f32[2,256,128]{2,1,0:T(8,128)}, f32[2,256,128]{2,1,0:T(8,128)}, f32[2,256,128]{2,1,0:T(8,128)}, f32[2,256,128]{2,1,0:T(8,128)}) custom-call(s32[4]{0:T(128)S(1)} %pad_add_fusion.place, bf16[256,1024]{1,0:T(8,128)(2,1)S(1)} %get-tuple-element.56.refs_0_, bf16[256,1024]{1,0:T(8,128)(2,1)S(1)} %collective-permute-done.1.refs_1_, ...), custom_call_target="tpu_custom_call" | custom-call | flops 1073741824 | bytes 1048576 | tf_op jit(solution)/shard_map/project/pallas_call | solution.py:339
  73.0 1.9 %collective-permute-start.19 = (f32[256,256]{1,0:T(8,128)S(1)}, f32[256,256]{1,0:T(8,128)S(1)}, u32[]{:S(2)}, u32[]{:S(2)}) collective-permute-start(f32[256,256]{1,0:T(8,128)S(1)} %get-tuple-element.75), channel_id=1, source_target_pairs={{0,2},{2,0},{1,3},{3,1},{4,6},{6,4},{5,7},{7,5},{8,10},{10,8},{9,1... | collective-permute-start | bytes 786440 | tf_op jit(solution)/shard_map/ppermute | solution.py:222
  74.8 3.3 %early.1 = (f32[2,256,128]{2,1,0:T(8,128)S(1)}, f32[2,256,128]{2,1,0:T(8,128)S(1)}, f32[2,256,128]{2,1,0:T(8,128)S(1)}, f32[2,256,128]{2,1,0:T(8,128)S(1)}, bf16[4,256,512]{2,1,0:T(8,128)(2,1)S(1)}) custom-call(s32[4]{0:T(128)S(1)} %pad_add_fusion.place, bf16[256,1024]{1,0:T(8,128)(2,1)S(1)} %get-tuple-element.56.refs_0_, ...), custom_call_target="tpu_custom_call" | custom-call | flops 805306368 | bytes 1048576 | tf_op jit(solution)/shard_map/early/pallas_call | solution.py:313
  78.6 3.1 %collective-permute-done.18.refs_2_ = f32[256,256]{1,0:T(8,128)S(1)} collective-permute-done((f32[256,256]{1,0:T(8,128)S(1)}, f32[256,256]{1,0:T(8,128)S(1)}, u32[]{:S(2)}, u32[]{:S(2)}) %collective-permute-start.18) | collective-permute-done | bytes 262176 | tf_op jit(solution)/shard_map/ppermute | solution.py:224
  84.3 3.7 %all-to-all-start.1 = ((bf16[8,64,512]{2,1,0:T(8,128)(2,1)}), bf16[8,64,512]{2,1,0:T(8,128)(2,1)S(1)}, u32[]{:S(2)}, u32[]{:S(2)}) async-start(bf16[8,64,512]{2,1,0:T(8,128)(2,1)} %bitcast.29), calls=%async_computation.1 | async-start | bytes 1048576 | tf_op jit(solution)/shard_map/all_to_all | solution.py:414
  94.9 3.7 %attend.2.rest_0_ = bf16[256,4096]{1,0:T(8,128)(2,1)} custom-call(bf16[256,4096]{1,0:T(8,128)(2,1)S(1)} %copy-done.2, bf16[256,512]{1,0:T(8,128)(2,1)S(1)} %copy-done.15, f32[256,128]{1,0:T(8,128)S(1)} %get-tuple-element.105.cosine, f32[256,128]{1,0:T(8,128)S(1)} %get-tuple-element.106.sine, s32[256,1]{1,0:T(8,128)S(1)} %copy.15.start), custom_call_target="tpu_custom_call" | custom-call | flops 536870912 | bytes 1048576 | tf_op jit(solution)/shard_map/attend/pallas_call | solution.py:430
  98.6 3.2 %collective-permute-done.25.came_a.refs_7_ = f32[2,256,128]{2,1,0:T(8,128)} collective-permute-done((f32[2,256,128]{2,1,0:T(8,128)}, f32[2,256,128]{2,1,0:T(8,128)}, u32[]{:S(2)}, u32[]{:S(2)}) %collective-permute-start.25) | collective-permute-done | bytes 262176 | tf_op jit(solution)/shard_map/ppermute | solution.py:222
  104.6 3.2 %collective-permute-done.27.refs_8_ = f32[256,128]{1,0:T(8,128)S(1)} collective-permute-done((f32[256,128]{1,0:T(8,128)S(1)}, f32[256,128]{1,0:T(8,128)S(1)}, u32[]{:S(2)}, u32[]{:S(2)}) %collective-permute-start.27) | collective-permute-done | bytes 131104 | tf_op jit(solution)/shard_map/ppermute | solution.py:224
  109.6 2.2 %rows.3 = (bf16[256,512]{1,0:T(8,128)(2,1)}, bf16[512,512]{1,0:T(8,128)(2,1)}) custom-call(f32[1,512]{1,0:T(1,128)S(1)} %bitcast.27, s32[1,256]{1,0:T(1,128)S(1)} %bitcast_add_fusion.target, f32[2,256,128]{2,1,0:T(8,128)S(1)} %copy-done.7, f32[2,256,128]{2,1,0:T(8,128)S(1)} %copy-done.10, f32[256,128]{1,0:T(8,128)S(1)} %collective-permute-done.22.refs_2_, ...), custom_call_target="tpu_custom_call" | custom-call | flops 134217728 | bytes 1048576 | tf_op jit(solution)/shard_map/rows/pallas_call | solution.py:397
  111.8 4.5 %all-to-all-start = ((bf16[8,64,512]{2,1,0:T(8,128)(2,1)}), bf16[8,64,512]{2,1,0:T(8,128)(2,1)S(1)}, u32[]{:S(2)}, u32[]{:S(2)}) async-start(bf16[8,64,512]{2,1,0:T(8,128)(2,1)} %bitcast.30), calls=%async_computation | async-start | bytes 1048576 | tf_op jit(solution)/shard_map/all_to_all | solution.py:414
  118.8 3.7 %attend.3 = bf16[256,4096]{1,0:T(8,128)(2,1)} custom-call(bf16[256,4096]{1,0:T(8,128)(2,1)S(1)} %copy-done.3, bf16[256,512]{1,0:T(8,128)(2,1)S(1)} %copy-done.16, f32[256,128]{1,0:T(8,128)S(1)} %get-tuple-element.105.cosine, f32[256,128]{1,0:T(8,128)S(1)} %get-tuple-element.106.sine, s32[256,1]{1,0:T(8,128)S(1)} %copy.15.start, ...), custom_call_target="tpu_custom_call", output_to_operand_aliasing={{}: (5, {})} | custom-call | flops 536870912 | bytes 1048576 | tf_op jit(solution)/shard_map/attend/pallas_call | solution.py:430
  123.4 3.4 %all-to-all-done = bf16[8,64,512]{2,1,0:T(8,128)(2,1)S(1)} async-done(((bf16[8,64,512]{2,1,0:T(8,128)(2,1)}), bf16[8,64,512]{2,1,0:T(8,128)(2,1)S(1)}, u32[]{:S(2)}, u32[]{:S(2)}) %all-to-all-start) | async-done | bytes 524320 | tf_op jit(solution)/shard_map/all_to_all | solution.py:414
  (116 shorter events, 40.4 us)
Async XLA Ops:
  2.3 17.9 %collective-permute-start.5 = (bf16[512,512]{1,0:T(8,128)(2,1)S(1)}, bf16[512,512]{1,0:T(8,128)(2,1)S(1)}, u32[]{:S(2)}, u32[]{:S(2)}) collective-permute-start(bf16[512,512]{1,0:T(8,128)(2,1)S(1)} %constant_dynamic-slice_fusion.2.refs_8_), channel_id=1, source_target_pairs={{0,4},{4,8},{8,12},{12,0},{1,5},{5,9},{9,13},{13,1},{2,6},{6,10},{... | collective-permute-start | bytes 1572872 | tf_op jit(solution)/shard_map/ppermute | solution.py:252
  7.4 24.0 %collective-permute-start.9 = (bf16[512,512]{1,0:T(8,128)(2,1)S(1)}, bf16[512,512]{1,0:T(8,128)(2,1)}, u32[]{:S(2)}, u32[]{:S(2)}) collective-permute-start(bf16[512,512]{1,0:T(8,128)(2,1)S(1)} %constant_dynamic-slice_fusion.2.refs_8_), channel_id=1, source_target_pairs={{0,12},{4,0},{8,4},{12,8},{1,13},{5,1},{9,5},{13,9},{2,14},{6,2},{... | collective-permute-start | bytes 1572872 | tf_op jit(solution)/shard_map/ppermute | solution.py:254
  12.5 14.1 %collective-permute-start.2 = (bf16[256,1024]{1,0:T(8,128)(2,1)S(1)}, bf16[256,1024]{1,0:T(8,128)(2,1)S(1)}, u32[]{:S(2)}, u32[]{:S(2)}) collective-permute-start(bf16[256,1024]{1,0:T(8,128)(2,1)S(1)} %get-tuple-element.54), channel_id=1, source_target_pairs={{0,16},{16,0},{1,17},{17,1},{2,18},{18,2},{3,19},{19,3},{4,20},{20... | collective-permute-start | bytes 1572872 | tf_op jit(solution)/shard_map/ppermute | solution.py:224
  14.3 14.8 %collective-permute-start.1 = (bf16[256,1024]{1,0:T(8,128)(2,1)S(1)}, bf16[256,1024]{1,0:T(8,128)(2,1)S(1)}, u32[]{:S(2)}, u32[]{:S(2)}) collective-permute-start(bf16[256,1024]{1,0:T(8,128)(2,1)S(1)} %get-tuple-element.53), channel_id=1, source_target_pairs={{0,2},{2,0},{1,3},{3,1},{4,6},{6,4},{5,7},{7,5},{8,10},{10,8},{9,1... | collective-permute-start | bytes 1572872 | tf_op jit(solution)/shard_map/ppermute | solution.py:222
  15.8 23.3 %collective-permute-start.3 = (bf16[256,1024]{1,0:T(8,128)(2,1)S(1)}, bf16[256,1024]{1,0:T(8,128)(2,1)S(1)}, u32[]{:S(2)}, u32[]{:S(2)}) collective-permute-start(bf16[256,1024]{1,0:T(8,128)(2,1)S(1)} %get-tuple-element.55), channel_id=1, source_target_pairs={{0,18},{2,16},{16,2},{18,0},{1,19},{3,17},{17,3},{19,1},{4,22},{6,... | collective-permute-start | bytes 1572872 | tf_op jit(solution)/shard_map/ppermute | solution.py:225
  20.2 21.6 %collective-permute-start.10 = (bf16[512,512]{1,0:T(8,128)(2,1)S(1)}, bf16[512,512]{1,0:T(8,128)(2,1)S(1)}, u32[]{:S(2)}, u32[]{:S(2)}) collective-permute-start(bf16[512,512]{1,0:T(8,128)(2,1)S(1)} %collective-permute-done.5.refs_9_), channel_id=1, source_target_pairs={{0,4},{4,8},{8,12},{12,0},{1,5},{5,9},{9,13},{13,1},{2,6},{6,10},{... | collective-permute-start | bytes 1572872 | tf_op jit(solution)/shard_map/ppermute | solution.py:252
  26.6 17.8 %collective-permute-start.4 = (bf16[256,1024]{1,0:T(8,128)(2,1)S(1)}, bf16[256,1024]{1,0:T(8,128)(2,1)S(1)}, u32[]{:S(2)}, u32[]{:S(2)}) collective-permute-start(bf16[256,1024]{1,0:T(8,128)(2,1)S(1)} %get-tuple-element.56.refs_0_), channel_id=1, source_target_pairs={{0,1},{1,0},{2,3},{3,2},{4,5},{5,4},{6,7},{7,6},{8,9},{9,8},{10,11... | collective-permute-start | bytes 1572872 | tf_op jit(solution)/shard_map/ppermute | solution.py:282
  29.1 19.1 %collective-permute-start.6 = (bf16[256,1024]{1,0:T(8,128)(2,1)S(1)}, bf16[256,1024]{1,0:T(8,128)(2,1)S(1)}, u32[]{:S(2)}, u32[]{:S(2)}) collective-permute-start(bf16[256,1024]{1,0:T(8,128)(2,1)S(1)} %collective-permute-done.1.refs_1_), channel_id=1, source_target_pairs={{0,1},{1,0},{2,3},{3,2},{4,5},{5,4},{6,7},{7,6},{8,9},{9,8},{10,11... | collective-permute-start | bytes 1572872 | tf_op jit(solution)/shard_map/ppermute | solution.py:282
  31.4 16.8 %collective-permute-start.7 = (bf16[256,1024]{1,0:T(8,128)(2,1)S(1)}, bf16[256,1024]{1,0:T(8,128)(2,1)S(1)}, u32[]{:S(2)}, u32[]{:S(2)}) collective-permute-start(bf16[256,1024]{1,0:T(8,128)(2,1)S(1)} %collective-permute-done.2.refs_2_), channel_id=1, source_target_pairs={{0,1},{1,0},{2,3},{3,2},{4,5},{5,4},{6,7},{7,6},{8,9},{9,8},{10,11... | collective-permute-start | bytes 1572872 | tf_op jit(solution)/shard_map/ppermute | solution.py:282
  41.8 11.1 %collective-permute-start.13 = (bf16[512,256]{1,0:T(8,128)(2,1)S(1)}, bf16[512,256]{1,0:T(8,128)(2,1)S(1)}, u32[]{:S(2)}, u32[]{:S(2)}) collective-permute-start(bf16[512,256]{1,0:T(8,128)(2,1)S(1)} %constant_dynamic-slice_fusion.1.refs_8_), channel_id=1, source_target_pairs={{0,4},{4,8},{8,12},{12,0},{1,5},{5,9},{9,13},{13,1},{2,6},{6,10},{... | collective-permute-start | bytes 786440 | tf_op jit(solution)/shard_map/ppermute | solution.py:252
  44.4 12.0 %collective-permute-start.11 = (bf16[512,256]{1,0:T(8,128)(2,1)S(1)}, bf16[512,256]{1,0:T(8,128)(2,1)S(1)}, u32[]{:S(2)}, u32[]{:S(2)}) collective-permute-start(bf16[512,256]{1,0:T(8,128)(2,1)S(1)} %constant_dynamic-slice_fusion.1.refs_8_), channel_id=1, source_target_pairs={{0,12},{4,0},{8,4},{12,8},{1,13},{5,1},{9,5},{13,9},{2,14},{6,2},{... | collective-permute-start | bytes 786440 | tf_op jit(solution)/shard_map/ppermute | solution.py:254
  53.0 17.6 %collective-permute-start.16 = (f32[2,256,256]{2,1,0:T(8,128)S(1)}, f32[2,256,256]{2,1,0:T(8,128)S(1)}, u32[]{:S(2)}, u32[]{:S(2)}) collective-permute-start(f32[2,256,256]{2,1,0:T(8,128)S(1)} %get-tuple-element.68), channel_id=1, source_target_pairs={{0,2},{2,0},{1,3},{3,1},{4,6},{6,4},{5,7},{7,5},{8,10},{10,8},{9,1... | collective-permute-start | bytes 1572872 | tf_op jit(solution)/shard_map/ppermute | solution.py:222
  54.6 17.8 %collective-permute-start.17 = (f32[2,256,256]{2,1,0:T(8,128)S(1)}, f32[2,256,256]{2,1,0:T(8,128)S(1)}, u32[]{:S(2)}, u32[]{:S(2)}) collective-permute-start(f32[2,256,256]{2,1,0:T(8,128)S(1)} %get-tuple-element.73), channel_id=1, source_target_pairs={{0,16},{16,0},{1,17},{17,1},{2,18},{18,2},{3,19},{19,3},{4,20},{20... | collective-permute-start | bytes 1572872 | tf_op jit(solution)/shard_map/ppermute | solution.py:224
  56.5 12.6 %collective-permute-start.12 = (bf16[512,256]{1,0:T(8,128)(2,1)S(1)}, bf16[512,256]{1,0:T(8,128)(2,1)S(1)}, u32[]{:S(2)}, u32[]{:S(2)}) collective-permute-start(bf16[512,256]{1,0:T(8,128)(2,1)S(1)} %constant_dynamic-slice_fusion.refs_8_), channel_id=1, source_target_pairs={{0,4},{4,8},{8,12},{12,0},{1,5},{5,9},{9,13},{13,1},{2,6},{6,10},{... | collective-permute-start | bytes 786440 | tf_op jit(solution)/shard_map/ppermute | solution.py:252
  62.3 10.7 %collective-permute-start.15 = (bf16[512,256]{1,0:T(8,128)(2,1)S(1)}, bf16[512,256]{1,0:T(8,128)(2,1)S(1)}, u32[]{:S(2)}, u32[]{:S(2)}) collective-permute-start(bf16[512,256]{1,0:T(8,128)(2,1)S(1)} %constant_dynamic-slice_fusion.refs_8_), channel_id=1, source_target_pairs={{0,12},{4,0},{8,4},{12,8},{1,13},{5,1},{9,5},{13,9},{2,14},{6,2},{... | collective-permute-start | bytes 786440 | tf_op jit(solution)/shard_map/ppermute | solution.py:254
  67.5 10.7 %collective-permute-start.20 = (f32[2,256,128]{2,1,0:T(8,128)}, f32[2,256,128]{2,1,0:T(8,128)S(1)}, u32[]{:S(2)}, u32[]{:S(2)}) collective-permute-start(f32[2,256,128]{2,1,0:T(8,128)} %get-tuple-element.78), channel_id=1, source_target_pairs={{0,2},{2,0},{1,3},{3,1},{4,6},{6,4},{5,7},{7,5},{8,10},{10,8},{9,1... | collective-permute-start | bytes 786440 | tf_op jit(solution)/shard_map/ppermute | solution.py:222
  69.1 9.5 %collective-permute-start.21 = (f32[2,256,128]{2,1,0:T(8,128)}, f32[2,256,128]{2,1,0:T(8,128)S(1)}, u32[]{:S(2)}, u32[]{:S(2)}) collective-permute-start(f32[2,256,128]{2,1,0:T(8,128)} %get-tuple-element.81), channel_id=1, source_target_pairs={{0,16},{16,0},{1,17},{17,1},{2,18},{18,2},{3,19},{19,3},{4,20},{20... | collective-permute-start | bytes 786440 | tf_op jit(solution)/shard_map/ppermute | solution.py:224
  70.6 12.3 %collective-permute-start.24 = (bf16[512,256]{1,0:T(8,128)(2,1)S(1)}, bf16[512,256]{1,0:T(8,128)(2,1)S(1)}, u32[]{:S(2)}, u32[]{:S(2)}) collective-permute-start(bf16[512,256]{1,0:T(8,128)(2,1)S(1)} %collective-permute-done.12.refs_9_), channel_id=1, source_target_pairs={{0,4},{4,8},{8,12},{12,0},{1,5},{5,9},{9,13},{13,1},{2,6},{6,10},{... | collective-permute-start | bytes 786440 | tf_op jit(solution)/shard_map/ppermute | solution.py:252
  84.3 27.5 %all-to-all-start.1 = ((bf16[8,64,512]{2,1,0:T(8,128)(2,1)}), bf16[8,64,512]{2,1,0:T(8,128)(2,1)S(1)}, u32[]{:S(2)}, u32[]{:S(2)}) async-start(bf16[8,64,512]{2,1,0:T(8,128)(2,1)} %bitcast.29), calls=%async_computation.1 | async-start | bytes 1048576 | tf_op jit(solution)/shard_map/all_to_all | solution.py:414
  88.0 13.8 %collective-permute-start.25 = (f32[2,256,128]{2,1,0:T(8,128)}, f32[2,256,128]{2,1,0:T(8,128)}, u32[]{:S(2)}, u32[]{:S(2)}) collective-permute-start(f32[2,256,128]{2,1,0:T(8,128)} %get-tuple-element.90), channel_id=1, source_target_pairs={{0,2},{2,0},{1,3},{3,1},{4,6},{6,4},{5,7},{7,5},{8,10},{10,8},{9,1... | collective-permute-start | bytes 786440 | tf_op jit(solution)/shard_map/ppermute | solution.py:222
  89.7 12.1 %collective-permute-start.26 = (f32[2,256,128]{2,1,0:T(8,128)}, f32[2,256,128]{2,1,0:T(8,128)}, u32[]{:S(2)}, u32[]{:S(2)}) collective-permute-start(f32[2,256,128]{2,1,0:T(8,128)} %get-tuple-element.93), channel_id=1, source_target_pairs={{0,16},{16,0},{1,17},{17,1},{2,18},{18,2},{3,19},{19,3},{4,20},{20... | collective-permute-start | bytes 786440 | tf_op jit(solution)/shard_map/ppermute | solution.py:224
  91.4 13.2 %collective-permute-start.22 = (f32[256,128]{1,0:T(8,128)}, f32[256,128]{1,0:T(8,128)S(1)}, u32[]{:S(2)}, u32[]{:S(2)}) collective-permute-start(f32[256,128]{1,0:T(8,128)} %copy-done.19), channel_id=1, source_target_pairs={{0,16},{16,0},{1,17},{17,1},{2,18},{18,2},{3,19},{19,3},{4,20},{20... | collective-permute-start | bytes 393224 | tf_op jit(solution)/shard_map/ppermute | solution.py:224
  92.0 12.7 %collective-permute-start.23 = (f32[256,128]{1,0:T(8,128)}, f32[256,128]{1,0:T(8,128)S(1)}, u32[]{:S(2)}, u32[]{:S(2)}) collective-permute-start(f32[256,128]{1,0:T(8,128)} %copy-done.18), channel_id=1, source_target_pairs={{0,2},{2,0},{1,3},{3,1},{4,6},{6,4},{5,7},{7,5},{8,10},{10,8},{9,1... | collective-permute-start | bytes 393224 | tf_op jit(solution)/shard_map/ppermute | solution.py:222
  111.8 15.0 %all-to-all-start = ((bf16[8,64,512]{2,1,0:T(8,128)(2,1)}), bf16[8,64,512]{2,1,0:T(8,128)(2,1)S(1)}, u32[]{:S(2)}, u32[]{:S(2)}) async-start(bf16[8,64,512]{2,1,0:T(8,128)(2,1)} %bitcast.30), calls=%async_computation | async-start | bytes 1048576 | tf_op jit(solution)/shard_map/all_to_all | solution.py:414
  (30 other events, 219.2 us)

commit v5 on v4

--- a/solution.py
+++ b/solution.py
@@ -278,14 +278,7 @@
             part = lax.dynamic_index_in_dim(part, y ^ (k >> 1), 2, False)
             normed.append(part.reshape(count, features // 4))
     own = [normed[0]] + [to_chip(k, normed[k]) for k in (1, 2, 3)]
-    late = [after(own[0], own[2]), after(own[1], gathered[0][1])]
-    peer = [lax.ppermute(block, "tp", flip) for block in late + own[2:]]
-
-    dest = scoring_rank[:, 0]
     index = jnp.arange(count, dtype=jnp.int32)
-    earlier = (dest[:, None] == dest[None, :]) & (index[:, None] < index[None, :])
-    slot = jnp.sum(earlier.astype(jnp.int32), 0)
-    target = dest * capacity + slot
     row = lengths[0]
     ends = jnp.cumsum(row)
     starts = ends - row
@@ -299,13 +292,23 @@
     sine = jnp.concatenate([-sine, sine], 1)
     turned = pl.pallas_call(
         rotate_kernel,
-        out_shape=jax.ShapeDtypeStruct(queries.shape, jnp.bfloat16),
-        in_specs=[VMEM] * 3,
-        out_specs=VMEM,
+        out_shape=pltpu.HBM(queries.shape, jnp.bfloat16),
+        grid=(1,),
+        in_specs=[pl.BlockSpec(queries.shape, lambda i: (0, 0))]
+        + [pl.BlockSpec((count, HD), lambda i: (0, 0))] * 2,
+        out_specs=pl.BlockSpec(queries.shape, lambda i: (0, 0)),
         compiler_params=PARAMS,
         cost_estimate=cost(4 * count * queries.shape[1], 4 * count * queries.shape[1]),
         name="rotate",
     )(queries, cosine, sine)
+    late = [after(own[0], own[2], turned), after(own[1], gathered[0][1])]
+    peer = [lax.ppermute(block, "tp", flip) for block in late + own[2:]]
+
+    dest = scoring_rank[:, 0]
+    index = jnp.arange(count, dtype=jnp.int32)
+    earlier = (dest[:, None] == dest[None, :]) & (index[:, None] < index[None, :])
+    slot = jnp.sum(earlier.astype(jnp.int32), 0)
+    target = dest * capacity + slot
 
     bias = kv_bias[None, :]
     def begin_sums(blocks, sums, wide):
@@ -455,7 +458,7 @@
         sums = [jax.ShapeDtypeStruct((2, count, wide // 2), jnp.float32)] * 4
         begun = begin_sums(gathered[-1], sums, wide)
     parts_1 = add_up(1, None, (parts_0[0],))
-    _, share_0 = exchange(0, parts_0, (parts_1[0], gathered[1][-1]))
+    _, share_0 = exchange(0, parts_0, (gathered[1][-1],))
     folded, share_1 = exchange(1, parts_1, (gathered[2][-1], *([] if begun is None else begun[:1])))
     split = chunks[1][0] * 2 * HD
     keyval, outgoing = rows_of(0, [share_0], (*([] if begun is None else begun[:1]),))

time: 128 us -> 128 us (level)
  waiting for transfers between devices: 45.6 us -> 43 us
  starting transfers between devices: 38.1 us -> 40.4 us
  local copies, waits for them, and re-layouts: 11.5 us -> 10.1 us
  Pallas kernels: 30.3 us -> 31.6 us
    ppermute x7, waiting for transfers between devices: 13.1 us -> 6.97 us  [to_chip(): return lax.ppermute(array, 'groups', flip)]
    ppermute x6, waiting for transfers between devices: 11.4 us -> 15 us  [gather(): ups.append(lax.ppermute(held, 'fz', right))]
    pallas_call x1, Pallas kernels: 1.11 us -> 2.51 us  [shards(): pl.pallas_call(rotate_kernel, out_shape=pltpu.HBM(queries.shape, jnp.bflo...]
    unnamed x46 -> x44, local copies, waits for them, and re-layouts: 11.2 us -> 9.88 us
    ppermute x6, starting transfers between devices: 5.51 us -> 6.82 us  [gather(): ups.append(lax.ppermute(held, 'fz', right))]
  transfers between devices with their start and end apart: 31 -> 31, of which waited for: 14 -> 14; matrix products, arithmetic and copies ran while one was open for 1% -> 1% of each run, Pallas kernels for 22% -> 23%
where the time goes in v5:
time: 128 us; the launch traced here: 127 us
  waiting for transfers between devices  43 us (34%)
  starting transfers between devices  40.4 us (32%)
  Pallas kernels  31.6 us (25%)
  local copies, waits for them, and re-layouts  10.1 us (8%)
    ppermute x6, waiting for transfers between devices, gather(): ups.append(lax.ppermute(held, 'fz', right))  15 us
    unnamed x44, local copies, waits for them, and re-layouts  9.88 us
    ppermute x7, starting transfers between devices, to_chip(): return lax.ppermute(array, 'fx', flip)  9.51 us
    pallas_call x2, Pallas kernels, add_up(): pl.pallas_call(functools.partial(matmul_kernel, count=steps, piece=piece)...  9.34 us
    ppermute x7, starting transfers between devices, to_chip(): return lax.ppermute(array, 'groups', flip)  9.02 us
    all_to_all x2, starting transfers between devices, send(): lax.all_to_all(outgoing, ('fz', 'fx'), split_axis=0, concat_axis=0, tiled...  8.85 us
    ppermute x7, waiting for transfers between devices, to_chip(): return lax.ppermute(array, 'fx', flip)  7.76 us
    ppermute x1, waiting for transfers between devices, to_chip(): return lax.ppermute(array, ('groups', 'fx'), flip_both)  7.74 us
  transfers between devices with their start and end apart: 31, of which 14 were waited for; matrix products, arithmetic and copies ran while one was open for 1% of the time, Pallas kernels for 23%

profile of v5, /device:TPU:0, one launch (start us, length us, event | category | flops | bytes accessed | tf_op | source)
XLA Modules:
  0.0 127.3 jit_solution(5790442351070469180)
XLA Ops:
  2.3 3.1 %collective-permute-start.5 = (bf16[512,512]{1,0:T(8,128)(2,1)S(1)}, bf16[512,512]{1,0:T(8,128)(2,1)S(1)}, u32[]{:S(2)}, u32[]{:S(2)}) collective-permute-start(bf16[512,512]{1,0:T(8,128)(2,1)S(1)} %constant_dynamic-slice_fusion.2.refs_8_), channel_id=1, source_target_pairs={{0,4},{4,8},{8,12},{12,0},{1,5},{5,9},{9,13},{13,1},{2,6},{6,10},{... | collective-permute-start | bytes 1572872 | tf_op jit(solution)/shard_map/ppermute | solution.py:252
  7.4 2.1 %collective-permute-start.9 = (bf16[512,512]{1,0:T(8,128)(2,1)S(1)}, bf16[512,512]{1,0:T(8,128)(2,1)}, u32[]{:S(2)}, u32[]{:S(2)}) collective-permute-start(bf16[512,512]{1,0:T(8,128)(2,1)S(1)} %constant_dynamic-slice_fusion.2.refs_8_), channel_id=1, source_target_pairs={{0,12},{4,0},{8,4},{12,8},{1,13},{5,1},{9,5},{13,9},{2,14},{6,2},{... | collective-permute-start | bytes 1572872 | tf_op jit(solution)/shard_map/ppermute | solution.py:254
  16.7 3.4 %collective-permute-done.5.refs_9_ = bf16[512,512]{1,0:T(8,128)(2,1)S(1)} collective-permute-done((bf16[512,512]{1,0:T(8,128)(2,1)S(1)}, bf16[512,512]{1,0:T(8,128)(2,1)S(1)}, u32[]{:S(2)}, u32[]{:S(2)}) %collective-permute-start.5) | collective-permute-done | bytes 524320 | tf_op jit(solution)/shard_map/ppermute | solution.py:252
  20.3 2.5 %rotate.1.queries = bf16[256,4096]{1,0:T(8,128)(2,1)} custom-call(bf16[256,4096]{1,0:T(8,128)(2,1)S(1)} %copy-done.5, f32[256,128]{1,0:T(8,128)S(1)} %get-tuple-element.105.cosine, f32[256,128]{1,0:T(8,128)S(1)} %get-tuple-element.106.sine), custom_call_target="tpu_custom_call" | custom-call | flops 4194304 | bytes 4194304 | tf_op jit(solution)/shard_map/rotate/pallas_call | solution.py:293
  22.8 3.9 %collective-permute-done.2.refs_2_ = bf16[256,1024]{1,0:T(8,128)(2,1)S(1)} collective-permute-done((bf16[256,1024]{1,0:T(8,128)(2,1)S(1)}, bf16[256,1024]{1,0:T(8,128)(2,1)S(1)}, u32[]{:S(2)}, u32[]{:S(2)}) %collective-permute-start.2) | collective-permute-done | bytes 524320 | tf_op jit(solution)/shard_map/ppermute | solution.py:224
  26.7 2.5 %collective-permute-done.1.refs_1_ = bf16[256,1024]{1,0:T(8,128)(2,1)S(1)} collective-permute-done((bf16[256,1024]{1,0:T(8,128)(2,1)S(1)}, bf16[256,1024]{1,0:T(8,128)(2,1)S(1)}, u32[]{:S(2)}, u32[]{:S(2)}) %collective-permute-start.1) | collective-permute-done | bytes 524320 | tf_op jit(solution)/shard_map/ppermute | solution.py:222
  29.2 2.2 %collective-permute-done.9.refs_11_ = bf16[512,512]{1,0:T(8,128)(2,1)} collective-permute-done((bf16[512,512]{1,0:T(8,128)(2,1)S(1)}, bf16[512,512]{1,0:T(8,128)(2,1)}, u32[]{:S(2)}, u32[]{:S(2)}) %collective-permute-start.9) | collective-permute-done | bytes 524320 | tf_op jit(solution)/shard_map/ppermute | solution.py:254
  31.4 7.7 %collective-permute-done.3.refs_3_ = bf16[256,1024]{1,0:T(8,128)(2,1)S(1)} collective-permute-done((bf16[256,1024]{1,0:T(8,128)(2,1)S(1)}, bf16[256,1024]{1,0:T(8,128)(2,1)S(1)}, u32[]{:S(2)}, u32[]{:S(2)}) %collective-permute-start.3) | collective-permute-done | bytes 524320 | tf_op jit(solution)/shard_map/ppermute | solution.py:225
  39.2 2.6 %collective-permute-done.10.refs_10_ = bf16[512,512]{1,0:T(8,128)(2,1)S(1)} collective-permute-done((bf16[512,512]{1,0:T(8,128)(2,1)S(1)}, bf16[512,512]{1,0:T(8,128)(2,1)S(1)}, u32[]{:S(2)}, u32[]{:S(2)}) %collective-permute-start.10) | collective-permute-done | bytes 524320 | tf_op jit(solution)/shard_map/ppermute | solution.py:252
  41.8 3.8 %collective-permute-start.11 = (bf16[512,256]{1,0:T(8,128)(2,1)S(1)}, bf16[512,256]{1,0:T(8,128)(2,1)S(1)}, u32[]{:S(2)}, u32[]{:S(2)}) collective-permute-start(bf16[512,256]{1,0:T(8,128)(2,1)S(1)} %constant_dynamic-slice_fusion.1.refs_8_), channel_id=1, source_target_pairs={{0,12},{4,0},{8,4},{12,8},{1,13},{5,1},{9,5},{13,9},{2,14},{6,2},{... | collective-permute-start | bytes 786440 | tf_op jit(solution)/shard_map/ppermute | solution.py:254
  45.6 4.7 %project.2 = (f32[2,256,256]{2,1,0:T(8,128)S(1)}, f32[2,256,256]{2,1,0:T(8,128)S(1)}, f32[2,256,256]{2,1,0:T(8,128)S(1)}, f32[2,256,256]{2,1,0:T(8,128)S(1)}) custom-call(s32[4]{0:T(128)S(1)} %pad_add_fusion.place, bf16[256,1024]{1,0:T(8,128)(2,1)S(1)} %get-tuple-element.56.refs_0_, bf16[256,1024]{1,0:T(8,128)(2,1)S(1)} %collective-permute-done.1.refs_1_, ...), custom_call_target="tpu_custom_call" | custom-call | flops 2147483648 | bytes 1048576 | tf_op jit(solution)/shard_map/project/pallas_call | solution.py:342
  50.3 2.6 %collective-permute-done.13.refs_9_ = bf16[512,256]{1,0:T(8,128)(2,1)S(1)} collective-permute-done((bf16[512,256]{1,0:T(8,128)(2,1)S(1)}, bf16[512,256]{1,0:T(8,128)(2,1)S(1)}, u32[]{:S(2)}, u32[]{:S(2)}) %collective-permute-start.13) | collective-permute-done | bytes 262176 | tf_op jit(solution)/shard_map/ppermute | solution.py:252
  57.6 6.5 %collective-permute-done.14.refs_10_ = bf16[512,256]{1,0:T(8,128)(2,1)S(1)} collective-permute-done((bf16[512,256]{1,0:T(8,128)(2,1)S(1)}, bf16[512,256]{1,0:T(8,128)(2,1)S(1)}, u32[]{:S(2)}, u32[]{:S(2)}) %collective-permute-start.14) | collective-permute-done | bytes 262176 | tf_op jit(solution)/shard_map/ppermute | solution.py:252
  64.2 4.7 %project.3 = (f32[2,256,128]{2,1,0:T(8,128)}, f32[2,256,128]{2,1,0:T(8,128)}, f32[2,256,128]{2,1,0:T(8,128)}, f32[2,256,128]{2,1,0:T(8,128)}) custom-call(s32[4]{0:T(128)S(1)} %pad_add_fusion.place, bf16[256,1024]{1,0:T(8,128)(2,1)S(1)} %get-tuple-element.56.refs_0_, bf16[256,1024]{1,0:T(8,128)(2,1)S(1)} %collective-permute-done.1.refs_1_, ...), custom_call_target="tpu_custom_call" | custom-call | flops 1073741824 | bytes 1048576 | tf_op jit(solution)/shard_map/project/pallas_call | solution.py:342
  74.7 2.1 %collective-permute-start.19 = (f32[256,256]{1,0:T(8,128)S(1)}, f32[256,256]{1,0:T(8,128)S(1)}, u32[]{:S(2)}, u32[]{:S(2)}) collective-permute-start(f32[256,256]{1,0:T(8,128)S(1)} %get-tuple-element.73), channel_id=1, source_target_pairs={{0,2},{2,0},{1,3},{3,1},{4,6},{6,4},{5,7},{7,5},{8,10},{10,8},{9,1... | collective-permute-start | bytes 786440 | tf_op jit(solution)/shard_map/ppermute | solution.py:222
  76.8 3.3 %early.1 = (f32[2,256,128]{2,1,0:T(8,128)S(1)}, f32[2,256,128]{2,1,0:T(8,128)S(1)}, f32[2,256,128]{2,1,0:T(8,128)S(1)}, f32[2,256,128]{2,1,0:T(8,128)S(1)}, bf16[4,256,512]{2,1,0:T(8,128)(2,1)S(1)}) custom-call(s32[4]{0:T(128)S(1)} %pad_add_fusion.place, bf16[256,1024]{1,0:T(8,128)(2,1)S(1)} %get-tuple-element.56.refs_0_, ...), custom_call_target="tpu_custom_call" | custom-call | flops 805306368 | bytes 1048576 | tf_op jit(solution)/shard_map/early/pallas_call | solution.py:316
  83.8 4.3 %all-to-all-start.1 = ((bf16[8,64,512]{2,1,0:T(8,128)(2,1)}), bf16[8,64,512]{2,1,0:T(8,128)(2,1)S(1)}, u32[]{:S(2)}, u32[]{:S(2)}) async-start(bf16[8,64,512]{2,1,0:T(8,128)(2,1)} %bitcast.29), calls=%async_computation.1 | async-start | bytes 1048576 | tf_op jit(solution)/shard_map/all_to_all | solution.py:417
  95.0 3.7 %attend.2.rest_0_ = bf16[256,4096]{1,0:T(8,128)(2,1)} custom-call(bf16[256,4096]{1,0:T(8,128)(2,1)S(1)} %copy-done.1, bf16[256,512]{1,0:T(8,128)(2,1)S(1)} %copy-done.14, f32[256,128]{1,0:T(8,128)S(1)} %get-tuple-element.105.cosine, f32[256,128]{1,0:T(8,128)S(1)} %get-tuple-element.106.sine, s32[256,1]{1,0:T(8,128)S(1)} %copy.15.start), custom_call_target="tpu_custom_call" | custom-call | flops 536870912 | bytes 1048576 | tf_op jit(solution)/shard_map/attend/pallas_call | solution.py:433
  98.7 3.2 %collective-permute-done.25.came_a.refs_7_ = f32[2,256,128]{2,1,0:T(8,128)} collective-permute-done((f32[2,256,128]{2,1,0:T(8,128)}, f32[2,256,128]{2,1,0:T(8,128)}, u32[]{:S(2)}, u32[]{:S(2)}) %collective-permute-start.25) | collective-permute-done | bytes 262176 | tf_op jit(solution)/shard_map/ppermute | solution.py:222
  105.2 2.7 %collective-permute-done.27.refs_8_ = f32[256,128]{1,0:T(8,128)S(1)} collective-permute-done((f32[256,128]{1,0:T(8,128)S(1)}, f32[256,128]{1,0:T(8,128)S(1)}, u32[]{:S(2)}, u32[]{:S(2)}) %collective-permute-start.27) | collective-permute-done | bytes 131104 | tf_op jit(solution)/shard_map/ppermute | solution.py:224
  109.4 2.2 %rows.3 = (bf16[256,512]{1,0:T(8,128)(2,1)}, bf16[512,512]{1,0:T(8,128)(2,1)}) custom-call(f32[1,512]{1,0:T(1,128)S(1)} %bitcast.27, s32[1,256]{1,0:T(1,128)S(1)} %bitcast_add_fusion.target, f32[2,256,128]{2,1,0:T(8,128)S(1)} %copy-done.6, f32[2,256,128]{2,1,0:T(8,128)S(1)} %copy-done.9, f32[256,128]{1,0:T(8,128)S(1)} %collective-permute-done.22.refs_2_, ...), custom_call_target="tpu_custom_call" | custom-call | flops 134217728 | bytes 1048576 | tf_op jit(solution)/shard_map/rows/pallas_call | solution.py:400
  111.5 4.5 %all-to-all-start = ((bf16[8,64,512]{2,1,0:T(8,128)(2,1)}), bf16[8,64,512]{2,1,0:T(8,128)(2,1)S(1)}, u32[]{:S(2)}, u32[]{:S(2)}) async-start(bf16[8,64,512]{2,1,0:T(8,128)(2,1)} %bitcast.30), calls=%async_computation | async-start | bytes 1048576 | tf_op jit(solution)/shard_map/all_to_all | solution.py:417
  118.6 3.7 %attend.3 = bf16[256,4096]{1,0:T(8,128)(2,1)} custom-call(bf16[256,4096]{1,0:T(8,128)(2,1)S(1)} %copy-done.2, bf16[256,512]{1,0:T(8,128)(2,1)S(1)} %copy-done.15, f32[256,128]{1,0:T(8,128)S(1)} %get-tuple-element.105.cosine, f32[256,128]{1,0:T(8,128)S(1)} %get-tuple-element.106.sine, s32[256,1]{1,0:T(8,128)S(1)} %copy.15.start, ...), custom_call_target="tpu_custom_call", output_to_operand_aliasing={{}: (5, {})} | custom-call | flops 536870912 | bytes 1048576 | tf_op jit(solution)/shard_map/attend/pallas_call | solution.py:433
  123.2 3.3 %all-to-all-done = bf16[8,64,512]{2,1,0:T(8,128)(2,1)S(1)} async-done(((bf16[8,64,512]{2,1,0:T(8,128)(2,1)}), bf16[8,64,512]{2,1,0:T(8,128)(2,1)S(1)}, u32[]{:S(2)}, u32[]{:S(2)}) %all-to-all-start) | async-done | bytes 524320 | tf_op jit(solution)/shard_map/all_to_all | solution.py:417
  (114 shorter events, 41.1 us)
Async XLA Ops:
  2.3 17.9 %collective-permute-start.5 = (bf16[512,512]{1,0:T(8,128)(2,1)S(1)}, bf16[512,512]{1,0:T(8,128)(2,1)S(1)}, u32[]{:S(2)}, u32[]{:S(2)}) collective-permute-start(bf16[512,512]{1,0:T(8,128)(2,1)S(1)} %constant_dynamic-slice_fusion.2.refs_8_), channel_id=1, source_target_pairs={{0,4},{4,8},{8,12},{12,0},{1,5},{5,9},{9,13},{13,1},{2,6},{6,10},{... | collective-permute-start | bytes 1572872 | tf_op jit(solution)/shard_map/ppermute | solution.py:252
  7.4 24.0 %collective-permute-start.9 = (bf16[512,512]{1,0:T(8,128)(2,1)S(1)}, bf16[512,512]{1,0:T(8,128)(2,1)}, u32[]{:S(2)}, u32[]{:S(2)}) collective-permute-start(bf16[512,512]{1,0:T(8,128)(2,1)S(1)} %constant_dynamic-slice_fusion.2.refs_8_), channel_id=1, source_target_pairs={{0,12},{4,0},{8,4},{12,8},{1,13},{5,1},{9,5},{13,9},{2,14},{6,2},{... | collective-permute-start | bytes 1572872 | tf_op jit(solution)/shard_map/ppermute | solution.py:254
  12.6 14.1 %collective-permute-start.2 = (bf16[256,1024]{1,0:T(8,128)(2,1)S(1)}, bf16[256,1024]{1,0:T(8,128)(2,1)S(1)}, u32[]{:S(2)}, u32[]{:S(2)}) collective-permute-start(bf16[256,1024]{1,0:T(8,128)(2,1)S(1)} %get-tuple-element.54), channel_id=1, source_target_pairs={{0,16},{16,0},{1,17},{17,1},{2,18},{18,2},{3,19},{19,3},{4,20},{20... | collective-permute-start | bytes 1572872 | tf_op jit(solution)/shard_map/ppermute | solution.py:224
  14.4 14.8 %collective-permute-start.1 = (bf16[256,1024]{1,0:T(8,128)(2,1)S(1)}, bf16[256,1024]{1,0:T(8,128)(2,1)S(1)}, u32[]{:S(2)}, u32[]{:S(2)}) collective-permute-start(bf16[256,1024]{1,0:T(8,128)(2,1)S(1)} %get-tuple-element.53), channel_id=1, source_target_pairs={{0,2},{2,0},{1,3},{3,1},{4,6},{6,4},{5,7},{7,5},{8,10},{10,8},{9,1... | collective-permute-start | bytes 1572872 | tf_op jit(solution)/shard_map/ppermute | solution.py:222
  15.9 23.3 %collective-permute-start.3 = (bf16[256,1024]{1,0:T(8,128)(2,1)S(1)}, bf16[256,1024]{1,0:T(8,128)(2,1)S(1)}, u32[]{:S(2)}, u32[]{:S(2)}) collective-permute-start(bf16[256,1024]{1,0:T(8,128)(2,1)S(1)} %get-tuple-element.55), channel_id=1, source_target_pairs={{0,18},{2,16},{16,2},{18,0},{1,19},{3,17},{17,3},{19,1},{4,22},{6,... | collective-permute-start | bytes 1572872 | tf_op jit(solution)/shard_map/ppermute | solution.py:225
  20.2 21.6 %collective-permute-start.10 = (bf16[512,512]{1,0:T(8,128)(2,1)S(1)}, bf16[512,512]{1,0:T(8,128)(2,1)S(1)}, u32[]{:S(2)}, u32[]{:S(2)}) collective-permute-start(bf16[512,512]{1,0:T(8,128)(2,1)S(1)} %collective-permute-done.5.refs_9_), channel_id=1, source_target_pairs={{0,4},{4,8},{8,12},{12,0},{1,5},{5,9},{9,13},{13,1},{2,6},{6,10},{... | collective-permute-start | bytes 1572872 | tf_op jit(solution)/shard_map/ppermute | solution.py:252
  26.7 15.1 %collective-permute-start.4 = (bf16[256,1024]{1,0:T(8,128)(2,1)S(1)}, bf16[256,1024]{1,0:T(8,128)(2,1)S(1)}, u32[]{:S(2)}, u32[]{:S(2)}) collective-permute-start(bf16[256,1024]{1,0:T(8,128)(2,1)S(1)} %get-tuple-element.56.refs_0_), channel_id=1, source_target_pairs={{0,1},{1,0},{2,3},{3,2},{4,5},{5,4},{6,7},{7,6},{8,9},{9,8},{10,11... | collective-permute-start | bytes 1572872 | tf_op jit(solution)/shard_map/ppermute | solution.py:305
  29.2 16.4 %collective-permute-start.6 = (bf16[256,1024]{1,0:T(8,128)(2,1)S(1)}, bf16[256,1024]{1,0:T(8,128)(2,1)S(1)}, u32[]{:S(2)}, u32[]{:S(2)}) collective-permute-start(bf16[256,1024]{1,0:T(8,128)(2,1)S(1)} %collective-permute-done.1.refs_1_), channel_id=1, source_target_pairs={{0,1},{1,0},{2,3},{3,2},{4,5},{5,4},{6,7},{7,6},{8,9},{9,8},{10,11... | collective-permute-start | bytes 1572872 | tf_op jit(solution)/shard_map/ppermute | solution.py:305
  31.4 14.2 %collective-permute-start.7 = (bf16[256,1024]{1,0:T(8,128)(2,1)S(1)}, bf16[256,1024]{1,0:T(8,128)(2,1)S(1)}, u32[]{:S(2)}, u32[]{:S(2)}) collective-permute-start(bf16[256,1024]{1,0:T(8,128)(2,1)S(1)} %collective-permute-done.2.refs_2_), channel_id=1, source_target_pairs={{0,1},{1,0},{2,3},{3,2},{4,5},{5,4},{6,7},{7,6},{8,9},{9,8},{10,11... | collective-permute-start | bytes 1572872 | tf_op jit(solution)/shard_map/ppermute | solution.py:305
  41.8 11.1 %collective-permute-start.13 = (bf16[512,256]{1,0:T(8,128)(2,1)S(1)}, bf16[512,256]{1,0:T(8,128)(2,1)S(1)}, u32[]{:S(2)}, u32[]{:S(2)}) collective-permute-start(bf16[512,256]{1,0:T(8,128)(2,1)S(1)} %constant_dynamic-slice_fusion.1.refs_8_), channel_id=1, source_target_pairs={{0,4},{4,8},{8,12},{12,0},{1,5},{5,9},{9,13},{13,1},{2,6},{6,10},{... | collective-permute-start | bytes 786440 | tf_op jit(solution)/shard_map/ppermute | solution.py:252
  41.8 14.1 %collective-permute-start.11 = (bf16[512,256]{1,0:T(8,128)(2,1)S(1)}, bf16[512,256]{1,0:T(8,128)(2,1)S(1)}, u32[]{:S(2)}, u32[]{:S(2)}) collective-permute-start(bf16[512,256]{1,0:T(8,128)(2,1)S(1)} %constant_dynamic-slice_fusion.1.refs_8_), channel_id=1, source_target_pairs={{0,12},{4,0},{8,4},{12,8},{1,13},{5,1},{9,5},{13,9},{2,14},{6,2},{... | collective-permute-start | bytes 786440 | tf_op jit(solution)/shard_map/ppermute | solution.py:254
  52.9 11.2 %collective-permute-start.14 = (bf16[512,256]{1,0:T(8,128)(2,1)S(1)}, bf16[512,256]{1,0:T(8,128)(2,1)S(1)}, u32[]{:S(2)}, u32[]{:S(2)}) collective-permute-start(bf16[512,256]{1,0:T(8,128)(2,1)S(1)} %collective-permute-done.13.refs_9_), channel_id=1, source_target_pairs={{0,4},{4,8},{8,12},{12,0},{1,5},{5,9},{9,13},{13,1},{2,6},{6,10},{... | collective-permute-start | bytes 786440 | tf_op jit(solution)/shard_map/ppermute | solution.py:252
  52.9 19.2 %collective-permute-start.16 = (f32[2,256,256]{2,1,0:T(8,128)S(1)}, f32[2,256,256]{2,1,0:T(8,128)S(1)}, u32[]{:S(2)}, u32[]{:S(2)}) collective-permute-start(f32[2,256,256]{2,1,0:T(8,128)S(1)} %get-tuple-element.68), channel_id=1, source_target_pairs={{0,2},{2,0},{1,3},{3,1},{4,6},{6,4},{5,7},{7,5},{8,10},{10,8},{9,1... | collective-permute-start | bytes 1572872 | tf_op jit(solution)/shard_map/ppermute | solution.py:222
  54.4 19.8 %collective-permute-start.17 = (f32[2,256,256]{2,1,0:T(8,128)S(1)}, f32[2,256,256]{2,1,0:T(8,128)S(1)}, u32[]{:S(2)}, u32[]{:S(2)}) collective-permute-start(f32[2,256,256]{2,1,0:T(8,128)S(1)} %get-tuple-element.71), channel_id=1, source_target_pairs={{0,16},{16,0},{1,17},{17,1},{2,18},{18,2},{3,19},{19,3},{4,20},{20... | collective-permute-start | bytes 1572872 | tf_op jit(solution)/shard_map/ppermute | solution.py:224
  55.9 14.6 %collective-permute-start.12 = (bf16[512,256]{1,0:T(8,128)(2,1)S(1)}, bf16[512,256]{1,0:T(8,128)(2,1)S(1)}, u32[]{:S(2)}, u32[]{:S(2)}) collective-permute-start(bf16[512,256]{1,0:T(8,128)(2,1)S(1)} %constant_dynamic-slice_fusion.refs_8_), channel_id=1, source_target_pairs={{0,4},{4,8},{8,12},{12,0},{1,5},{5,9},{9,13},{13,1},{2,6},{6,10},{... | collective-permute-start | bytes 786440 | tf_op jit(solution)/shard_map/ppermute | solution.py:252
  64.1 10.7 %collective-permute-start.15 = (bf16[512,256]{1,0:T(8,128)(2,1)S(1)}, bf16[512,256]{1,0:T(8,128)(2,1)S(1)}, u32[]{:S(2)}, u32[]{:S(2)}) collective-permute-start(bf16[512,256]{1,0:T(8,128)(2,1)S(1)} %constant_dynamic-slice_fusion.refs_8_), channel_id=1, source_target_pairs={{0,12},{4,0},{8,4},{12,8},{1,13},{5,1},{9,5},{13,9},{2,14},{6,2},{... | collective-permute-start | bytes 786440 | tf_op jit(solution)/shard_map/ppermute | solution.py:254
  68.9 11.2 %collective-permute-start.20 = (f32[2,256,128]{2,1,0:T(8,128)}, f32[2,256,128]{2,1,0:T(8,128)S(1)}, u32[]{:S(2)}, u32[]{:S(2)}) collective-permute-start(f32[2,256,128]{2,1,0:T(8,128)} %get-tuple-element.78), channel_id=1, source_target_pairs={{0,2},{2,0},{1,3},{3,1},{4,6},{6,4},{5,7},{7,5},{8,10},{10,8},{9,1... | collective-permute-start | bytes 786440 | tf_op jit(solution)/shard_map/ppermute | solution.py:222
  72.1 10.3 %collective-permute-start.24 = (bf16[512,256]{1,0:T(8,128)(2,1)S(1)}, bf16[512,256]{1,0:T(8,128)(2,1)S(1)}, u32[]{:S(2)}, u32[]{:S(2)}) collective-permute-start(bf16[512,256]{1,0:T(8,128)(2,1)S(1)} %collective-permute-done.12.refs_9_), channel_id=1, source_target_pairs={{0,4},{4,8},{8,12},{12,0},{1,5},{5,9},{9,13},{13,1},{2,6},{6,10},{... | collective-permute-start | bytes 786440 | tf_op jit(solution)/shard_map/ppermute | solution.py:252
  83.8 27.7 %all-to-all-start.1 = ((bf16[8,64,512]{2,1,0:T(8,128)(2,1)}), bf16[8,64,512]{2,1,0:T(8,128)(2,1)S(1)}, u32[]{:S(2)}, u32[]{:S(2)}) async-start(bf16[8,64,512]{2,1,0:T(8,128)(2,1)} %bitcast.29), calls=%async_computation.1 | async-start | bytes 1048576 | tf_op jit(solution)/shard_map/all_to_all | solution.py:417
  88.1 13.7 %collective-permute-start.25 = (f32[2,256,128]{2,1,0:T(8,128)}, f32[2,256,128]{2,1,0:T(8,128)}, u32[]{:S(2)}, u32[]{:S(2)}) collective-permute-start(f32[2,256,128]{2,1,0:T(8,128)} %get-tuple-element.90), channel_id=1, source_target_pairs={{0,2},{2,0},{1,3},{3,1},{4,6},{6,4},{5,7},{7,5},{8,10},{10,8},{9,1... | collective-permute-start | bytes 786440 | tf_op jit(solution)/shard_map/ppermute | solution.py:222
  90.1 11.7 %collective-permute-start.26 = (f32[2,256,128]{2,1,0:T(8,128)}, f32[2,256,128]{2,1,0:T(8,128)}, u32[]{:S(2)}, u32[]{:S(2)}) collective-permute-start(f32[2,256,128]{2,1,0:T(8,128)} %get-tuple-element.93), channel_id=1, source_target_pairs={{0,16},{16,0},{1,17},{17,1},{2,18},{18,2},{3,19},{19,3},{4,20},{20... | collective-permute-start | bytes 786440 | tf_op jit(solution)/shard_map/ppermute | solution.py:224
  91.9 13.3 %collective-permute-start.22 = (f32[256,128]{1,0:T(8,128)}, f32[256,128]{1,0:T(8,128)S(1)}, u32[]{:S(2)}, u32[]{:S(2)}) collective-permute-start(f32[256,128]{1,0:T(8,128)} %copy-done.18), channel_id=1, source_target_pairs={{0,16},{16,0},{1,17},{17,1},{2,18},{18,2},{3,19},{19,3},{4,20},{20... | collective-permute-start | bytes 393224 | tf_op jit(solution)/shard_map/ppermute | solution.py:224
  92.4 12.8 %collective-permute-start.23 = (f32[256,128]{1,0:T(8,128)}, f32[256,128]{1,0:T(8,128)S(1)}, u32[]{:S(2)}, u32[]{:S(2)}) collective-permute-start(f32[256,128]{1,0:T(8,128)} %copy-done.17), channel_id=1, source_target_pairs={{0,2},{2,0},{1,3},{3,1},{4,6},{6,4},{5,7},{7,5},{8,10},{10,8},{9,1... | collective-permute-start | bytes 393224 | tf_op jit(solution)/shard_map/ppermute | solution.py:222
  111.5 14.9 %all-to-all-start = ((bf16[8,64,512]{2,1,0:T(8,128)(2,1)}), bf16[8,64,512]{2,1,0:T(8,128)(2,1)S(1)}, u32[]{:S(2)}, u32[]{:S(2)}) async-start(bf16[8,64,512]{2,1,0:T(8,128)(2,1)} %bitcast.30), calls=%async_computation | async-start | bytes 1048576 | tf_op jit(solution)/shard_map/all_to_all | solution.py:417
  (29 other events, 191.6 us)
